TPU v7x, 32 devices: a whole 2x2x4 slice. The times are simulated.
32 devices in a mesh: groups: 2 (over y), wide: 8 (over z, x), tp: 2 (over core).
Axes of the slice: x: 2, y: 2, z: 4, core: 2. Of those that a mesh axis runs over, the one named last changes fastest.
Arguments:
- pre_codes: bfloat16 [64, 4, 4, 2, 512], P(('groups', 'wide'), None, 'tp'), parts along dimension 0, may hold values from -6 to 6
- pre_scales: bfloat16 [64, 4, 4, 2, 4], P(('groups', 'wide'), None, 'tp'), parts along dimension 0, may hold values from 0.099609375 to 1
- req_dest: int32 [64], P(('groups', 'wide')), parts along dimension 0, may hold values from 0 to 7, as said below
- req_blocks: int32 [64], P(('groups', 'wide')), parts along dimension 0, may hold values from 1 to 4, as said below
- res_codes: bfloat16 [128, 64, 2, 512], P(('groups', 'wide'), None, None, 'tp'), parts along dimension 0, may hold values from -6 to 6
- res_scales: bfloat16 [128, 64, 2, 4], P(('groups', 'wide'), None, None, 'tp'), parts along dimension 0, may hold values from 0.099609375 to 1
- res_len: int32 [128], P(('groups', 'wide')), parts along dimension 0, may hold values from 1 to 64, as said below
- res_query: bfloat16 [128, 2, 8192], P(('groups', 'wide'), None, 'tp'), parts along dimension 0, may hold values from -128 to 128
- res_new: bfloat16 [128, 2, 2, 512], P(('groups', 'wide'), None, None, 'tp'), parts along dimension 0, may hold values from -6 to 6
- arr_query: bfloat16 [96, 2, 8192], P(('groups', 'wide'), None, 'tp'), parts along dimension 0, may hold values from -128 to 128
- arr_new: bfloat16 [96, 2, 2, 512], P(('groups', 'wide'), None, None, 'tp'), parts along dimension 0, may hold values from -6 to 6
Outputs:
- res_out: bfloat16 [128, 2, 8192], P(('groups', 'wide'), None, 'tp'), parts along dimension 0
- arr_out: bfloat16 [96, 2, 8192], P(('groups', 'wide'), None, 'tp'), parts along dimension 0
There are 2 independent parts, one for each index of `groups`. A program takes and returns all parts, laid end to end along the dimension named above; each array names one. Nothing has to cross between parts.
Inputs may be any that keep to these rules, and one draw needn't show every extreme that they name: `req_dest`: each prefill instance sends at most one request to one decode instance; each decode instance receives at least 2 and at most 6 requests, and some decode instance receives 6 in every draw. For every even r, request r of each prefill instance goes to the instance a fixed distance away along the axis, the same distance for all prefill instances, and request r + 1 to the instance at one of two further such distances. `req_blocks`: some request holds 4 blocks in every draw. `res_len`: some resident request has 64 tokens in every draw.
All inputs are finite; a program needn't handle non-finite values.
Results may differ from a plain program's by a relative error of at most 0.0032.
Values may be sent and summed in bfloat16 or wider, within the bound.
No kernel may reach another device: no remote copies, remote signals or barrier semaphores. Data moves between devices by JAX's collectives and lax.ppermute only.
A program may use at most 64 MiB of HBM per device.

v0:
```python
import math

import jax
import jax.numpy as jnp
from jax import lax
from jax.sharding import PartitionSpec as P

KVH = 4
HD = 128
HQ = 64
MAXB = 4


NEGATIVE = -1e30


def dequantize(quantized, scales):
    heads = scales.shape[-1]
    leading = quantized.shape[:-2]
    expanded = quantized.reshape(leading + (2, heads, HD)).astype(jnp.float32)
    factors = scales.astype(jnp.float32)[..., None]
    return (expanded * factors).astype(jnp.bfloat16)


def attend(query, fresh_kv, cache, is_valid):
    slot_count = query.shape[0]
    heads = fresh_kv.shape[-1] // HD
    score_scale = 1.0 / math.sqrt(HD)
    queries = query.reshape(slot_count, 2, heads, HQ // KVH, HD)
    cache_keys = cache[:, :, 0]
    cache_values = cache[:, :, 1]
    new_keys = fresh_kv[:, :, 0].reshape(slot_count, 2, heads, HD)
    new_values = fresh_kv[:, :, 1].reshape(slot_count, 2, heads, HD)
    cache_scores = (
        jnp.einsum("sekgd,stkd->sekgt", queries, cache_keys, preferred_element_type=jnp.float32)
        * score_scale
    )
    fresh_scores = (
        jnp.einsum("sekgd,sfkd->sekgf", queries, new_keys, preferred_element_type=jnp.float32)
        * score_scale
    )
    step_index = jnp.arange(2)
    cache_mask = is_valid[:, None, None, None, :]
    fresh_mask = (step_index[None, :] <= step_index[:, None])[None, :, None, None, :]
    cache_scores = jnp.where(cache_mask, cache_scores, NEGATIVE)
    fresh_scores = jnp.where(fresh_mask, fresh_scores, NEGATIVE)
    row_top = jnp.maximum(jnp.max(cache_scores, axis=-1), jnp.max(fresh_scores, axis=-1))
    cache_weights = jnp.where(cache_mask, jnp.exp(cache_scores - row_top[..., None]), 0.0)
    fresh_weights = jnp.where(fresh_mask, jnp.exp(fresh_scores - row_top[..., None]), 0.0)
    row_total = jnp.sum(cache_weights, axis=-1) + jnp.sum(fresh_weights, axis=-1)
    mixed_sum = jnp.einsum(
        "sekgt,stkd->sekgd",
        cache_weights.astype(jnp.bfloat16),
        cache_values,
        preferred_element_type=jnp.float32,
    )
    mixed_sum = mixed_sum + jnp.einsum(
        "sekgf,sfkd->sekgd",
        fresh_weights.astype(jnp.bfloat16),
        new_values,
        preferred_element_type=jnp.float32,
    )
    return (
        (mixed_sum / row_total[..., None])
        .reshape(slot_count, 2, heads * (HQ // KVH) * HD)
        .astype(jnp.bfloat16)
    )


def locate(flat_counts, slot_total):
    present = (flat_counts > 0).astype(jnp.int32)
    slot_order = jnp.cumsum(present) - present
    target = jnp.where(present > 0, slot_order, slot_total)
    item_index = (
        jnp.zeros((slot_total,), jnp.int32)
        .at[target]
        .set(jnp.arange(flat_counts.shape[0], dtype=jnp.int32), mode="drop")
    )
    arrival_blocks = jnp.zeros((slot_total,), jnp.int32).at[target].set(flat_counts, mode="drop")
    return (item_index, arrival_blocks)


def shards(
    pre_codes,
    pre_scales,
    req_dest,
    req_blocks,
    res_codes,
    res_scales,
    res_len,
    res_query,
    res_new,
    arr_query,
    arr_new,
):
    peer_count = lax.axis_size("wide")
    slot_total = arr_query.shape[0]
    send_codes = (
        jnp.zeros((peer_count,) + pre_codes.shape[1:], jnp.bfloat16).at[req_dest].set(pre_codes)
    )
    send_scales = (
        jnp.zeros((peer_count,) + pre_scales.shape[1:], jnp.bfloat16).at[req_dest].set(pre_scales)
    )
    send_count = jnp.zeros((peer_count,), jnp.int32).at[req_dest].set(req_blocks)
    got_codes, got_scales, got_count = (
        lax.all_to_all(send_codes, "wide", split_axis=0, concat_axis=0, tiled=True),
        lax.all_to_all(send_scales, "wide", split_axis=0, concat_axis=0, tiled=True),
        lax.all_to_all(send_count, "wide", split_axis=0, concat_axis=0, tiled=True),
    )
    got_codes, got_scales = (
        lax.all_to_all(got_codes, "tp", split_axis=4, concat_axis=2, tiled=True),
        lax.all_to_all(got_scales, "tp", split_axis=4, concat_axis=2, tiled=True),
    )
    item_index, arrival_blocks = locate(got_count, slot_total)
    arrived_codes = got_codes[item_index]
    arrived_scales = got_scales[item_index]
    res_valid = jnp.arange(res_codes.shape[1])[None, :] < res_len[:, None]
    resident = dequantize(res_codes, res_scales)
    res_out = attend(res_query, res_new, resident, res_valid)
    block_tokens = arrived_codes.shape[2]
    arrived = dequantize(arrived_codes, arrived_scales)
    arrived = arrived.reshape((slot_total, MAXB * block_tokens) + arrived.shape[3:])
    token_block = jnp.arange(MAXB * block_tokens) // block_tokens
    arr_valid = token_block[None, :] < arrival_blocks[:, None]
    arr_out = attend(arr_query, arr_new, arrived, arr_valid)
    return (res_out, arr_out)


def solution(mesh):
    in_specs = (
        P(("groups", "wide"), None, "tp", None, None),
        P(("groups", "wide"), None, "tp", None, None),
        P(("groups", "wide")),
        P(("groups", "wide")),
        P(("groups", "wide"), None, None, "tp"),
        P(("groups", "wide"), None, None, "tp"),
        P(("groups", "wide")),
        P(("groups", "wide"), None, "tp"),
        P(("groups", "wide"), None, None, "tp"),
        P(("groups", "wide"), None, "tp"),
        P(("groups", "wide"), None, None, "tp"),
    )
    out_specs = (P(("groups", "wide"), None, "tp"), P(("groups", "wide"), None, "tp"))
    return jax.shard_map(shards, mesh=mesh, in_specs=in_specs, out_specs=out_specs, check_vma=False)
```

profile of v0, /device:TPU:0, one launch (start us, length us, event | category | flops | bytes accessed | tf_op | source)
XLA Modules:
  0.0 69.7 jit_solution(509462496480570441)
XLA Ops:
  1.3 0.7 %scatter_custom_fusion.1 = s32[8]{0:T(128)S(1)} fusion(s32[4]{0:T(128)S(1)} %compare_select_fusion.2, s32[4]{0:T(128)} %param.14, s32[]{:T(128)} %constant.17.clone.1), kind=kCustom, calls=%fused_computation.82 | custom fusion | bytes 544 | tf_op jit(solution)/shard_map/scatter | solution.py:104
  2.7 7.3 %all-to-all-start.2 = ((s32[8,1,1]{2,1,0:T(1,128)}), s32[8,1,1]{2,1,0:T(1,128)S(1)}, u32[]{:S(2)}, u32[]{:S(2)}) async-start(s32[8,1,1]{2,1,0:T(1,128)} %copy.148), calls=%async_computation.2 | async-start | bytes 8192 | tf_op jit(solution)/shard_map/all_to_all | solution.py:108
  10.0 0.9 %copy.144 = bf16[4,4,2,2,512]{4,1,3,2,0:T(4,128)(2,1)S(1)} copy(bf16[4,4,2,2,512]{4,3,2,1,0:T(2,128)(2,1)} %param.11) | data formatting | bytes 131072 | tf_op args[0]
  10.8 0.7 %copy.151 = bf16[4,4,2,2,4]{4,1,3,2,0:T(4,128)(2,1)S(1)} copy(bf16[4,4,2,2,4]{4,3,2,1,0:T(2,128)(2,1)} %param.12) | data formatting | bytes 1024 | tf_op args[1]
  11.6 1.0 %reshape.163 = bf16[6,2,2,16,128]{4,3,2,1,0:T(8,128)(2,1)S(1)} reshape(bf16[6,2,4096]{2,1,0:T(2,128)(2,1)} %param.20) | data formatting | bytes 196608 | tf_op jit(solution)/shard_map/reshape | solution.py:29
  12.5 0.9 %slice_reduce_fusion.2 = (bf16[6,2,256]{2,1,0:T(2,128)(2,1)S(1)}, bf16[6,2,256]{2,1,0:T(2,128)(2,1)S(1)}) fusion(bf16[6,2,2,256]{3,2,1,0:T(2,128)(2,1)} %param.21), kind=kLoop, calls=%fused_computation.59 | loop fusion | bytes 24576 | tf_op jit(solution)/shard_map/slice | solution.py:33
  13.4 1.0 %reshape.162 = bf16[8,2,2,16,128]{4,3,2,1,0:T(8,128)(2,1)S(1)} reshape(bf16[8,2,4096]{2,1,0:T(2,128)(2,1)} %param.18) | data formatting | bytes 262144 | tf_op jit(solution)/shard_map/reshape | solution.py:29
  14.5 0.9 %slice_reduce_fusion.1 = (bf16[8,2,256]{2,1,0:T(2,128)(2,1)S(1)}, bf16[8,2,256]{2,1,0:T(2,128)(2,1)S(1)}) fusion(bf16[8,2,2,256]{3,2,1,0:T(2,128)(2,1)} %param.19), kind=kLoop, calls=%fused_computation.57 | loop fusion | bytes 32768 | tf_op jit(solution)/shard_map/slice | solution.py:32
  15.4 0.7 %iota_compare_fusion = pred[8,64]{1,0:T(8,128)(4,1)S(1)} fusion(s32[8]{0:T(128)} %param.17), kind=kLoop, calls=%fused_computation.68 | loop fusion | flops 512 | bytes 544 | tf_op jit(solution)/shard_map/lt | solution.py:117
  16.1 2.3 %reshape.237 = f32[8,64,2,2,128]{4,3,2,1,0:T(2,128)S(1)} reshape(bf16[8,64,2,256]{3,2,1,0:T(2,128)(2,1)} %param.15) | data formatting | bytes 1572864 | tf_op jit(solution)/shard_map/convert_element_type | solution.py:20
  20.6 0.7 reshape.240
  21.3 0.7 broadcast_in_dim.128
  22.0 2.0 %scatter_fusion = bf16[8,4,2,2,512]{4,1,3,2,0:T(4,128)(2,1)} fusion(bf16[8,4,2,2,512]{4,1,3,2,0:T(4,128)(2,1)} %broadcast_in_dim.128, s32[4]{0:T(128)S(1)} %compare_select_fusion.2, bf16[4,4,2,2,512]{4,1,3,2,0:T(4,128)(2,1)S(1)} %copy.144), kind=kCustom, calls=%fused_computation.2 | custom fusion | bytes 196624 | tf_op jit(solution)/shard_map/scatter | solution.py:99
  25.0 1.9 %scatter_fusion.1 = bf16[8,4,2,2,4]{4,1,3,2,0:T(4,128)(2,1)} fusion(bf16[8,4,2,2,4]{4,1,3,2,0:T(4,128)(2,1)} %broadcast_in_dim.132, s32[4]{0:T(128)S(1)} %compare_select_fusion.2, bf16[4,4,2,2,4]{4,1,3,2,0:T(4,128)(2,1)S(1)} %copy.151), kind=kCustom, calls=%fused_computation.5 | custom fusion | bytes 1552 | tf_op jit(solution)/shard_map/scatter | solution.py:102
  26.9 6.0 %all-to-all-start.3 = ((bf16[8,4,2,2,4]{4,1,3,2,0:T(4,128)(2,1)}), bf16[8,4,2,2,4]{4,1,3,2,0:T(4,128)(2,1)S(1)}, u32[]{:S(2)}, u32[]{:S(2)}) async-start(bf16[8,4,2,2,4]{4,1,3,2,0:T(4,128)(2,1)} %scatter_fusion.1), calls=%async_computation.3 | async-start | bytes 65536 | tf_op jit(solution)/shard_map/all_to_all | solution.py:107
  34.1 5.5 %all-to-all-done.3 = bf16[8,4,2,2,4]{4,1,3,2,0:T(4,128)(2,1)S(1)} async-done(((bf16[8,4,2,2,4]{4,1,3,2,0:T(4,128)(2,1)}), bf16[8,4,2,2,4]{4,1,3,2,0:T(4,128)(2,1)S(1)}, u32[]{:S(2)}, u32[]{:S(2)}) %all-to-all-start.3) | async-done | bytes 1056 | tf_op jit(solution)/shard_map/all_to_all | solution.py:107
  39.8 3.7 %all_to_all.58 = bf16[2,2,128]{2,1,0:T(2,128)(2,1)S(1)} all-to-all(bf16[2,2,128]{2,1,0:T(2,128)(2,1)S(1)} %reshape.255), channel_id=1, replica_groups=mesh['groups'=2,'wide'=8,'tp'=2] {'tp'}, dimensions={0} | all-to-all | bytes 2048 | tf_op jit(solution)/shard_map/all_to_all | solution.py:112
  43.5 3.4 %all-to-all-start = ((bf16[8,4,2,2,512]{4,1,3,2,0:T(4,128)(2,1)}), bf16[8,4,2,2,512]{4,1,3,2,0:T(4,128)(2,1)S(1)}, u32[]{:S(2)}, u32[]{:S(2)}) async-start(bf16[8,4,2,2,512]{4,1,3,2,0:T(4,128)(2,1)} %scatter_fusion), calls=%async_computation | async-start | bytes 262144 | tf_op jit(solution)/shard_map/all_to_all | solution.py:106
  48.6 5.9 %all-to-all-done = bf16[8,4,2,2,512]{4,1,3,2,0:T(4,128)(2,1)S(1)} async-done(((bf16[8,4,2,2,512]{4,1,3,2,0:T(4,128)(2,1)}), bf16[8,4,2,2,512]{4,1,3,2,0:T(4,128)(2,1)S(1)}, u32[]{:S(2)}, u32[]{:S(2)}) %all-to-all-start) | async-done | bytes 131104 | tf_op jit(solution)/shard_map/all_to_all | solution.py:106
  54.5 1.8 %copy.145 = bf16[8,4,2,2,512]{0,1,3,2,4:T(4,128)(2,1)S(1)} copy(bf16[8,4,2,2,512]{4,1,3,2,0:T(4,128)(2,1)S(1)} %all-to-all-done) | data formatting | bytes 262144 | tf_op jit(solution)/shard_map/all_to_all | solution.py:106
  56.3 2.2 %reshape.253 = bf16[2,2,16384]{2,1,0:T(2,128)(2,1)S(1)} reshape(bf16[512,2,2,4,8]{4,3,2,1,0:T(4,128)(2,1)S(1)} %bitcast.86) | data formatting | bytes 262144
  58.5 3.8 %all_to_all.59 = bf16[2,2,16384]{2,1,0:T(2,128)(2,1)S(1)} all-to-all(bf16[2,2,16384]{2,1,0:T(2,128)(2,1)S(1)} %reshape.253), channel_id=1, replica_groups=mesh['groups'=2,'wide'=8,'tp'=2] {'tp'}, dimensions={0} | all-to-all | bytes 262144 | tf_op jit(solution)/shard_map/all_to_all | solution.py:111
  62.4 2.4 %reshape.254 = bf16[512,2,2,4,8]{4,3,2,1,0:T(4,128)(2,1)S(1)} reshape(bf16[2,2,16384]{2,1,0:T(2,128)(2,1)S(1)} %all_to_all.59) | data formatting | bytes 262144
  64.8 1.8 %copy.185 = bf16[8,4,2,2,2,256]{5,4,0,3,2,1:T(2,128)(2,1)S(1)} copy(bf16[8,4,2,2,2,256]{0,1,3,2,5,4:T(4,128)(2,1)S(1)} %bitcast.87) | data formatting | bytes 262144 | tf_op jit(solution)/shard_map/all_to_all | solution.py:111
  (55 shorter events, 10.7 us)
Async XLA Ops:
  0.6 17.8 %copy-start = (bf16[8,64,2,2]{1,3,2,0:T(2,128)(2,1)S(1)}, bf16[8,64,2,2]{1,3,2,0:T(2,128)(2,1)}, u32[]{:S(2)}) copy-start(bf16[8,64,2,2]{1,3,2,0:T(2,128)(2,1)} %param.16) | copy-start | bytes 12292
  2.7 24.2 %all-to-all-start.2 = ((s32[8,1,1]{2,1,0:T(1,128)}), s32[8,1,1]{2,1,0:T(1,128)S(1)}, u32[]{:S(2)}, u32[]{:S(2)}) async-start(s32[8,1,1]{2,1,0:T(1,128)} %copy.148), calls=%async_computation.2 | async-start | bytes 8192 | tf_op jit(solution)/shard_map/all_to_all | solution.py:108
  26.9 12.7 %all-to-all-start.3 = ((bf16[8,4,2,2,4]{4,1,3,2,0:T(4,128)(2,1)}), bf16[8,4,2,2,4]{4,1,3,2,0:T(4,128)(2,1)S(1)}, u32[]{:S(2)}, u32[]{:S(2)}) async-start(bf16[8,4,2,2,4]{4,1,3,2,0:T(4,128)(2,1)} %scatter_fusion.1), calls=%async_computation.3 | async-start | bytes 65536 | tf_op jit(solution)/shard_map/all_to_all | solution.py:107
  43.5 10.9 %all-to-all-start = ((bf16[8,4,2,2,512]{4,1,3,2,0:T(4,128)(2,1)}), bf16[8,4,2,2,512]{4,1,3,2,0:T(4,128)(2,1)S(1)}, u32[]{:S(2)}, u32[]{:S(2)}) async-start(bf16[8,4,2,2,512]{4,1,3,2,0:T(4,128)(2,1)} %scatter_fusion), calls=%async_computation | async-start | bytes 262144 | tf_op jit(solution)/shard_map/all_to_all | solution.py:106
where the time goes:
time: 70.8 us; the launch traced here: 69.7 us
  local copies, waits for them, and re-layouts  27.4 us (39%)
  starting transfers between devices  16.6 us (23%)
  waiting for transfers between devices  11.4 us (16%)
  blocking collectives  7.49 us (11%)
  other arithmetic  3.24 us (5%)
  matrix products  2.66 us (4%)
  between operations  0.94 us (1%)
    all_to_all x1, starting transfers between devices, shards(): lax.all_to_all(send_count, 'wide', split_axis=0, concat_axis=0, tiled=True)  7.25 us
    unnamed x10, local copies, waits for them, and re-layouts  7.13 us
    all_to_all x1, starting transfers between devices, shards(): lax.all_to_all(send_scales, 'wide', split_axis=0, concat_axis=0, tiled=True)  5.99 us
    all_to_all x1, waiting for transfers between devices, shards(): lax.all_to_all(send_codes, 'wide', split_axis=0, concat_axis=0, tiled=True)  5.88 us
    all_to_all x1, waiting for transfers between devices, shards(): lax.all_to_all(send_scales, 'wide', split_axis=0, concat_axis=0, tiled=True)  5.49 us
    all_to_all x1, blocking collectives, shards(): lax.all_to_all(got_codes, 'tp', split_axis=4, concat_axis=2, tiled=True)  3.84 us
    all_to_all x1, blocking collectives, shards(): lax.all_to_all(got_scales, 'tp', split_axis=4, concat_axis=2, tiled=True)  3.66 us
    all_to_all x1, starting transfers between devices, shards(): lax.all_to_all(send_codes, 'wide', split_axis=0, concat_axis=0, tiled=True)  3.37 us
  transfers between devices with their start and end apart: 3, of which 2 were waited for; matrix products, arithmetic and copies ran while one was open for 28% of the time, Pallas kernels for 0%

commit v1 on v0

v1 whole, which is shorter than its diff:
```python
import functools
import math

import jax
import jax.numpy as jnp
from jax import lax
from jax.experimental import pallas as pl
from jax.experimental.pallas import tpu as pltpu
from jax.sharding import PartitionSpec as P

KVH = 4
HD = 128
HQ = 64
GROUP = HQ // KVH
STEPS = 2

NEGATIVE = -1e30
EMPTY = 1024.0
SCORE_SCALE = 1.0 / math.sqrt(HD)

BF16 = jnp.bfloat16
F32 = jnp.float32


def iota(shape, axis):
    return lax.broadcasted_iota(jnp.int32, shape, axis)


def dot_nt(a, b):
    return lax.dot_general(a, b, (((1,), (1,)), ((), ())), preferred_element_type=F32)


def dot_nn(a, b):
    return lax.dot_general(a, b, (((1,), (0,)), ((), ())), preferred_element_type=F32)


def whole(memory_space=pltpu.VMEM):
    return pl.BlockSpec(memory_space=memory_space)


def pack_kernel(tp, block_rows, dest_ref, blocks_ref, codes_ref, scales_ref, send_ref):
    requests, tokens, heads = codes_ref.shape[:3]
    rows = 2 * tokens
    per_core = heads // tp
    send_ref[...] = jnp.full(send_ref.shape, EMPTY, BF16)
    row_block = iota((rows, HD), 0) // block_rows

    def place(r):
        there = dest_ref[r]
        held = row_block < blocks_ref[r]
        scales = scales_ref[r].astype(F32)
        for j in range(heads):
            codes = codes_ref[r, :, j].astype(F32).reshape(rows, HD)
            values = codes * scales[:, j : j + 1]
            values = jnp.where(held, values, EMPTY).astype(BF16)
            send_ref[there * tp + j // per_core, j % per_core] = values

    if requests <= 8:
        for r in range(requests):
            place(r)
    else:
        lax.fori_loop(0, requests, lambda r, c: (place(r), c)[1], 0)


def resident_kernel(len_ref, codes_ref, scales_ref, query_ref, new_ref, out_ref):
    slots, rows = codes_ref.shape[:2]
    heads = scales_ref.shape[2]
    tokens = rows // (2 * heads)
    queries = query_ref.shape[1]
    new_rows = new_ref.shape[1]

    from_scale = iota((rows, rows), 1)
    to_row = iota((rows, rows), 0)
    source = ((to_row % 2) * heads + (to_row // 2) % heads) * tokens + to_row // (2 * heads)
    spread = jnp.where(from_scale == source, 1.0, 0.0).astype(BF16)
    flat = jnp.concatenate(
        [scales_ref[:, p, h] for p in range(2) for h in range(heads)], axis=1
    )
    columns = dot_nt(spread, flat)

    col = iota((queries, rows), 1)
    row_head = iota((queries, rows), 0) // (queries // heads)
    is_key = (col % 2 == 0) & ((col // 2) % heads == row_head)
    col_token = jnp.where(is_key, col // (2 * heads), tokens)

    new_col = iota((queries, new_rows), 1)
    new_head = iota((queries, new_rows), 0) // (queries // heads)
    new_step = iota((queries, new_rows), 0) % STEPS
    new_ok = (
        (new_col % 2 == 0)
        & ((new_col // 2) % heads == new_head)
        & (new_col // (2 * heads) <= new_step)
    )

    for s in range(slots):
        cache = (codes_ref[s].astype(F32) * columns[:, s : s + 1]).astype(BF16)
        query = query_ref[s]
        new = new_ref[s]
        scores = jnp.where(
            col_token < len_ref[s], dot_nt(query, cache) * SCORE_SCALE, NEGATIVE
        )
        new_scores = jnp.where(new_ok, dot_nt(query, new) * SCORE_SCALE, NEGATIVE)
        top = jnp.maximum(
            jnp.max(scores, axis=1, keepdims=True), jnp.max(new_scores, axis=1, keepdims=True)
        )
        weights = jnp.exp(scores - top)
        new_weights = jnp.exp(new_scores - top)
        total = jnp.sum(weights, axis=1, keepdims=True) + jnp.sum(
            new_weights, axis=1, keepdims=True
        )
        weights = pltpu.roll(weights, 1, 1).astype(BF16)
        new_weights = jnp.concatenate(
            [jnp.zeros((queries, 1), F32), new_weights[:, : new_rows - 1]], axis=1
        ).astype(BF16)
        mixed = dot_nn(weights, cache) + dot_nn(new_weights, new)
        out_ref[s] = (mixed / total).astype(BF16)


def arrival_kernel(tp, got_ref, query_ref, new_ref, out_ref):
    chunks, heads, chunk_rows = got_ref.shape[:3]
    slots, _, per_head = query_ref.shape[:3]
    rows = slots * per_head
    columns = chunks * chunk_rows
    sender_rows = tp * chunk_rows
    piece = min(columns, 256)

    caches = [got_ref[:, h].reshape(columns, HD) for h in range(heads)]
    ones = jnp.ones((8, HD), BF16)
    sums = dot_nt(ones, caches[0])
    col = iota((8, columns), 1)
    held = sums < EMPTY
    first = jnp.where(held & (col % sender_rows == 0), 1.0, 0.0).astype(BF16)
    before = jnp.where(
        iota((piece, piece), 0) // sender_rows < iota((piece, piece), 1) // sender_rows, 1.0, 0.0
    ).astype(BF16)
    base = jnp.zeros((8, 1), F32)
    ranks = []
    for p in range(0, columns, piece):
        part = first[:, p : p + piece]
        ranks.append(dot_nn(part, before) + base)
        if p + piece < columns:
            base = base + jnp.sum(part.astype(F32), axis=1, keepdims=True)
    rank = ranks[0] if len(ranks) == 1 else jnp.concatenate(ranks, axis=1)
    slot_of = jnp.where(held & (col % 2 == 0), rank, -1.0)[:1]
    first_slot = (pl.program_id(0) * slots).astype(F32)

    new_rows = new_ref.shape[0] * new_ref.shape[1] // heads
    row_slot = iota((rows, new_rows), 0) // per_head
    row_step = iota((rows, new_rows), 0) % STEPS
    new_col = iota((rows, new_rows), 1)
    new_ok = (
        (new_col % 2 == 0)
        & (new_col // (2 * STEPS) == row_slot)
        & ((new_col // 2) % STEPS <= row_step)
    )
    slot_rows = (iota((rows, 1), 0) // per_head).astype(F32) + first_slot
    mask = slot_of == slot_rows

    for h in range(heads):
        query = query_ref[:, h].reshape(rows, HD)
        new = jnp.concatenate(
            [
                new_ref[a, 2 * (f * heads + h) : 2 * (f * heads + h) + 2]
                for a in range(slots)
                for f in range(STEPS)
            ],
            axis=0,
        )
        cache = caches[h]
        scores = jnp.where(mask, dot_nt(query, cache) * SCORE_SCALE, NEGATIVE)
        new_scores = jnp.where(new_ok, dot_nt(query, new) * SCORE_SCALE, NEGATIVE)
        top = jnp.maximum(
            jnp.max(scores, axis=1, keepdims=True), jnp.max(new_scores, axis=1, keepdims=True)
        )
        weights = jnp.exp(scores - top)
        new_weights = jnp.exp(new_scores - top)
        total = jnp.sum(weights, axis=1, keepdims=True) + jnp.sum(
            new_weights, axis=1, keepdims=True
        )
        weights = pltpu.roll(weights, 1, 1).astype(BF16)
        new_weights = jnp.concatenate(
            [jnp.zeros((rows, 1), F32), new_weights[:, : new_rows - 1]], axis=1
        ).astype(BF16)
        mixed = dot_nn(weights, cache) + dot_nn(new_weights, new)
        out_ref[:, h] = (mixed / total).astype(BF16).reshape(slots, per_head, HD)


def pack(pre_codes, pre_scales, req_dest, req_blocks, peers, tp):
    requests, blocks, block_tokens = pre_codes.shape[:3]
    tokens = blocks * block_tokens
    codes = pre_codes.reshape(requests, tokens, 2, KVH, HD).transpose(0, 1, 3, 2, 4)
    scales = pre_scales.reshape(requests, tokens * 2, KVH)
    out = jax.ShapeDtypeStruct((peers * tp, KVH // tp, tokens * 2, HD), BF16)
    return pl.pallas_call(
        functools.partial(pack_kernel, tp, 2 * block_tokens),
        out_shape=out,
        in_specs=[whole(pltpu.SMEM), whole(pltpu.SMEM), whole(), whole()],
        out_specs=whole(),
        name="pack",
    )(req_dest, req_blocks, codes, scales)


def query_rows(query):
    slots, steps, width = query.shape
    return query.reshape(slots, steps, width // HD, HD).transpose(0, 2, 1, 3)


def new_rows_of(new):
    slots, steps, pair, width = new.shape
    heads = width // HD
    return (
        new.reshape(slots, steps, pair, heads, HD)
        .transpose(0, 1, 3, 2, 4)
        .reshape(slots, steps * heads * pair, HD)
    )


def from_rows(out, shape):
    slots, steps, width = shape
    return out.reshape(slots, width // HD, steps, HD).transpose(0, 2, 1, 3).reshape(shape)


def resident(res_codes, res_scales, res_len, res_query, res_new):
    slots, tokens, _, width = res_codes.shape
    heads = width // HD
    codes = (
        res_codes.reshape(slots, tokens, 2, heads, HD)
        .transpose(0, 1, 3, 2, 4)
        .reshape(slots, tokens * heads * 2, HD)
    )
    scales = res_scales.transpose(0, 2, 3, 1)
    query = query_rows(res_query).reshape(slots, heads * GROUP * STEPS, HD)
    work = slots * heads * GROUP * STEPS * tokens * heads * 2
    out = pl.pallas_call(
        resident_kernel,
        out_shape=jax.ShapeDtypeStruct(query.shape, BF16),
        in_specs=[whole(pltpu.SMEM)] + [whole()] * 4,
        out_specs=whole(),
        cost_estimate=pl.CostEstimate(
            flops=4 * work * HD, bytes_accessed=2 * res_codes.size + 4 * query.size, transcendentals=work
        ),
        name="resident",
    )(res_len, codes, scales, query, new_rows_of(res_new))
    return from_rows(out, res_query.shape)


def arrivals(got, arr_query, arr_new, tp):
    slots, steps, width = arr_query.shape
    heads = width // (HD * GROUP)
    query = query_rows(arr_query).reshape(slots, heads, GROUP * steps, HD)
    new = new_rows_of(arr_new)
    size = max(n for n in range(1, 7) if slots % n == 0)
    out = pl.pallas_call(
        functools.partial(arrival_kernel, tp),
        out_shape=jax.ShapeDtypeStruct(query.shape, BF16),
        grid=(slots // size,),
        in_specs=[
            pl.BlockSpec(got.shape, lambda i: (0, 0, 0, 0)),
            pl.BlockSpec((size,) + query.shape[1:], lambda i: (i, 0, 0, 0)),
            pl.BlockSpec((size,) + new.shape[1:], lambda i: (i, 0, 0)),
        ],
        out_specs=pl.BlockSpec((size,) + query.shape[1:], lambda i: (i, 0, 0, 0)),
        compiler_params=pltpu.CompilerParams(vmem_limit_bytes=48 * 2**20),
        name="arrivals",
    )(got, query, new)
    return from_rows(out, arr_query.shape)


def shards(
    pre_codes,
    pre_scales,
    req_dest,
    req_blocks,
    res_codes,
    res_scales,
    res_len,
    res_query,
    res_new,
    arr_query,
    arr_new,
):
    peers = lax.axis_size("wide")
    tp = lax.axis_size("tp")
    send = pack(pre_codes, pre_scales, req_dest, req_blocks, peers, tp)
    got = lax.all_to_all(send, ("wide", "tp"), split_axis=0, concat_axis=0, tiled=True)
    res_out = resident(res_codes, res_scales, res_len, res_query, res_new)
    arr_out = arrivals(got, arr_query, arr_new, tp)
    return (res_out, arr_out)


def solution(mesh):
    in_specs = (
        P(("groups", "wide"), None, "tp", None, None),
        P(("groups", "wide"), None, "tp", None, None),
        P(("groups", "wide")),
        P(("groups", "wide")),
        P(("groups", "wide"), None, None, "tp"),
        P(("groups", "wide"), None, None, "tp"),
        P(("groups", "wide")),
        P(("groups", "wide"), None, "tp"),
        P(("groups", "wide"), None, None, "tp"),
        P(("groups", "wide"), None, "tp"),
        P(("groups", "wide"), None, None, "tp"),
    )
    out_specs = (P(("groups", "wide"), None, "tp"), P(("groups", "wide"), None, "tp"))
    return jax.shard_map(shards, mesh=mesh, in_specs=in_specs, out_specs=out_specs, check_vma=False)
```

time: 70.8 us -> 19.6 us (0.28); the launches traced: 69.7 us -> 19.3 us
  local copies, waits for them, and re-layouts: 27.4 us -> 0.01 us
  starting transfers between devices: 16.6 us -> 7.36 us
  waiting for transfers between devices: 11.4 us -> 2.9 us
  Pallas kernels: 0 us -> 8.35 us
  blocking collectives: 7.49 us -> 0 us
  other arithmetic: 3.24 us -> 0 us
  matrix products: 2.66 us -> 0 us
    all_to_all x3 -> x1, starting transfers between devices: 16.6 us -> 7.36 us  [shards(): lax.all_to_all(send, ('wide', 'tp'), split_axis=0, concat_axis=0, tiled=T...]
    all_to_all x3 -> x1, waiting for transfers between devices: 11.4 us -> 2.9 us  [shards(): lax.all_to_all(send, ('wide', 'tp'), split_axis=0, concat_axis=0, tiled=T...]
    pallas_call x0 -> x3, Pallas kernels: none -> 8.35 us  [the longest x1 5.02 us: resident(): pl.pallas_call(resident_kernel, out_shape=jax.ShapeDtypeStruct(query.shap...]
    all_to_all x2 -> x0, blocking collectives: 7.49 us -> none  [the longest x1 3.84 us: shards(): lax.all_to_all(got_codes, 'tp', split_axis=4, concat_axis=2, tiled=True)]
    unnamed x10 -> x4, local copies, waits for them, and re-layouts: 7.13 us -> 0.01 us
    scatter x5 -> x0, local copies, waits for them, and re-layouts: 5.8 us -> none  [the longest x1 1.98 us: shards(): jnp.zeros((peer_count,) + pre_codes.shape[1:], jnp.bfloat16).at[req_dest]]
    all_to_all x9 -> x0, local copies, waits for them, and re-layouts: 4.8 us -> none  [the longest x3 1.89 us: shards(): lax.all_to_all(got_codes, 'tp', split_axis=4, concat_axis=2, tiled=True)]
    convert_element_type x6 -> x0, local copies, waits for them, and re-layouts: 3.38 us -> none  [the longest x3 2.61 us: dequantize(): expanded = quantized.reshape(leading + (2, heads, HD)).astype(jnp.float32)]
  transfers between devices with their start and end apart: 3 -> 1, of which waited for: 2 -> 1; matrix products, arithmetic and copies ran while one was open for 28% -> 0% of each run, Pallas kernels for 0% -> 26%
where the time goes in v1:
time: 19.6 us; the launch traced here: 19.3 us
  Pallas kernels  8.35 us (43%)
  starting transfers between devices  7.36 us (38%)
  waiting for transfers between devices  2.9 us (15%)
  between operations  0.66 us (3%)
    all_to_all x1, starting transfers between devices, shards(): lax.all_to_all(send, ('wide', 'tp'), split_axis=0, concat_axis=0, tiled=T...  7.36 us
    pallas_call x1, Pallas kernels, resident(): pl.pallas_call(resident_kernel, out_shape=jax.ShapeDtypeStruct(query.shap...  5.02 us
    all_to_all x1, waiting for transfers between devices, shards(): lax.all_to_all(send, ('wide', 'tp'), split_axis=0, concat_axis=0, tiled=T...  2.9 us
    pallas_call x1, Pallas kernels, arrivals(): pl.pallas_call(functools.partial(arrival_kernel, tp), out_shape=jax.Shape...  1.68 us
    pallas_call x1, Pallas kernels, pack(): pl.pallas_call(functools.partial(pack_kernel, tp, 2 * block_tokens), out_...  1.66 us
  transfers between devices with their start and end apart: 1, of which 1 were waited for; matrix products, arithmetic and copies ran while one was open for 0% of the time, Pallas kernels for 26%

profile of v1, /device:TPU:0, one launch (start us, length us, event | category | flops | bytes accessed | tf_op | source)
XLA Modules:
  0.0 19.3 jit_solution(2417092485517923128)
XLA Ops:
  0.6 1.7 %pack.1 = bf16[16,2,16,128]{3,2,1,0:T(8,128)(2,1)} custom-call(s32[4]{0:T(128)} %dest_ref.1, s32[4]{0:T(128)} %blocks_ref.1, bf16[4,8,4,2,128]{4,3,2,1,0:T(2,128)(2,1)} %bitcast.46, bf16[4,16,4]{2,1,0:T(8,128)(2,1)} %bitcast.48), custom_call_target="tpu_custom_call" | custom-call | tf_op jit(solution)/shard_map/pack/pallas_call | solution.py:194
  2.3 7.4 %all-to-all-start = ((bf16[16,2,16,128]{3,2,1,0:T(8,128)(2,1)}), bf16[16,2,16,128]{3,2,1,0:T(8,128)(2,1)S(1)}, u32[]{:S(2)}, u32[]{:S(2)}) async-start(bf16[16,2,16,128]{3,2,1,0:T(8,128)(2,1)} %pack.1), calls=%async_computation | async-start | bytes 262144 | tf_op jit(solution)/shard_map/all_to_all | solution.py:285
  9.7 0.0 copy-start
  9.7 0.0 copy-start.1
  9.7 5.0 %resident.1 = bf16[8,64,128]{2,1,0:T(8,128)(2,1)} custom-call(s32[8]{0:T(128)} %len_ref.1, bf16[8,256,128]{2,1,0:T(8,128)(2,1)} %bitcast.42, bf16[8,2,2,64]{3,2,1,0:T(2,128)(2,1)} %bitcast.49, bf16[8,64,128]{2,1,0:T(8,128)(2,1)} %bitcast.43, bf16[8,8,128]{2,1,0:T(8,128)(2,1)} %bitcast.47), custom_call_target="tpu_custom_call" | custom-call | flops 67108864 | bytes 786432 | tf_op jit(solution)/shard_map/resident/pallas_call | solution.py:234
  14.7 2.9 %all-to-all-done.got_ref = bf16[16,2,16,128]{3,2,1,0:T(8,128)(2,1)S(1)} async-done(((bf16[16,2,16,128]{3,2,1,0:T(8,128)(2,1)}), bf16[16,2,16,128]{3,2,1,0:T(8,128)(2,1)S(1)}, u32[]{:S(2)}, u32[]{:S(2)}) %all-to-all-start) | async-done | bytes 131104 | tf_op jit(solution)/shard_map/all_to_all | solution.py:285
  17.6 0.0 copy-done
  17.6 0.0 copy-done.1
  17.6 1.7 %arrivals.1 = bf16[6,2,32,128]{3,2,1,0:T(8,128)(2,1)} custom-call(bf16[16,2,16,128]{3,2,1,0:T(8,128)(2,1)S(1)} %all-to-all-done.got_ref, bf16[6,2,32,128]{3,2,1,0:T(8,128)(2,1)S(1)} %bitcast.40, bf16[6,8,128]{2,1,0:T(8,128)(2,1)S(1)} %bitcast.41), custom_call_target="tpu_custom_call" | custom-call | tf_op jit(solution)/shard_map/arrivals/pallas_call | solution.py:253
Async XLA Ops:
  2.3 15.3 %all-to-all-start = ((bf16[16,2,16,128]{3,2,1,0:T(8,128)(2,1)}), bf16[16,2,16,128]{3,2,1,0:T(8,128)(2,1)S(1)}, u32[]{:S(2)}, u32[]{:S(2)}) async-start(bf16[16,2,16,128]{3,2,1,0:T(8,128)(2,1)} %pack.1), calls=%async_computation | async-start | bytes 262144 | tf_op jit(solution)/shard_map/all_to_all | solution.py:285
  9.7 7.9 %copy-start = (bf16[6,2,4096]{2,1,0:T(2,128)(2,1)S(1)}, bf16[6,2,4096]{2,1,0:T(2,128)(2,1)}, u32[]{:S(2)}) copy-start(bf16[6,2,4096]{2,1,0:T(2,128)(2,1)} %param.20) | copy-start | bytes 294916
  9.7 7.9 %copy-start.1 = (bf16[6,2,2,256]{3,2,1,0:T(2,128)(2,1)S(1)}, bf16[6,2,2,256]{3,2,1,0:T(2,128)(2,1)}, u32[]{:S(2)}) copy-start(bf16[6,2,2,256]{3,2,1,0:T(2,128)(2,1)} %param.21) | copy-start | bytes 36868

commit v2 on v1

--- a/solution.py
+++ b/solution.py
@@ -38,28 +38,36 @@
     return pl.BlockSpec(memory_space=memory_space)
 
 
-def pack_kernel(tp, block_rows, dest_ref, blocks_ref, codes_ref, scales_ref, send_ref):
+def pack_kernel(peers, tp, block_rows, dest_ref, blocks_ref, codes_ref, scales_ref, *refs):
     requests, tokens, heads = codes_ref.shape[:3]
     rows = 2 * tokens
     per_core = heads // tp
+    apart = len(refs) > 1
+    send_ref = refs[-1]
     send_ref[...] = jnp.full(send_ref.shape, EMPTY, BF16)
     row_block = iota((rows, HD), 0) // block_rows
+    here = lax.axis_index("wide") if apart else 0
+    core = lax.axis_index("tp") if apart else 0
 
     def place(r):
-        there = dest_ref[r]
+        there = lax.rem(dest_ref[r] - here + peers, peers)
         held = row_block < blocks_ref[r]
         scales = scales_ref[r].astype(F32)
         for j in range(heads):
             codes = codes_ref[r, :, j].astype(F32).reshape(rows, HD)
             values = codes * scales[:, j : j + 1]
             values = jnp.where(held, values, EMPTY).astype(BF16)
-            send_ref[there * tp + j // per_core, j % per_core] = values
+            to_core = lax.rem(j // per_core - core + tp, tp)
+            send_ref[there * tp + to_core, j % per_core] = values
 
     if requests <= 8:
         for r in range(requests):
             place(r)
     else:
         lax.fori_loop(0, requests, lambda r, c: (place(r), c)[1], 0)
+    if apart:
+        for k, ref in enumerate(refs[:-1]):
+            ref[...] = send_ref[k]
 
 
 def resident_kernel(len_ref, codes_ref, scales_ref, query_ref, new_ref, out_ref):
@@ -116,22 +124,35 @@
         out_ref[s] = (mixed / total).astype(BF16)
 
 
-def arrival_kernel(tp, got_ref, query_ref, new_ref, out_ref):
-    chunks, heads, chunk_rows = got_ref.shape[:3]
-    slots, _, per_head = query_ref.shape[:3]
+def arrival_kernel(peers, tp, query_ref, new_ref, *refs):
+    got_refs, out_ref = refs[:-1], refs[-1]
+    apart = len(got_refs) > 1
+    slots, heads, per_head = query_ref.shape[:3]
+    chunk_rows = got_refs[0].shape[-2]
     rows = slots * per_head
-    columns = chunks * chunk_rows
+    columns = peers * tp * chunk_rows
     sender_rows = tp * chunk_rows
     piece = min(columns, 256)
 
-    caches = [got_ref[:, h].reshape(columns, HD) for h in range(heads)]
+    if apart:
+        caches = [jnp.concatenate([ref[h] for ref in got_refs], axis=0) for h in range(heads)]
+        here = lax.axis_index("wide")
+    else:
+        caches = [got_refs[0][:, h].reshape(columns, HD) for h in range(heads)]
+
+    def sender(index):
+        return lax.rem(here - index + peers, peers) if apart else index
+
     ones = jnp.ones((8, HD), BF16)
     sums = dot_nt(ones, caches[0])
     col = iota((8, columns), 1)
     held = sums < EMPTY
     first = jnp.where(held & (col % sender_rows == 0), 1.0, 0.0).astype(BF16)
     before = jnp.where(
-        iota((piece, piece), 0) // sender_rows < iota((piece, piece), 1) // sender_rows, 1.0, 0.0
+        sender(iota((piece, piece), 0) // sender_rows)
+        < sender(iota((piece, piece), 1) // sender_rows),
+        1.0,
+        0.0,
     ).astype(BF16)
     base = jnp.zeros((8, 1), F32)
     ranks = []
@@ -185,19 +206,38 @@
         out_ref[:, h] = (mixed / total).astype(BF16).reshape(slots, per_head, HD)
 
 
-def pack(pre_codes, pre_scales, req_dest, req_blocks, peers, tp):
+def pack(pre_codes, pre_scales, req_dest, req_blocks, peers, tp, apart):
     requests, blocks, block_tokens = pre_codes.shape[:3]
     tokens = blocks * block_tokens
     codes = pre_codes.reshape(requests, tokens, 2, KVH, HD).transpose(0, 1, 3, 2, 4)
     scales = pre_scales.reshape(requests, tokens * 2, KVH)
-    out = jax.ShapeDtypeStruct((peers * tp, KVH // tp, tokens * 2, HD), BF16)
+    chunk = (KVH // tp, tokens * 2, HD)
+    send = (peers * tp,) + chunk
     return pl.pallas_call(
-        functools.partial(pack_kernel, tp, 2 * block_tokens),
-        out_shape=out,
+        functools.partial(pack_kernel, peers, tp, 2 * block_tokens),
+        out_shape=[jax.ShapeDtypeStruct(chunk, BF16)] * (peers * tp)
+        if apart
+        else [jax.ShapeDtypeStruct(send, BF16)],
         in_specs=[whole(pltpu.SMEM), whole(pltpu.SMEM), whole(), whole()],
-        out_specs=whole(),
+        out_specs=[whole()] * (peers * tp if apart else 1),
+        scratch_shapes=[pltpu.VMEM(send, BF16)] if apart else [],
         name="pack",
     )(req_dest, req_blocks, codes, scales)
+
+
+def exchange(chunks, peers, tp):
+    if len(chunks) == 1:
+        return [lax.all_to_all(chunks[0], ("wide", "tp"), split_axis=0, concat_axis=0, tiled=True)]
+    got = [chunks[0]]
+    for k in range(1, peers * tp):
+        ahead, across = divmod(k, tp)
+        pairs = [
+            (w * tp + t, (w + ahead) % peers * tp + (t + across) % tp)
+            for w in range(peers)
+            for t in range(tp)
+        ]
+        got.append(lax.ppermute(chunks[k], ("wide", "tp"), pairs))
+    return got
 
 
 def query_rows(query):
@@ -244,25 +284,28 @@
     return from_rows(out, res_query.shape)
 
 
-def arrivals(got, arr_query, arr_new, tp):
+def arrivals(got, arr_query, arr_new, peers, tp):
     slots, steps, width = arr_query.shape
     heads = width // (HD * GROUP)
     query = query_rows(arr_query).reshape(slots, heads, GROUP * steps, HD)
     new = new_rows_of(arr_new)
     size = max(n for n in range(1, 7) if slots % n == 0)
+
+    def fixed(ref):
+        return pl.BlockSpec(ref.shape, lambda i: (0,) * ref.ndim)
+
+    def by_slot(ref):
+        return pl.BlockSpec((size,) + ref.shape[1:], lambda i: (i,) + (0,) * (ref.ndim - 1))
+
     out = pl.pallas_call(
-        functools.partial(arrival_kernel, tp),
+        functools.partial(arrival_kernel, peers, tp),
         out_shape=jax.ShapeDtypeStruct(query.shape, BF16),
         grid=(slots // size,),
-        in_specs=[
-            pl.BlockSpec(got.shape, lambda i: (0, 0, 0, 0)),
-            pl.BlockSpec((size,) + query.shape[1:], lambda i: (i, 0, 0, 0)),
-            pl.BlockSpec((size,) + new.shape[1:], lambda i: (i, 0, 0)),
-        ],
-        out_specs=pl.BlockSpec((size,) + query.shape[1:], lambda i: (i, 0, 0, 0)),
+        in_specs=[by_slot(query), by_slot(new)] + [fixed(g) for g in got],
+        out_specs=by_slot(query),
         compiler_params=pltpu.CompilerParams(vmem_limit_bytes=48 * 2**20),
         name="arrivals",
-    )(got, query, new)
+    )(query, new, *got)
     return from_rows(out, arr_query.shape)
 
 
@@ -281,10 +324,10 @@
 ):
     peers = lax.axis_size("wide")
     tp = lax.axis_size("tp")
-    send = pack(pre_codes, pre_scales, req_dest, req_blocks, peers, tp)
-    got = lax.all_to_all(send, ("wide", "tp"), split_axis=0, concat_axis=0, tiled=True)
+    chunks = pack(pre_codes, pre_scales, req_dest, req_blocks, peers, tp, peers * tp <= 16)
+    got = exchange(chunks, peers, tp)
     res_out = resident(res_codes, res_scales, res_len, res_query, res_new)
-    arr_out = arrivals(got, arr_query, arr_new, tp)
+    arr_out = arrivals(got, arr_query, arr_new, peers, tp)
     return (res_out, arr_out)
 
 

time: 19.6 us -> 31.4 us (1.60)
  starting transfers between devices: 7.36 us -> 21.9 us
  waiting for transfers between devices: 2.9 us -> 0.15 us
    ppermute x0 -> x15, starting transfers between devices: none -> 21.9 us  [exchange(): got.append(lax.ppermute(chunks[k], ('wide', 'tp'), pairs))]
    all_to_all x1 -> x0, starting transfers between devices: 7.36 us -> none  [shards(): lax.all_to_all(send, ('wide', 'tp'), split_axis=0, concat_axis=0, tiled=T...]
    all_to_all x1 -> x0, waiting for transfers between devices: 2.9 us -> none  [shards(): lax.all_to_all(send, ('wide', 'tp'), split_axis=0, concat_axis=0, tiled=T...]
  transfers between devices with their start and end apart: 1 -> 15, of which waited for: 1 -> 1; matrix products, arithmetic and copies ran while one was open for 0% -> 0% of each run, Pallas kernels for 26% -> 16%
where the time goes in v2:
time: 31.4 us; the launch traced here: 31.2 us
  starting transfers between devices  21.9 us (70%)
  Pallas kernels  8.38 us (27%)
  between operations  0.7 us (2%)
    ppermute x15, starting transfers between devices, exchange(): got.append(lax.ppermute(chunks[k], ('wide', 'tp'), pairs))  21.9 us
    pallas_call x1, Pallas kernels, resident(): pl.pallas_call(resident_kernel, out_shape=jax.ShapeDtypeStruct(query.shap...  5.01 us
    pallas_call x1, Pallas kernels, arrivals(): pl.pallas_call(functools.partial(arrival_kernel, peers, tp), out_shape=ja...  1.69 us
    pallas_call x1, Pallas kernels, pack(): pl.pallas_call(functools.partial(pack_kernel, peers, tp, 2 * block_tokens...  1.68 us
  transfers between devices with their start and end apart: 15, of which 1 were waited for; matrix products, arithmetic and copies ran while one was open for 0% of the time, Pallas kernels for 16%

profile of v2, /device:TPU:0, one launch (start us, length us, event | category | flops | bytes accessed | tf_op | source)
XLA Modules:
  0.0 31.2 jit_solution(8220428543168393151)
XLA Ops:
  0.6 1.7 %pack.1 = (bf16[2,16,128]{2,1,0:T(8,128)(2,1)}, bf16[2,16,128]{2,1,0:T(8,128)(2,1)}, bf16[2,16,128]{2,1,0:T(8,128)(2,1)}, bf16[2,16,128]{2,1,0:T(8,128)(2,1)}, b...) custom-call(s32[4]{0:T(128)} %dest_ref.1, ...), custom_call_target="tpu_custom_call" | custom-call | tf_op jit(solution)/shard_map/pack/pallas_call | solution.py:216
  2.3 0.5 %collective-permute-start = (bf16[2,16,128]{2,1,0:T(8,128)(2,1)}, bf16[2,16,128]{2,1,0:T(8,128)(2,1)S(1)}, u32[]{:S(2)}, u32[]{:S(2)}) collective-permute-start(bf16[2,16,128]{2,1,0:T(8,128)(2,1)} %get-tuple-element.19), channel_id=1, source_target_pairs={{0,1},{1,0},{2,3},{3,2},{4,5},{5,4},{6,7},{7,6},{8,9},{9,8},{10,11... | collective-permute-start | bytes 24584 | tf_op jit(solution)/shard_map/ppermute | solution.py:239
  2.8 2.6 %collective-permute-start.1 = (bf16[2,16,128]{2,1,0:T(8,128)(2,1)}, bf16[2,16,128]{2,1,0:T(8,128)(2,1)S(1)}, u32[]{:S(2)}, u32[]{:S(2)}) collective-permute-start(bf16[2,16,128]{2,1,0:T(8,128)(2,1)} %get-tuple-element.20), channel_id=1, source_target_pairs={{0,2},{1,3},{2,4},{3,5},{4,6},{5,7},{6,8},{7,9},{8,10},{9,11},{10,... | collective-permute-start | bytes 24584 | tf_op jit(solution)/shard_map/ppermute | solution.py:239
  5.4 3.3 %collective-permute-start.10 = (bf16[2,16,128]{2,1,0:T(8,128)(2,1)}, bf16[2,16,128]{2,1,0:T(8,128)(2,1)S(1)}, u32[]{:S(2)}, u32[]{:S(2)}) collective-permute-start(bf16[2,16,128]{2,1,0:T(8,128)(2,1)} %get-tuple-element.29), channel_id=1, source_target_pairs={{0,11},{1,10},{2,13},{3,12},{4,15},{5,14},{6,1},{7,0},{8,3},{9,2},... | collective-permute-start | bytes 24584 | tf_op jit(solution)/shard_map/ppermute | solution.py:239
  8.7 1.3 %collective-permute-start.11 = (bf16[2,16,128]{2,1,0:T(8,128)(2,1)}, bf16[2,16,128]{2,1,0:T(8,128)(2,1)S(1)}, u32[]{:S(2)}, u32[]{:S(2)}) collective-permute-start(bf16[2,16,128]{2,1,0:T(8,128)(2,1)} %get-tuple-element.30), channel_id=1, source_target_pairs={{0,12},{1,13},{2,14},{3,15},{4,0},{5,1},{6,2},{7,3},{8,4},{9,5},{1... | collective-permute-start | bytes 24584 | tf_op jit(solution)/shard_map/ppermute | solution.py:239
  10.1 0.1 collective-permute-start.12
  10.2 0.5 %collective-permute-start.13 = (bf16[2,16,128]{2,1,0:T(8,128)(2,1)}, bf16[2,16,128]{2,1,0:T(8,128)(2,1)S(1)}, u32[]{:S(2)}, u32[]{:S(2)}) collective-permute-start(bf16[2,16,128]{2,1,0:T(8,128)(2,1)} %get-tuple-element.32), channel_id=1, source_target_pairs={{0,14},{1,15},{2,0},{3,1},{4,2},{5,3},{6,4},{7,5},{8,6},{9,7},{10,... | collective-permute-start | bytes 24584 | tf_op jit(solution)/shard_map/ppermute | solution.py:239
  10.7 0.0 collective-permute-done.1.refs_2_
  10.7 2.2 %collective-permute-start.14 = (bf16[2,16,128]{2,1,0:T(8,128)(2,1)}, bf16[2,16,128]{2,1,0:T(8,128)(2,1)S(1)}, u32[]{:S(2)}, u32[]{:S(2)}) collective-permute-start(bf16[2,16,128]{2,1,0:T(8,128)(2,1)} %get-tuple-element.33), channel_id=1, source_target_pairs={{0,15},{1,14},{2,1},{3,0},{4,3},{5,2},{6,5},{7,4},{8,7},{9,6},{10,... | collective-permute-start | bytes 24584 | tf_op jit(solution)/shard_map/ppermute | solution.py:239
  12.9 0.0 collective-permute-start.2
  12.9 0.0 collective-permute-done.11.refs_12_
  12.9 1.1 %collective-permute-start.3 = (bf16[2,16,128]{2,1,0:T(8,128)(2,1)}, bf16[2,16,128]{2,1,0:T(8,128)(2,1)S(1)}, u32[]{:S(2)}, u32[]{:S(2)}) collective-permute-start(bf16[2,16,128]{2,1,0:T(8,128)(2,1)} %get-tuple-element.22), channel_id=1, source_target_pairs={{0,4},{1,5},{2,6},{3,7},{4,8},{5,9},{6,10},{7,11},{8,12},{9,13},{1... | collective-permute-start | bytes 24584 | tf_op jit(solution)/shard_map/ppermute | solution.py:239
  14.0 0.0 collective-permute-done.12.refs_13_
  14.0 1.1 %collective-permute-start.4 = (bf16[2,16,128]{2,1,0:T(8,128)(2,1)}, bf16[2,16,128]{2,1,0:T(8,128)(2,1)S(1)}, u32[]{:S(2)}, u32[]{:S(2)}) collective-permute-start(bf16[2,16,128]{2,1,0:T(8,128)(2,1)} %get-tuple-element.23), channel_id=1, source_target_pairs={{0,5},{1,4},{2,7},{3,6},{4,9},{5,8},{6,11},{7,10},{8,13},{9,12},{1... | collective-permute-start | bytes 24584 | tf_op jit(solution)/shard_map/ppermute | solution.py:239
  15.1 0.0 collective-permute-done.13.refs_14_
  15.1 3.1 %collective-permute-start.5 = (bf16[2,16,128]{2,1,0:T(8,128)(2,1)}, bf16[2,16,128]{2,1,0:T(8,128)(2,1)S(1)}, u32[]{:S(2)}, u32[]{:S(2)}) collective-permute-start(bf16[2,16,128]{2,1,0:T(8,128)(2,1)} %get-tuple-element.24), channel_id=1, source_target_pairs={{0,6},{1,7},{2,8},{3,9},{4,10},{5,11},{6,12},{7,13},{8,14},{9,15},... | collective-permute-start | bytes 24584 | tf_op jit(solution)/shard_map/ppermute | solution.py:239
  18.2 0.6 %collective-permute-start.6 = (bf16[2,16,128]{2,1,0:T(8,128)(2,1)}, bf16[2,16,128]{2,1,0:T(8,128)(2,1)S(1)}, u32[]{:S(2)}, u32[]{:S(2)}) collective-permute-start(bf16[2,16,128]{2,1,0:T(8,128)(2,1)} %get-tuple-element.25), channel_id=1, source_target_pairs={{0,7},{1,6},{2,9},{3,8},{4,11},{5,10},{6,13},{7,12},{8,15},{9,14},... | collective-permute-start | bytes 24584 | tf_op jit(solution)/shard_map/ppermute | solution.py:239
  18.8 0.1 collective-permute-done.2.refs_3_
  18.9 1.6 %collective-permute-start.7 = (bf16[2,16,128]{2,1,0:T(8,128)(2,1)S(1)}, bf16[2,16,128]{2,1,0:T(8,128)(2,1)S(1)}, u32[]{:S(2)}, u32[]{:S(2)}) collective-permute-start(bf16[2,16,128]{2,1,0:T(8,128)(2,1)S(1)} %copy-done.5), channel_id=1, source_target_pairs={{0,8},{1,9},{2,10},{3,11},{4,12},{5,13},{6,14},{7,15},{8,0},{9,1},... | collective-permute-start | bytes 24584 | tf_op jit(solution)/shard_map/ppermute | solution.py:239
  20.5 0.0 collective-permute-done.3.refs_4_
  20.5 0.9 %collective-permute-start.8 = (bf16[2,16,128]{2,1,0:T(8,128)(2,1)S(1)}, bf16[2,16,128]{2,1,0:T(8,128)(2,1)S(1)}, u32[]{:S(2)}, u32[]{:S(2)}) collective-permute-start(bf16[2,16,128]{2,1,0:T(8,128)(2,1)S(1)} %copy-done.4), channel_id=1, source_target_pairs={{0,9},{1,8},{2,11},{3,10},{4,13},{5,12},{6,15},{7,14},{8,1},{9,0},... | collective-permute-start | bytes 24584 | tf_op jit(solution)/shard_map/ppermute | solution.py:239
  21.4 3.0 %collective-permute-start.9 = (bf16[2,16,128]{2,1,0:T(8,128)(2,1)S(1)}, bf16[2,16,128]{2,1,0:T(8,128)(2,1)S(1)}, u32[]{:S(2)}, u32[]{:S(2)}) collective-permute-start(bf16[2,16,128]{2,1,0:T(8,128)(2,1)S(1)} %copy-done.3), channel_id=1, source_target_pairs={{0,10},{1,11},{2,12},{3,13},{4,14},{5,15},{6,0},{7,1},{8,2},{9,3},... | collective-permute-start | bytes 24584 | tf_op jit(solution)/shard_map/ppermute | solution.py:239
  24.4 5.0 %resident.1 = bf16[8,64,128]{2,1,0:T(8,128)(2,1)} custom-call(s32[8]{0:T(128)} %len_ref.1, bf16[8,256,128]{2,1,0:T(8,128)(2,1)} %bitcast.42, bf16[8,2,2,64]{3,2,1,0:T(2,128)(2,1)} %bitcast.49, bf16[8,64,128]{2,1,0:T(8,128)(2,1)} %bitcast.43, bf16[8,8,128]{2,1,0:T(8,128)(2,1)} %bitcast.47), custom_call_target="tpu_custom_call" | custom-call | flops 67108864 | bytes 786432 | tf_op jit(solution)/shard_map/resident/pallas_call | solution.py:274
  29.5 1.7 %arrivals.1 = bf16[6,2,32,128]{3,2,1,0:T(8,128)(2,1)} custom-call(bf16[6,2,32,128]{3,2,1,0:T(8,128)(2,1)S(1)} %bitcast.40, bf16[6,8,128]{2,1,0:T(8,128)(2,1)S(1)} %bitcast.41, bf16[2,16,128]{2,1,0:T(8,128)(2,1)S(1)} %copy-done.2, bf16[2,16,128]{2,1,0:T(8,128)(2,1)S(1)} %collective-permute-done.refs_1_, ...), custom_call_target="tpu_custom_call" | custom-call | tf_op jit(solution)/shard_map/arrivals/pallas_call | solution.py:300
  (21 shorter events, 0.0 us)
Async XLA Ops:
  2.3 7.9 %collective-permute-start = (bf16[2,16,128]{2,1,0:T(8,128)(2,1)}, bf16[2,16,128]{2,1,0:T(8,128)(2,1)S(1)}, u32[]{:S(2)}, u32[]{:S(2)}) collective-permute-start(bf16[2,16,128]{2,1,0:T(8,128)(2,1)} %get-tuple-element.19), channel_id=1, source_target_pairs={{0,1},{1,0},{2,3},{3,2},{4,5},{5,4},{6,7},{7,6},{8,9},{9,8},{10,11... | collective-permute-start | bytes 24584 | tf_op jit(solution)/shard_map/ppermute | solution.py:239
  2.8 7.9 %collective-permute-start.1 = (bf16[2,16,128]{2,1,0:T(8,128)(2,1)}, bf16[2,16,128]{2,1,0:T(8,128)(2,1)S(1)}, u32[]{:S(2)}, u32[]{:S(2)}) collective-permute-start(bf16[2,16,128]{2,1,0:T(8,128)(2,1)} %get-tuple-element.20), channel_id=1, source_target_pairs={{0,2},{1,3},{2,4},{3,5},{4,6},{5,7},{6,8},{7,9},{8,10},{9,11},{10,... | collective-permute-start | bytes 24584 | tf_op jit(solution)/shard_map/ppermute | solution.py:239
  5.4 13.5 %copy-start.5 = (bf16[2,16,128]{2,1,0:T(8,128)(2,1)S(1)}, bf16[2,16,128]{2,1,0:T(8,128)(2,1)}, u32[]{:S(2)}) copy-start(bf16[2,16,128]{2,1,0:T(8,128)(2,1)} %get-tuple-element.26) | copy-start | bytes 24580
  5.4 7.5 %collective-permute-start.10 = (bf16[2,16,128]{2,1,0:T(8,128)(2,1)}, bf16[2,16,128]{2,1,0:T(8,128)(2,1)S(1)}, u32[]{:S(2)}, u32[]{:S(2)}) collective-permute-start(bf16[2,16,128]{2,1,0:T(8,128)(2,1)} %get-tuple-element.29), channel_id=1, source_target_pairs={{0,11},{1,10},{2,13},{3,12},{4,15},{5,14},{6,1},{7,0},{8,3},{9,2},... | collective-permute-start | bytes 24584 | tf_op jit(solution)/shard_map/ppermute | solution.py:239
  8.7 4.2 %collective-permute-start.11 = (bf16[2,16,128]{2,1,0:T(8,128)(2,1)}, bf16[2,16,128]{2,1,0:T(8,128)(2,1)S(1)}, u32[]{:S(2)}, u32[]{:S(2)}) collective-permute-start(bf16[2,16,128]{2,1,0:T(8,128)(2,1)} %get-tuple-element.30), channel_id=1, source_target_pairs={{0,12},{1,13},{2,14},{3,15},{4,0},{5,1},{6,2},{7,3},{8,4},{9,5},{1... | collective-permute-start | bytes 24584 | tf_op jit(solution)/shard_map/ppermute | solution.py:239
  10.1 3.9 %collective-permute-start.12 = (bf16[2,16,128]{2,1,0:T(8,128)(2,1)}, bf16[2,16,128]{2,1,0:T(8,128)(2,1)S(1)}, u32[]{:S(2)}, u32[]{:S(2)}) collective-permute-start(bf16[2,16,128]{2,1,0:T(8,128)(2,1)} %get-tuple-element.31), channel_id=1, source_target_pairs={{0,13},{1,12},{2,15},{3,14},{4,1},{5,0},{6,3},{7,2},{8,5},{9,4},{1... | collective-permute-start | bytes 24584 | tf_op jit(solution)/shard_map/ppermute | solution.py:239
  10.2 10.3 %copy-start.4 = (bf16[2,16,128]{2,1,0:T(8,128)(2,1)S(1)}, bf16[2,16,128]{2,1,0:T(8,128)(2,1)}, u32[]{:S(2)}) copy-start(bf16[2,16,128]{2,1,0:T(8,128)(2,1)} %get-tuple-element.27) | copy-start | bytes 24580
  10.2 4.9 %collective-permute-start.13 = (bf16[2,16,128]{2,1,0:T(8,128)(2,1)}, bf16[2,16,128]{2,1,0:T(8,128)(2,1)S(1)}, u32[]{:S(2)}, u32[]{:S(2)}) collective-permute-start(bf16[2,16,128]{2,1,0:T(8,128)(2,1)} %get-tuple-element.32), channel_id=1, source_target_pairs={{0,14},{1,15},{2,0},{3,1},{4,2},{5,3},{6,4},{7,5},{8,6},{9,7},{10,... | collective-permute-start | bytes 24584 | tf_op jit(solution)/shard_map/ppermute | solution.py:239
  10.7 10.7 %copy-start.3 = (bf16[2,16,128]{2,1,0:T(8,128)(2,1)S(1)}, bf16[2,16,128]{2,1,0:T(8,128)(2,1)}, u32[]{:S(2)}) copy-start(bf16[2,16,128]{2,1,0:T(8,128)(2,1)} %get-tuple-element.28) | copy-start | bytes 24580
  10.7 7.5 %collective-permute-start.14 = (bf16[2,16,128]{2,1,0:T(8,128)(2,1)}, bf16[2,16,128]{2,1,0:T(8,128)(2,1)S(1)}, u32[]{:S(2)}, u32[]{:S(2)}) collective-permute-start(bf16[2,16,128]{2,1,0:T(8,128)(2,1)} %get-tuple-element.33), channel_id=1, source_target_pairs={{0,15},{1,14},{2,1},{3,0},{4,3},{5,2},{6,5},{7,4},{8,7},{9,6},{10,... | collective-permute-start | bytes 24584 | tf_op jit(solution)/shard_map/ppermute | solution.py:239
  12.9 6.0 %collective-permute-start.2 = (bf16[2,16,128]{2,1,0:T(8,128)(2,1)}, bf16[2,16,128]{2,1,0:T(8,128)(2,1)S(1)}, u32[]{:S(2)}, u32[]{:S(2)}) collective-permute-start(bf16[2,16,128]{2,1,0:T(8,128)(2,1)} %get-tuple-element.21), channel_id=1, source_target_pairs={{0,3},{1,2},{2,5},{3,4},{4,7},{5,6},{6,9},{7,8},{8,11},{9,10},{10,... | collective-permute-start | bytes 24584 | tf_op jit(solution)/shard_map/ppermute | solution.py:239
  12.9 7.6 %collective-permute-start.3 = (bf16[2,16,128]{2,1,0:T(8,128)(2,1)}, bf16[2,16,128]{2,1,0:T(8,128)(2,1)S(1)}, u32[]{:S(2)}, u32[]{:S(2)}) collective-permute-start(bf16[2,16,128]{2,1,0:T(8,128)(2,1)} %get-tuple-element.22), channel_id=1, source_target_pairs={{0,4},{1,5},{2,6},{3,7},{4,8},{5,9},{6,10},{7,11},{8,12},{9,13},{1... | collective-permute-start | bytes 24584 | tf_op jit(solution)/shard_map/ppermute | solution.py:239
  14.0 7.3 %collective-permute-start.4 = (bf16[2,16,128]{2,1,0:T(8,128)(2,1)}, bf16[2,16,128]{2,1,0:T(8,128)(2,1)S(1)}, u32[]{:S(2)}, u32[]{:S(2)}) collective-permute-start(bf16[2,16,128]{2,1,0:T(8,128)(2,1)} %get-tuple-element.23), channel_id=1, source_target_pairs={{0,5},{1,4},{2,7},{3,6},{4,9},{5,8},{6,11},{7,10},{8,13},{9,12},{1... | collective-permute-start | bytes 24584 | tf_op jit(solution)/shard_map/ppermute | solution.py:239
  15.1 14.3 %collective-permute-start.5 = (bf16[2,16,128]{2,1,0:T(8,128)(2,1)}, bf16[2,16,128]{2,1,0:T(8,128)(2,1)S(1)}, u32[]{:S(2)}, u32[]{:S(2)}) collective-permute-start(bf16[2,16,128]{2,1,0:T(8,128)(2,1)} %get-tuple-element.24), channel_id=1, source_target_pairs={{0,6},{1,7},{2,8},{3,9},{4,10},{5,11},{6,12},{7,13},{8,14},{9,15},... | collective-permute-start | bytes 24584 | tf_op jit(solution)/shard_map/ppermute | solution.py:239
  18.2 11.2 %collective-permute-start.6 = (bf16[2,16,128]{2,1,0:T(8,128)(2,1)}, bf16[2,16,128]{2,1,0:T(8,128)(2,1)S(1)}, u32[]{:S(2)}, u32[]{:S(2)}) collective-permute-start(bf16[2,16,128]{2,1,0:T(8,128)(2,1)} %get-tuple-element.25), channel_id=1, source_target_pairs={{0,7},{1,6},{2,9},{3,8},{4,11},{5,10},{6,13},{7,12},{8,15},{9,14},... | collective-permute-start | bytes 24584 | tf_op jit(solution)/shard_map/ppermute | solution.py:239
  18.9 10.6 %collective-permute-start.7 = (bf16[2,16,128]{2,1,0:T(8,128)(2,1)S(1)}, bf16[2,16,128]{2,1,0:T(8,128)(2,1)S(1)}, u32[]{:S(2)}, u32[]{:S(2)}) collective-permute-start(bf16[2,16,128]{2,1,0:T(8,128)(2,1)S(1)} %copy-done.5), channel_id=1, source_target_pairs={{0,8},{1,9},{2,10},{3,11},{4,12},{5,13},{6,14},{7,15},{8,0},{9,1},... | collective-permute-start | bytes 24584 | tf_op jit(solution)/shard_map/ppermute | solution.py:239
  20.5 9.0 %collective-permute-start.8 = (bf16[2,16,128]{2,1,0:T(8,128)(2,1)S(1)}, bf16[2,16,128]{2,1,0:T(8,128)(2,1)S(1)}, u32[]{:S(2)}, u32[]{:S(2)}) collective-permute-start(bf16[2,16,128]{2,1,0:T(8,128)(2,1)S(1)} %copy-done.4), channel_id=1, source_target_pairs={{0,9},{1,8},{2,11},{3,10},{4,13},{5,12},{6,15},{7,14},{8,1},{9,0},... | collective-permute-start | bytes 24584 | tf_op jit(solution)/shard_map/ppermute | solution.py:239
  21.4 8.1 %collective-permute-start.9 = (bf16[2,16,128]{2,1,0:T(8,128)(2,1)S(1)}, bf16[2,16,128]{2,1,0:T(8,128)(2,1)S(1)}, u32[]{:S(2)}, u32[]{:S(2)}) collective-permute-start(bf16[2,16,128]{2,1,0:T(8,128)(2,1)S(1)} %copy-done.3), channel_id=1, source_target_pairs={{0,10},{1,11},{2,12},{3,13},{4,14},{5,15},{6,0},{7,1},{8,2},{9,3},... | collective-permute-start | bytes 24584 | tf_op jit(solution)/shard_map/ppermute | solution.py:239
  24.4 5.1 %copy-start = (bf16[6,2,4096]{2,1,0:T(2,128)(2,1)S(1)}, bf16[6,2,4096]{2,1,0:T(2,128)(2,1)}, u32[]{:S(2)}) copy-start(bf16[6,2,4096]{2,1,0:T(2,128)(2,1)} %param.20) | copy-start | bytes 294916
  24.4 5.1 %copy-start.1 = (bf16[6,2,2,256]{3,2,1,0:T(2,128)(2,1)S(1)}, bf16[6,2,2,256]{3,2,1,0:T(2,128)(2,1)}, u32[]{:S(2)}) copy-start(bf16[6,2,2,256]{3,2,1,0:T(2,128)(2,1)} %param.21) | copy-start | bytes 36868
  24.4 5.1 %copy-start.2 = (bf16[2,16,128]{2,1,0:T(8,128)(2,1)S(1)}, bf16[2,16,128]{2,1,0:T(8,128)(2,1)}, u32[]{:S(2)}) copy-start(bf16[2,16,128]{2,1,0:T(8,128)(2,1)} %get-tuple-element.18.refs_0_) | copy-start | bytes 24580

commit v3 on v2

--- a/solution.py
+++ b/solution.py
@@ -18,6 +18,8 @@
 EMPTY = 1024.0
 SCORE_SCALE = 1.0 / math.sqrt(HD)
 
+SWAPS = 4
+
 BF16 = jnp.bfloat16
 F32 = jnp.float32
 
@@ -38,7 +40,7 @@
     return pl.BlockSpec(memory_space=memory_space)
 
 
-def pack_kernel(peers, tp, block_rows, dest_ref, blocks_ref, codes_ref, scales_ref, *refs):
+def pack_kernel(tp, block_rows, dest_ref, blocks_ref, codes_ref, scales_ref, *refs):
     requests, tokens, heads = codes_ref.shape[:3]
     rows = 2 * tokens
     per_core = heads // tp
@@ -46,19 +48,20 @@
     send_ref = refs[-1]
     send_ref[...] = jnp.full(send_ref.shape, EMPTY, BF16)
     row_block = iota((rows, HD), 0) // block_rows
-    here = lax.axis_index("wide") if apart else 0
-    core = lax.axis_index("tp") if apart else 0
+    here = lax.axis_index("wide") * tp + lax.axis_index("tp") if apart else 0
 
     def place(r):
-        there = lax.rem(dest_ref[r] - here + peers, peers)
         held = row_block < blocks_ref[r]
         scales = scales_ref[r].astype(F32)
         for j in range(heads):
             codes = codes_ref[r, :, j].astype(F32).reshape(rows, HD)
             values = codes * scales[:, j : j + 1]
             values = jnp.where(held, values, EMPTY).astype(BF16)
-            to_core = lax.rem(j // per_core - core + tp, tp)
-            send_ref[there * tp + to_core, j % per_core] = values
+            there = dest_ref[r] * tp + j // per_core
+            if apart:
+                there = jnp.bitwise_xor(there, here)
+                there = (there % SWAPS) * SWAPS + there // SWAPS
+            send_ref[there, j % per_core] = values
 
     if requests <= 8:
         for r in range(requests):
@@ -67,10 +70,11 @@
         lax.fori_loop(0, requests, lambda r, c: (place(r), c)[1], 0)
     if apart:
         for k, ref in enumerate(refs[:-1]):
-            ref[...] = send_ref[k]
-
-
-def resident_kernel(len_ref, codes_ref, scales_ref, query_ref, new_ref, out_ref):
+            ref[...] = send_ref[k * SWAPS : (k + 1) * SWAPS]
+
+
+def resident_kernel(first, len_ref, codes_ref, scales_ref, query_ref, new_ref, *refs):
+    out_ref = refs[-1]
     slots, rows = codes_ref.shape[:2]
     heads = scales_ref.shape[2]
     tokens = rows // (2 * heads)
@@ -105,7 +109,7 @@
         query = query_ref[s]
         new = new_ref[s]
         scores = jnp.where(
-            col_token < len_ref[s], dot_nt(query, cache) * SCORE_SCALE, NEGATIVE
+            col_token < len_ref[first + s], dot_nt(query, cache) * SCORE_SCALE, NEGATIVE
         )
         new_scores = jnp.where(new_ok, dot_nt(query, new) * SCORE_SCALE, NEGATIVE)
         top = jnp.maximum(
@@ -135,13 +139,15 @@
     piece = min(columns, 256)
 
     if apart:
-        caches = [jnp.concatenate([ref[h] for ref in got_refs], axis=0) for h in range(heads)]
+        chunks = [ref[0] for ref in got_refs[:SWAPS]]
+        chunks += [ref[k] for ref in got_refs[SWAPS:] for k in range(SWAPS)]
+        caches = [jnp.concatenate([chunk[h] for chunk in chunks], axis=0) for h in range(heads)]
         here = lax.axis_index("wide")
     else:
         caches = [got_refs[0][:, h].reshape(columns, HD) for h in range(heads)]
 
     def sender(index):
-        return lax.rem(here - index + peers, peers) if apart else index
+        return jnp.bitwise_xor(index, here) if apart else index
 
     ones = jnp.ones((8, HD), BF16)
     sums = dot_nt(ones, caches[0])
@@ -214,29 +220,32 @@
     chunk = (KVH // tp, tokens * 2, HD)
     send = (peers * tp,) + chunk
     return pl.pallas_call(
-        functools.partial(pack_kernel, peers, tp, 2 * block_tokens),
-        out_shape=[jax.ShapeDtypeStruct(chunk, BF16)] * (peers * tp)
+        functools.partial(pack_kernel, tp, 2 * block_tokens),
+        out_shape=[jax.ShapeDtypeStruct((SWAPS,) + chunk, BF16)] * SWAPS
         if apart
         else [jax.ShapeDtypeStruct(send, BF16)],
         in_specs=[whole(pltpu.SMEM), whole(pltpu.SMEM), whole(), whole()],
-        out_specs=[whole()] * (peers * tp if apart else 1),
+        out_specs=[whole()] * (SWAPS if apart else 1),
         scratch_shapes=[pltpu.VMEM(send, BF16)] if apart else [],
+        compiler_params=pltpu.CompilerParams(vmem_limit_bytes=16 * 2**20),
         name="pack",
     )(req_dest, req_blocks, codes, scales)
 
 
-def exchange(chunks, peers, tp):
-    if len(chunks) == 1:
-        return [lax.all_to_all(chunks[0], ("wide", "tp"), split_axis=0, concat_axis=0, tiled=True)]
-    got = [chunks[0]]
-    for k in range(1, peers * tp):
-        ahead, across = divmod(k, tp)
-        pairs = [
-            (w * tp + t, (w + ahead) % peers * tp + (t + across) % tp)
-            for w in range(peers)
-            for t in range(tp)
-        ]
-        got.append(lax.ppermute(chunks[k], ("wide", "tp"), pairs))
+def swap(x, bits, peers, tp):
+    pairs = [(i, i ^ bits) for i in range(peers * tp)]
+    return lax.ppermute(x, ("wide", "tp"), pairs)
+
+
+def exchange_low(chunks, peers, tp):
+    return [chunks[0]] + [swap(chunks[k], k, peers, tp) for k in range(1, SWAPS)]
+
+
+def exchange_high(chunks, peers, tp):
+    got = list(chunks)
+    for k in range(1, SWAPS):
+        part = jnp.stack([chunk[k] for chunk in chunks])
+        got.append(swap(part, k * SWAPS, peers, tp))
     return got
 
 
@@ -260,7 +269,7 @@
     return out.reshape(slots, width // HD, steps, HD).transpose(0, 2, 1, 3).reshape(shape)
 
 
-def resident(res_codes, res_scales, res_len, res_query, res_new):
+def resident(res_codes, res_scales, res_len, res_query, res_new, piece, pieces, before):
     slots, tokens, _, width = res_codes.shape
     heads = width // HD
     codes = (
@@ -270,18 +279,32 @@
     )
     scales = res_scales.transpose(0, 2, 3, 1)
     query = query_rows(res_query).reshape(slots, heads * GROUP * STEPS, HD)
-    work = slots * heads * GROUP * STEPS * tokens * heads * 2
+    new = new_rows_of(res_new)
+    size = slots // pieces
+    work = size * heads * GROUP * STEPS * tokens * heads * 2
+
+    def part(ref):
+        return pl.BlockSpec(
+            (size,) + ref.shape[1:], lambda i: (piece,) + (0,) * (ref.ndim - 1)
+        )
+
+    ins = [codes, scales, query, new]
     out = pl.pallas_call(
-        resident_kernel,
+        functools.partial(resident_kernel, piece * size),
         out_shape=jax.ShapeDtypeStruct(query.shape, BF16),
-        in_specs=[whole(pltpu.SMEM)] + [whole()] * 4,
-        out_specs=whole(),
+        grid=(1,),
+        in_specs=[whole(pltpu.SMEM)] + [part(x) for x in ins] + [whole(pl.ANY)] * len(before),
+        out_specs=part(query),
+        input_output_aliases={5: 0} if before else {},
         cost_estimate=pl.CostEstimate(
-            flops=4 * work * HD, bytes_accessed=2 * res_codes.size + 4 * query.size, transcendentals=work
+            flops=4 * work * HD,
+            bytes_accessed=2 * (codes.size + 2 * query.size) // pieces,
+            transcendentals=work,
         ),
+        compiler_params=pltpu.CompilerParams(vmem_limit_bytes=16 * 2**20),
         name="resident",
-    )(res_len, codes, scales, query, new_rows_of(res_new))
-    return from_rows(out, res_query.shape)
+    )(res_len, *ins, *before)
+    return out
 
 
 def arrivals(got, arr_query, arr_new, peers, tp):
@@ -303,7 +326,9 @@
         grid=(slots // size,),
         in_specs=[by_slot(query), by_slot(new)] + [fixed(g) for g in got],
         out_specs=by_slot(query),
-        compiler_params=pltpu.CompilerParams(vmem_limit_bytes=48 * 2**20),
+        compiler_params=pltpu.CompilerParams(
+            vmem_limit_bytes=(16 if peers * tp <= 16 else 48) * 2**20
+        ),
         name="arrivals",
     )(query, new, *got)
     return from_rows(out, arr_query.shape)
@@ -324,9 +349,18 @@
 ):
     peers = lax.axis_size("wide")
     tp = lax.axis_size("tp")
-    chunks = pack(pre_codes, pre_scales, req_dest, req_blocks, peers, tp, peers * tp <= 16)
-    got = exchange(chunks, peers, tp)
-    res_out = resident(res_codes, res_scales, res_len, res_query, res_new)
+    apart = peers * tp == SWAPS * SWAPS and tp < SWAPS
+    res = (res_codes, res_scales, res_len, res_query, res_new)
+    chunks = pack(pre_codes, pre_scales, req_dest, req_blocks, peers, tp, apart)
+    if apart:
+        near = exchange_low(chunks, peers, tp)
+        out = resident(*res, 0, 2, [])
+        got = exchange_high(near, peers, tp)
+        out = resident(*res, 1, 2, [out])
+    else:
+        got = [lax.all_to_all(chunks[0], ("wide", "tp"), split_axis=0, concat_axis=0, tiled=True)]
+        out = resident(*res, 0, 1, [])
+    res_out = from_rows(out, res_query.shape)
     arr_out = arrivals(got, arr_query, arr_new, peers, tp)
     return (res_out, arr_out)
 

time: 31.4 us -> 24.2 us (0.77)
  starting transfers between devices: 21.9 us -> 7.65 us
  local copies, waits for them, and re-layouts: 0.02 us -> 3.93 us
  waiting for transfers between devices: 0.15 us -> 3.27 us
    ppermute x15 -> x6, starting transfers between devices: 21.9 us -> 7.65 us  [swap(): return lax.ppermute(x, ('wide', 'tp'), pairs)]
    unnamed x12 -> x22, local copies, waits for them, and re-layouts: 0.02 us -> 3.92 us
    ppermute x15 -> x6, waiting for transfers between devices: 0.15 us -> 3.27 us  [swap(): return lax.ppermute(x, ('wide', 'tp'), pairs)]
    pallas_call x2 -> x3, Pallas kernels: 6.69 us -> 6.65 us  [the longest x2 5.94 us: resident(): pl.pallas_call(functools.partial(resident_kernel, piece * size), out_shap...]
  transfers between devices with their start and end apart: 15 -> 6, of which waited for: 1 -> 2; matrix products, arithmetic and copies ran while one was open for 0% -> 0% of each run, Pallas kernels for 16% -> 25%
where the time goes in v3:
time: 24.2 us; the launch traced here: 23.9 us
  Pallas kernels  8.33 us (34%)
  starting transfers between devices  7.65 us (32%)
  local copies, waits for them, and re-layouts  3.93 us (16%)
  waiting for transfers between devices  3.27 us (14%)
  between operations  0.73 us (3%)
    ppermute x6, starting transfers between devices, swap(): return lax.ppermute(x, ('wide', 'tp'), pairs)  7.65 us
    pallas_call x2, Pallas kernels, resident(): pl.pallas_call(functools.partial(resident_kernel, piece * size), out_shap...  5.94 us
    unnamed x22, local copies, waits for them, and re-layouts  3.92 us
    ppermute x6, waiting for transfers between devices, swap(): return lax.ppermute(x, ('wide', 'tp'), pairs)  3.27 us
    pallas_call x1, Pallas kernels, arrivals(): pl.pallas_call(functools.partial(arrival_kernel, peers, tp), out_shape=ja...  1.68 us
    pallas_call x1, Pallas kernels, pack(): pl.pallas_call(functools.partial(pack_kernel, tp, 2 * block_tokens), out_...  0.71 us
  transfers between devices with their start and end apart: 6, of which 2 were waited for; matrix products, arithmetic and copies ran while one was open for 0% of the time, Pallas kernels for 25%

profile of v3, /device:TPU:0, one launch (start us, length us, event | category | flops | bytes accessed | tf_op | source)
XLA Modules:
  0.0 23.9 jit_solution(11000852961518152159)
XLA Ops:
  0.7 0.6 %copy-done.9 = s32[4]{0:T(128)S(1)} copy-done((s32[4]{0:T(128)S(1)}, s32[4]{0:T(128)}, u32[]{:S(2)}) %copy-start.9) | copy-done | bytes 40
  1.3 0.0 copy-done.10
  1.3 0.8 %copy-done.4 = bf16[4,4,2,2,512]{4,3,2,1,0:T(2,128)(2,1)S(1)} copy-done((bf16[4,4,2,2,512]{4,3,2,1,0:T(2,128)(2,1)S(1)}, bf16[4,4,2,2,512]{4,3,2,1,0:T(2,128)(2,1)}, u32[]{:S(2)}) %copy-start.4) | copy-done | bytes 65560
  2.1 0.7 %copy-done.6 = bf16[4,4,2,2,4]{4,3,2,1,0:T(2,128)(2,1)S(1)} copy-done((bf16[4,4,2,2,4]{4,3,2,1,0:T(2,128)(2,1)S(1)}, bf16[4,4,2,2,4]{4,3,2,1,0:T(2,128)(2,1)}, u32[]{:S(2)}) %copy-start.6) | copy-done | bytes 536
  2.9 0.7 %pack.1 = (bf16[4,2,16,128]{3,2,1,0:T(8,128)(2,1)S(1)}, bf16[4,2,16,128]{3,2,1,0:T(8,128)(2,1)S(1)}, bf16[4,2,16,128]{3,2,1,0:T(8,128)(2,1)S(1)}, bf16[4,2,16,128]{3,2,1,0:T(8,128)(2,1)S(1)}) custom-call(s32[4]{0:T(128)S(1)} %copy-done.9, s32[4]{0:T(128)S(1)} %copy-done.10, bf16[4,8,4,2,128]{4,3,2,1,0:T(2,128)(2,1)S(1)} %bitcast.47, ...), custom_call_target="tpu_custom_call" | custom-call | tf_op jit(solution)/shard_map/pack/pallas_call | solution.py:222
  3.6 0.5 %collective-permute-start = (bf16[4,2,16,128]{3,2,1,0:T(8,128)(2,1)S(1)}, bf16[4,2,16,128]{3,2,1,0:T(8,128)(2,1)S(1)}, u32[]{:S(2)}, u32[]{:S(2)}) collective-permute-start(bf16[4,2,16,128]{3,2,1,0:T(8,128)(2,1)S(1)} %get-tuple-element.7), channel_id=1, source_target_pairs={{0,1},{1,0},{2,3},{3,2},{4,5},{5,4},{6,7},{7,6},{8,9},{9,8},{10,11... | collective-permute-start | bytes 98312 | tf_op jit(solution)/shard_map/ppermute | solution.py:237
  4.1 2.6 %collective-permute-start.1 = (bf16[4,2,16,128]{3,2,1,0:T(8,128)(2,1)S(1)}, bf16[4,2,16,128]{3,2,1,0:T(8,128)(2,1)S(1)}, u32[]{:S(2)}, u32[]{:S(2)}) collective-permute-start(bf16[4,2,16,128]{3,2,1,0:T(8,128)(2,1)S(1)} %get-tuple-element.8), channel_id=1, source_target_pairs={{0,2},{1,3},{2,0},{3,1},{4,6},{5,7},{6,4},{7,5},{8,10},{9,11},{10,... | collective-permute-start | bytes 98312 | tf_op jit(solution)/shard_map/ppermute | solution.py:237
  6.7 0.1 collective-permute-start.2
  6.7 0.0 collective-permute-done.refs_1_
  6.7 1.9 %collective-permute-done.1.refs_2_ = bf16[4,2,16,128]{3,2,1,0:T(8,128)(2,1)S(1)} collective-permute-done((bf16[4,2,16,128]{3,2,1,0:T(8,128)(2,1)S(1)}, bf16[4,2,16,128]{3,2,1,0:T(8,128)(2,1)S(1)}, u32[]{:S(2)}, u32[]{:S(2)}) %collective-permute-start.1) | collective-permute-done | bytes 32800 | tf_op jit(solution)/shard_map/ppermute | solution.py:237
  8.6 1.4 %collective-permute-done.2.refs_3_ = bf16[4,2,16,128]{3,2,1,0:T(8,128)(2,1)S(1)} collective-permute-done((bf16[4,2,16,128]{3,2,1,0:T(8,128)(2,1)S(1)}, bf16[4,2,16,128]{3,2,1,0:T(8,128)(2,1)S(1)}, u32[]{:S(2)}, u32[]{:S(2)}) %collective-permute-start.2) | collective-permute-done | bytes 32800 | tf_op jit(solution)/shard_map/ppermute | solution.py:237
  10.0 3.7 %collective-permute-start.5 = (bf16[4,2,16,128]{3,2,1,0:T(8,128)(2,1)S(1)}, bf16[4,2,16,128]{3,2,1,0:T(8,128)(2,1)S(1)}, u32[]{:S(2)}, u32[]{:S(2)}) collective-permute-start(bf16[4,2,16,128]{3,2,1,0:T(8,128)(2,1)S(1)} %pad_maximum_fusion.2), channel_id=1, source_target_pairs={{0,12},{1,13},{2,14},{3,15},{4,8},{5,9},{6,10},{7,11},{8,4},{9,5},... | collective-permute-start | bytes 98312 | tf_op jit(solution)/shard_map/ppermute | solution.py:237
  13.7 0.0 collective-permute-start.4
  13.7 0.0 copy-start.3
  13.7 0.0 copy-start.5
  13.7 0.8 %collective-permute-start.3 = (bf16[4,2,16,128]{3,2,1,0:T(8,128)(2,1)S(1)}, bf16[4,2,16,128]{3,2,1,0:T(8,128)(2,1)S(1)}, u32[]{:S(2)}, u32[]{:S(2)}) collective-permute-start(bf16[4,2,16,128]{3,2,1,0:T(8,128)(2,1)S(1)} %pad_maximum_fusion), channel_id=1, source_target_pairs={{0,4},{1,5},{2,6},{3,7},{4,0},{5,1},{6,2},{7,3},{8,12},{9,13},{10,... | collective-permute-start | bytes 98312 | tf_op jit(solution)/shard_map/ppermute | solution.py:237
  14.6 0.6 %copy-done.8 = s32[8]{0:T(128)S(1)} copy-done((s32[8]{0:T(128)S(1)}, s32[8]{0:T(128)}, u32[]{:S(2)}) %copy-start.8) | copy-done | bytes 56
  15.2 1.0 %copy-done = bf16[8,64,2,256]{3,2,1,0:T(2,128)(2,1)S(1)} copy-done((bf16[8,64,2,256]{3,2,1,0:T(2,128)(2,1)S(1)}, bf16[8,64,2,256]{3,2,1,0:T(2,128)(2,1)}, u32[]{:S(2)}) %copy-start) | copy-done | bytes 524312
  16.3 3.0 %resident.2.refs_0_ = bf16[8,64,128]{2,1,0:T(8,128)(2,1)} custom-call(s32[8]{0:T(128)S(1)} %copy-done.8, bf16[8,256,128]{2,1,0:T(8,128)(2,1)S(1)} %bitcast.40, bf16[8,2,2,64]{3,2,1,0:T(2,128)(2,1)S(1)} %bitcast.48, bf16[8,64,128]{2,1,0:T(8,128)(2,1)S(1)} %bitcast.42, bf16[8,8,128]{2,1,0:T(8,128)(2,1)S(1)} %bitcast.45), custom_call_target="tpu_custom_call" | custom-call | flops 33554432 | bytes 393216 | tf_op jit(solution)/shard_map/resident/pallas_call | solution.py:292
  19.2 3.0 %resident.3 = bf16[8,64,128]{2,1,0:T(8,128)(2,1)} custom-call(s32[8]{0:T(128)S(1)} %copy-done.8, bf16[8,256,128]{2,1,0:T(8,128)(2,1)S(1)} %bitcast.41, bf16[8,2,2,64]{3,2,1,0:T(2,128)(2,1)S(1)} %bitcast.49, bf16[8,64,128]{2,1,0:T(8,128)(2,1)S(1)} %bitcast.43, bf16[8,8,128]{2,1,0:T(8,128)(2,1)S(1)} %bitcast.46, ...), custom_call_target="tpu_custom_call", output_to_operand_aliasing={{}: (5, {})} | custom-call | flops 33554432 | bytes 393216 | tf_op jit(solution)/shard_map/resident/pallas_call | solution.py:292
  22.2 0.0 collective-permute-done.5.refs_6_
  22.2 0.0 collective-permute-done.4.refs_5_
  22.2 0.0 collective-permute-done.3.refs_4_
  22.2 1.7 %arrivals.1 = bf16[6,2,32,128]{3,2,1,0:T(8,128)(2,1)} custom-call(bf16[6,2,32,128]{3,2,1,0:T(8,128)(2,1)S(1)} %bitcast.44, bf16[6,8,128]{2,1,0:T(8,128)(2,1)S(1)} %bitcast.51, bf16[4,2,16,128]{3,2,1,0:T(8,128)(2,1)S(1)} %get-tuple-element.6.refs_0_, bf16[4,2,16,128]{3,2,1,0:T(8,128)(2,1)S(1)} %collective-permute-done.refs_1_, ...), custom_call_target="tpu_custom_call" | custom-call | tf_op jit(solution)/shard_map/arrivals/pallas_call | solution.py:323
  (21 shorter events, 0.1 us)
Async XLA Ops:
  0.6 0.7 %copy-start.9 = (s32[4]{0:T(128)S(1)}, s32[4]{0:T(128)}, u32[]{:S(2)}) copy-start(s32[4]{0:T(128)} %dest_ref.1) | copy-start | bytes 52
  0.6 0.7 %copy-start.10 = (s32[4]{0:T(128)S(1)}, s32[4]{0:T(128)}, u32[]{:S(2)}) copy-start(s32[4]{0:T(128)} %blocks_ref.1) | copy-start | bytes 52
  1.3 0.8 %copy-start.4 = (bf16[4,4,2,2,512]{4,3,2,1,0:T(2,128)(2,1)S(1)}, bf16[4,4,2,2,512]{4,3,2,1,0:T(2,128)(2,1)}, u32[]{:S(2)}) copy-start(bf16[4,4,2,2,512]{4,3,2,1,0:T(2,128)(2,1)} %param.11) | copy-start | bytes 196612
  2.1 0.7 %copy-start.6 = (bf16[4,4,2,2,4]{4,3,2,1,0:T(2,128)(2,1)S(1)}, bf16[4,4,2,2,4]{4,3,2,1,0:T(2,128)(2,1)}, u32[]{:S(2)}) copy-start(bf16[4,4,2,2,4]{4,3,2,1,0:T(2,128)(2,1)} %param.12) | copy-start | bytes 1540
  3.6 3.2 %collective-permute-start = (bf16[4,2,16,128]{3,2,1,0:T(8,128)(2,1)S(1)}, bf16[4,2,16,128]{3,2,1,0:T(8,128)(2,1)S(1)}, u32[]{:S(2)}, u32[]{:S(2)}) collective-permute-start(bf16[4,2,16,128]{3,2,1,0:T(8,128)(2,1)S(1)} %get-tuple-element.7), channel_id=1, source_target_pairs={{0,1},{1,0},{2,3},{3,2},{4,5},{5,4},{6,7},{7,6},{8,9},{9,8},{10,11... | collective-permute-start | bytes 98312 | tf_op jit(solution)/shard_map/ppermute | solution.py:237
  4.1 4.5 %collective-permute-start.1 = (bf16[4,2,16,128]{3,2,1,0:T(8,128)(2,1)S(1)}, bf16[4,2,16,128]{3,2,1,0:T(8,128)(2,1)S(1)}, u32[]{:S(2)}, u32[]{:S(2)}) collective-permute-start(bf16[4,2,16,128]{3,2,1,0:T(8,128)(2,1)S(1)} %get-tuple-element.8), channel_id=1, source_target_pairs={{0,2},{1,3},{2,0},{3,1},{4,6},{5,7},{6,4},{7,5},{8,10},{9,11},{10,... | collective-permute-start | bytes 98312 | tf_op jit(solution)/shard_map/ppermute | solution.py:237
  6.7 3.3 %collective-permute-start.2 = (bf16[4,2,16,128]{3,2,1,0:T(8,128)(2,1)S(1)}, bf16[4,2,16,128]{3,2,1,0:T(8,128)(2,1)S(1)}, u32[]{:S(2)}, u32[]{:S(2)}) collective-permute-start(bf16[4,2,16,128]{3,2,1,0:T(8,128)(2,1)S(1)} %get-tuple-element.9), channel_id=1, source_target_pairs={{0,3},{1,2},{2,1},{3,0},{4,7},{5,6},{6,5},{7,4},{8,11},{9,10},{10,... | collective-permute-start | bytes 98312 | tf_op jit(solution)/shard_map/ppermute | solution.py:237
  8.6 5.9 %copy-start.1 = (bf16[8,2,4096]{2,1,0:T(2,128)(2,1)S(1)}, bf16[8,2,4096]{2,1,0:T(2,128)(2,1)}, u32[]{:S(2)}) copy-start(bf16[8,2,4096]{2,1,0:T(2,128)(2,1)} %param.18) | copy-start | bytes 393220
  10.0 12.2 %collective-permute-start.5 = (bf16[4,2,16,128]{3,2,1,0:T(8,128)(2,1)S(1)}, bf16[4,2,16,128]{3,2,1,0:T(8,128)(2,1)S(1)}, u32[]{:S(2)}, u32[]{:S(2)}) collective-permute-start(bf16[4,2,16,128]{3,2,1,0:T(8,128)(2,1)S(1)} %pad_maximum_fusion.2), channel_id=1, source_target_pairs={{0,12},{1,13},{2,14},{3,15},{4,8},{5,9},{6,10},{7,11},{8,4},{9,5},... | collective-permute-start | bytes 98312 | tf_op jit(solution)/shard_map/ppermute | solution.py:237
  13.7 8.5 %collective-permute-start.4 = (bf16[4,2,16,128]{3,2,1,0:T(8,128)(2,1)S(1)}, bf16[4,2,16,128]{3,2,1,0:T(8,128)(2,1)S(1)}, u32[]{:S(2)}, u32[]{:S(2)}) collective-permute-start(bf16[4,2,16,128]{3,2,1,0:T(8,128)(2,1)S(1)} %pad_maximum_fusion.1), channel_id=1, source_target_pairs={{0,8},{1,9},{2,10},{3,11},{4,12},{5,13},{6,14},{7,15},{8,0},{9,1},... | collective-permute-start | bytes 98312 | tf_op jit(solution)/shard_map/ppermute | solution.py:237
  13.7 0.9 %copy-start.3 = (bf16[8,2,2,256]{3,2,1,0:T(2,128)(2,1)S(1)}, bf16[8,2,2,256]{3,2,1,0:T(2,128)(2,1)}, u32[]{:S(2)}) copy-start(bf16[8,2,2,256]{3,2,1,0:T(2,128)(2,1)} %param.19) | copy-start | bytes 49156
  13.7 0.9 %copy-start.5 = (bf16[8,64,2,2]{1,3,2,0:T(2,128)(2,1)S(1)}, bf16[8,64,2,2]{1,3,2,0:T(2,128)(2,1)}, u32[]{:S(2)}) copy-start(bf16[8,64,2,2]{1,3,2,0:T(2,128)(2,1)} %param.16) | copy-start | bytes 12292
  13.7 8.5 %collective-permute-start.3 = (bf16[4,2,16,128]{3,2,1,0:T(8,128)(2,1)S(1)}, bf16[4,2,16,128]{3,2,1,0:T(8,128)(2,1)S(1)}, u32[]{:S(2)}, u32[]{:S(2)}) collective-permute-start(bf16[4,2,16,128]{3,2,1,0:T(8,128)(2,1)S(1)} %pad_maximum_fusion), channel_id=1, source_target_pairs={{0,4},{1,5},{2,6},{3,7},{4,0},{5,1},{6,2},{7,3},{8,12},{9,13},{10,... | collective-permute-start | bytes 98312 | tf_op jit(solution)/shard_map/ppermute | solution.py:237
  14.6 0.7 %copy-start.8 = (s32[8]{0:T(128)S(1)}, s32[8]{0:T(128)}, u32[]{:S(2)}) copy-start(s32[8]{0:T(128)} %len_ref.3) | copy-start | bytes 100
  15.2 1.0 %copy-start = (bf16[8,64,2,256]{3,2,1,0:T(2,128)(2,1)S(1)}, bf16[8,64,2,256]{3,2,1,0:T(2,128)(2,1)}, u32[]{:S(2)}) copy-start(bf16[8,64,2,256]{3,2,1,0:T(2,128)(2,1)} %param.15) | copy-start | bytes 1572868
  19.2 3.0 %copy-start.2 = (bf16[6,2,4096]{2,1,0:T(2,128)(2,1)S(1)}, bf16[6,2,4096]{2,1,0:T(2,128)(2,1)}, u32[]{:S(2)}) copy-start(bf16[6,2,4096]{2,1,0:T(2,128)(2,1)} %param.20) | copy-start | bytes 294916
  19.2 3.0 %copy-start.7 = (bf16[6,2,2,256]{3,2,1,0:T(2,128)(2,1)S(1)}, bf16[6,2,2,256]{3,2,1,0:T(2,128)(2,1)}, u32[]{:S(2)}) copy-start(bf16[6,2,2,256]{3,2,1,0:T(2,128)(2,1)} %param.21) | copy-start | bytes 36868

commit v4 on v1

v4 whole, which is shorter than its diff:
```python
import functools
import math

import jax
import jax.numpy as jnp
from jax import lax
from jax.experimental import pallas as pl
from jax.experimental.pallas import tpu as pltpu
from jax.sharding import PartitionSpec as P

KVH = 4
HD = 128
HQ = 64
GROUP = HQ // KVH
STEPS = 2

NEGATIVE = -1e30
EMPTY = 1024.0
SCORE_SCALE = 1.0 / math.sqrt(HD)

BF16 = jnp.bfloat16
F32 = jnp.float32


def iota(shape, axis):
    return lax.broadcasted_iota(jnp.int32, shape, axis)


def over(x, n):
    return jnp.right_shift(x, n.bit_length() - 1) if n & (n - 1) == 0 else x // n


def mod(x, n):
    return jnp.bitwise_and(x, n - 1) if n & (n - 1) == 0 else x % n


def dot_nt(a, b):
    return lax.dot_general(a, b, (((1,), (1,)), ((), ())), preferred_element_type=F32)


def dot_nn(a, b):
    return lax.dot_general(a, b, (((1,), (0,)), ((), ())), preferred_element_type=F32)


def top_of(*parts):
    return functools.reduce(jnp.maximum, [jnp.max(p, axis=1, keepdims=True) for p in parts])


def sum_of(*parts):
    return functools.reduce(jnp.add, [jnp.sum(p, axis=1, keepdims=True) for p in parts])


def to_values(weights):
    width = weights.shape[1]
    if width % HD:
        zero = jnp.zeros((weights.shape[0], 1), F32)
        return jnp.concatenate([zero, weights[:, : width - 1]], axis=1).astype(BF16)
    tiles = [pltpu.roll(weights[:, c : c + HD], 1, 1) for c in range(0, width, HD)]
    return jnp.concatenate(tiles, axis=1).astype(BF16)


def pack_kernel(
    tp, block_rows, dest_hbm, blocks_hbm, codes_hbm, scales_hbm, send_ref,
    dest_ref, blocks_ref, codes_ref, scales_ref, sems,
):
    pairs = [
        (codes_hbm, codes_ref), (scales_hbm, scales_ref),
        (dest_hbm, dest_ref), (blocks_hbm, blocks_ref),
    ]
    copies = [pltpu.make_async_copy(a, b, sems.at[i]) for i, (a, b) in enumerate(pairs)]
    for copy in copies:
        copy.start()
    requests, tokens, heads = codes_ref.shape[:3]
    rows = 2 * tokens
    per_core = heads // tp
    last = send_ref.shape[0] - 1
    send_ref[...] = jnp.full(send_ref.shape, EMPTY, BF16)
    row_block = over(iota((rows, HD), 0), block_rows)
    for copy in copies:
        copy.wait()

    def place(r):
        there = last - dest_ref[r] * tp
        held = row_block < blocks_ref[r]
        scales = scales_ref[r].astype(F32)
        for j in range(heads):
            codes = codes_ref[r, :, j].astype(F32).reshape(rows, HD)
            values = codes * scales[:, j : j + 1]
            values = jnp.where(held, values, EMPTY).astype(BF16)
            send_ref[there - j // per_core, j % per_core] = values

    if requests <= 8:
        for r in range(requests):
            place(r)
    else:
        lax.fori_loop(0, requests, lambda r, c: (place(r), c)[1], 0)


def resident_kernel(len_ref, codes_ref, scales_ref, query_ref, new_ref, out_ref):
    slots, rows = codes_ref.shape[:2]
    heads = scales_ref.shape[2]
    tokens = rows // (2 * heads)
    queries = query_ref.shape[1]
    new_rows = new_ref.shape[1]

    row = iota((rows, HD), 0)
    source = (mod(row, 2) * heads + mod(over(row, 2), heads)) * tokens + over(row, 2 * heads)
    lane = iota((rows, HD), 1)
    spread = jnp.concatenate(
        [jnp.where(source == lane + c, 1.0, 0.0).astype(BF16) for c in range(0, rows, HD)],
        axis=1,
    )
    flat = jnp.concatenate(
        [scales_ref[:, p, h] for p in range(2) for h in range(heads)], axis=1
    )
    columns = dot_nt(spread, flat).astype(BF16)

    col = iota((queries, rows), 1)
    row_head = over(iota((queries, rows), 0), queries // heads)
    is_key = (mod(col, 2) == 0) & (mod(over(col, 2), heads) == row_head)
    col_token = jnp.where(is_key, over(col, 2 * heads), tokens)

    new_col = iota((queries, new_rows), 1)
    new_row = iota((queries, new_rows), 0)
    new_ok = (
        (mod(new_col, 2) == 0)
        & (mod(over(new_col, 2), heads) == over(new_row, queries // heads))
        & (over(new_col, 2 * heads) <= mod(new_row, STEPS))
    )

    every = range(slots)
    caches = [codes_ref[s] * columns[:, s : s + 1] for s in every]
    scores = [dot_nt(query_ref[s], caches[s]) for s in every]
    new_scores = [dot_nt(query_ref[s], new_ref[s]) for s in every]
    scores = [jnp.where(col_token < len_ref[s], scores[s] * SCORE_SCALE, NEGATIVE) for s in every]
    new_scores = [jnp.where(new_ok, new_scores[s] * SCORE_SCALE, NEGATIVE) for s in every]
    top = [top_of(scores[s], new_scores[s]) for s in every]
    weights = [jnp.exp(scores[s] - top[s]) for s in every]
    new_weights = [jnp.exp(new_scores[s] - top[s]) for s in every]
    total = [sum_of(weights[s], new_weights[s]) for s in every]
    mixed = [
        dot_nn(to_values(weights[s]), caches[s]) + dot_nn(to_values(new_weights[s]), new_ref[s])
        for s in every
    ]
    for s in every:
        out_ref[s] = (mixed[s] / total[s]).astype(BF16)


def arrival_kernel(tp, got_ref, query_ref, new_ref, out_ref):
    chunks, heads, chunk_rows = got_ref.shape[:3]
    slots, _, per_head = query_ref.shape[:3]
    rows = slots * per_head
    columns = chunks * chunk_rows
    sender_rows = tp * chunk_rows
    piece = min(columns, 256)

    caches = [got_ref[:, h].reshape(columns, HD) for h in range(heads)]
    queries = [query_ref[:, h].reshape(rows, HD) for h in range(heads)]
    new = new_ref[...].reshape(slots * new_ref.shape[1], HD)
    sums = dot_nt(jnp.ones((8, HD), BF16), caches[0])
    scores = [dot_nt(queries[h], caches[h]) for h in range(heads)]
    new_scores = [dot_nt(queries[h], new) for h in range(heads)]

    col = iota((8, columns), 1)
    held = sums < EMPTY
    first = jnp.where(held & (mod(col, sender_rows) == 0), 1.0, 0.0).astype(BF16)
    before = jnp.where(
        over(iota((piece, piece), 0), sender_rows) > over(iota((piece, piece), 1), sender_rows),
        1.0,
        0.0,
    ).astype(BF16)
    base = jnp.zeros((8, 1), F32)
    ranks = []
    for p in reversed(range(0, columns, piece)):
        part = first[:, p : p + piece]
        ranks.insert(0, dot_nn(part, before) + base)
        if p:
            base = base + jnp.sum(part.astype(F32), axis=1, keepdims=True)
    rank = ranks[0] if len(ranks) == 1 else jnp.concatenate(ranks, axis=1)
    slot_of = jnp.where(held & (mod(col, 2) == 0), rank, -1.0)[:1]
    first_slot = (pl.program_id(0) * slots).astype(F32)
    mine = [slot_of == first_slot + a for a in range(slots)]

    new_col = iota((rows, new.shape[0]), 1)
    new_row = iota((rows, new.shape[0]), 0)
    new_here = (
        (mod(new_col, 2) == 0)
        & (over(new_col, 2 * heads * STEPS) == over(new_row, per_head))
        & (mod(over(new_col, 2 * heads), STEPS) <= mod(new_row, STEPS))
    )
    new_head = jnp.where(new_here, mod(over(new_col, 2), heads), heads)

    every = range(heads)
    scores = [
        jnp.concatenate(
            [
                jnp.where(mine[a], scores[h][a * per_head : (a + 1) * per_head] * SCORE_SCALE, NEGATIVE)
                for a in range(slots)
            ],
            axis=0,
        )
        for h in every
    ]
    new_scores = [jnp.where(new_head == h, new_scores[h] * SCORE_SCALE, NEGATIVE) for h in every]
    top = [top_of(scores[h], new_scores[h]) for h in every]
    weights = [jnp.exp(scores[h] - top[h]) for h in every]
    new_weights = [jnp.exp(new_scores[h] - top[h]) for h in every]
    total = [sum_of(weights[h], new_weights[h]) for h in every]
    mixed = [
        dot_nn(to_values(weights[h]), caches[h]) + dot_nn(to_values(new_weights[h]), new)
        for h in every
    ]
    for h in every:
        out_ref[:, h] = (mixed[h] / total[h]).astype(BF16).reshape(slots, per_head, HD)


def whole(memory_space=pltpu.VMEM):
    return pl.BlockSpec(memory_space=memory_space)


def in_hbm(x):
    return pltpu.with_memory_space_constraint(x, pltpu.HBM)


def limit(mib):
    return pltpu.CompilerParams(vmem_limit_bytes=mib * 2**20)


def pack(pre_codes, pre_scales, req_dest, req_blocks, peers, tp):
    requests, blocks, block_tokens = pre_codes.shape[:3]
    tokens = blocks * block_tokens
    codes = pre_codes.reshape(requests, tokens, 2, KVH, HD).transpose(0, 1, 3, 2, 4)
    scales = pre_scales.reshape(requests, tokens * 2, KVH)
    return pl.pallas_call(
        functools.partial(pack_kernel, tp, 2 * block_tokens),
        out_shape=pltpu.VMEM((peers * tp, KVH // tp, tokens * 2, HD), BF16),
        in_specs=[whole(pltpu.HBM)] * 4,
        out_specs=whole(),
        scratch_shapes=[
            pltpu.SMEM(req_dest.shape, jnp.int32),
            pltpu.SMEM(req_blocks.shape, jnp.int32),
            pltpu.VMEM(codes.shape, BF16),
            pltpu.VMEM(scales.shape, BF16),
            pltpu.SemaphoreType.DMA((4,)),
        ],
        compiler_params=limit(16),
        name="pack",
    )(*[in_hbm(x) for x in (req_dest, req_blocks, codes, scales)])


def query_rows(query):
    slots, steps, width = query.shape
    return query.reshape(slots, steps, width // HD, HD).transpose(0, 2, 1, 3)


def new_rows_of(new):
    slots, steps, pair, width = new.shape
    heads = width // HD
    return (
        new.reshape(slots, steps, pair, heads, HD)
        .transpose(0, 1, 3, 2, 4)
        .reshape(slots, steps * heads * pair, HD)
    )


def from_rows(out, shape):
    slots, steps, width = shape
    return out.reshape(slots, width // HD, steps, HD).transpose(0, 2, 1, 3).reshape(shape)


def resident(res_codes, res_scales, res_len, res_query, res_new):
    slots, tokens, _, width = res_codes.shape
    heads = width // HD
    codes = (
        res_codes.reshape(slots, tokens, 2, heads, HD)
        .transpose(0, 1, 3, 2, 4)
        .reshape(slots, tokens * heads * 2, HD)
    )
    scales = res_scales.transpose(0, 2, 3, 1)
    query = query_rows(res_query).reshape(slots, heads * GROUP * STEPS, HD)
    work = slots * heads * GROUP * STEPS * tokens * heads * 2
    out = pl.pallas_call(
        resident_kernel,
        out_shape=jax.ShapeDtypeStruct(query.shape, BF16),
        in_specs=[whole(pltpu.SMEM)] + [whole()] * 4,
        out_specs=whole(),
        cost_estimate=pl.CostEstimate(
            flops=4 * work * HD,
            bytes_accessed=2 * (codes.size + 2 * query.size),
            transcendentals=work,
        ),
        compiler_params=limit(16),
        name="resident",
    )(in_hbm(res_len), codes, scales, query, new_rows_of(res_new))
    return from_rows(out, res_query.shape)


def arrivals(got, arr_query, arr_new, tp):
    slots, steps, width = arr_query.shape
    heads = width // (HD * GROUP)
    query = query_rows(arr_query).reshape(slots, heads, GROUP * steps, HD)
    new = new_rows_of(arr_new)
    size = max(n for n in range(1, 7) if slots % n == 0)
    small = got.size <= 2**18
    out = pl.pallas_call(
        functools.partial(arrival_kernel, tp),
        out_shape=jax.ShapeDtypeStruct(query.shape, BF16),
        grid=(slots // size,),
        in_specs=[
            pl.BlockSpec(got.shape, lambda i: (0, 0, 0, 0)),
            pl.BlockSpec((size,) + query.shape[1:], lambda i: (i, 0, 0, 0)),
            pl.BlockSpec((size,) + new.shape[1:], lambda i: (i, 0, 0)),
        ],
        out_specs=pl.BlockSpec((size,) + query.shape[1:], lambda i: (i, 0, 0, 0)),
        compiler_params=limit(16 if small else 48),
        name="arrivals",
    )(got, query, new)
    return from_rows(out, arr_query.shape)


def shards(
    pre_codes,
    pre_scales,
    req_dest,
    req_blocks,
    res_codes,
    res_scales,
    res_len,
    res_query,
    res_new,
    arr_query,
    arr_new,
):
    peers = lax.axis_size("wide")
    tp = lax.axis_size("tp")
    send = pack(pre_codes, pre_scales, req_dest, req_blocks, peers, tp)
    got = lax.all_to_all(
        send,
        ("wide", "tp"),
        split_axis=0,
        concat_axis=0,
        tiled=True,
        axis_index_groups=[list(reversed(range(peers * tp)))],
    )
    res_out = resident(res_codes, res_scales, res_len, res_query, res_new)
    arr_out = arrivals(got, arr_query, arr_new, tp)
    return (res_out, arr_out)


def solution(mesh):
    in_specs = (
        P(("groups", "wide"), None, "tp", None, None),
        P(("groups", "wide"), None, "tp", None, None),
        P(("groups", "wide")),
        P(("groups", "wide")),
        P(("groups", "wide"), None, None, "tp"),
        P(("groups", "wide"), None, None, "tp"),
        P(("groups", "wide")),
        P(("groups", "wide"), None, "tp"),
        P(("groups", "wide"), None, None, "tp"),
        P(("groups", "wide"), None, "tp"),
        P(("groups", "wide"), None, None, "tp"),
    )
    out_specs = (P(("groups", "wide"), None, "tp"), P(("groups", "wide"), None, "tp"))
    return jax.shard_map(shards, mesh=mesh, in_specs=in_specs, out_specs=out_specs, check_vma=False)
```

time: 19.6 us -> 17.3 us (0.88)
  waiting for transfers between devices: 2.9 us -> 0.13 us
  Pallas kernels: 8.35 us -> 6.06 us
  starting transfers between devices: 7.36 us -> 8.98 us
  local copies, waits for them, and re-layouts: 0.01 us -> 1.06 us
    all_to_all x1, waiting for transfers between devices: 2.9 us -> 0.13 us  [shards(): lax.all_to_all(send, ('wide', 'tp'), split_axis=0, concat_axis=0, tiled=T...]
    pallas_call x1, Pallas kernels: 5.02 us -> 2.99 us  [resident(): pl.pallas_call(resident_kernel, out_shape=jax.ShapeDtypeStruct(query.shap...]
    all_to_all x1, starting transfers between devices: 7.36 us -> 8.98 us  [shards(): lax.all_to_all(send, ('wide', 'tp'), split_axis=0, concat_axis=0, tiled=T...]
    unnamed x4 -> x12, local copies, waits for them, and re-layouts: 0.01 us -> 1.06 us
    pallas_call x1, Pallas kernels: 1.68 us -> 1.39 us  [arrivals(): pl.pallas_call(functools.partial(arrival_kernel, tp), out_shape=jax.Shape...]
  transfers between devices with their start and end apart: 1 -> 1, of which waited for: 1 -> 1; matrix products, arithmetic and copies ran while one was open for 0% -> 0% of each run, Pallas kernels for 26% -> 18%
where the time goes in v4:
time: 17.3 us; the launch traced here: 16.9 us
  starting transfers between devices  8.98 us (52%)
  Pallas kernels  6.06 us (35%)
  local copies, waits for them, and re-layouts  1.06 us (6%)
  between operations  0.69 us (4%)
    all_to_all x1, starting transfers between devices, shards(): lax.all_to_all(send, ('wide', 'tp'), split_axis=0, concat_axis=0, tiled=T...  8.98 us
    pallas_call x1, Pallas kernels, resident(): pl.pallas_call(resident_kernel, out_shape=jax.ShapeDtypeStruct(query.shap...  2.99 us
    pallas_call x1, Pallas kernels, pack(): pl.pallas_call(functools.partial(pack_kernel, tp, 2 * block_tokens), out_...  1.69 us
    pallas_call x1, Pallas kernels, arrivals(): pl.pallas_call(functools.partial(arrival_kernel, tp), out_shape=jax.Shape...  1.39 us
    unnamed x12, local copies, waits for them, and re-layouts  1.06 us
  transfers between devices with their start and end apart: 1, of which 1 were waited for; matrix products, arithmetic and copies ran while one was open for 0% of the time, Pallas kernels for 18%

profile of v4, /device:TPU:0, one launch (start us, length us, event | category | flops | bytes accessed | tf_op | source)
XLA Modules:
  0.0 16.9 jit_solution(3935553587350543021)
XLA Ops:
  0.6 1.7 %pack.1 = bf16[16,2,16,128]{3,2,1,0:T(8,128)(2,1)} custom-call(s32[4]{0:T(128)} %dest_hbm.1, s32[4]{0:T(128)} %blocks_hbm.1, bf16[4,8,4,2,128]{4,3,2,1,0:T(2,128)(2,1)} %bitcast.48, bf16[4,16,4]{2,1,0:T(8,128)(2,1)} %bitcast.49), custom_call_target="tpu_custom_call" | custom-call | tf_op jit(solution)/shard_map/pack/pallas_call | solution.py:234
  2.3 0.0 copy-start.1
  2.3 0.0 copy-start.3
  2.3 0.0 copy-start.5
  2.4 9.0 %all-to-all-start = ((bf16[16,2,16,128]{3,2,1,0:T(8,128)(2,1)}), bf16[16,2,16,128]{3,2,1,0:T(8,128)(2,1)S(1)}, u32[]{:S(2)}, u32[]{:S(2)}) async-start(bf16[16,2,16,128]{3,2,1,0:T(8,128)(2,1)} %pack.1), calls=%async_computation | async-start | bytes 262144 | tf_op jit(solution)/shard_map/all_to_all | solution.py:337
  11.3 0.0 copy-done.1
  11.3 0.0 copy-done.3
  11.4 0.0 copy-done.5
  11.4 0.0 copy-start
  11.4 1.0 %copy-done = bf16[8,64,2,256]{3,2,1,0:T(2,128)(2,1)S(1)} copy-done((bf16[8,64,2,256]{3,2,1,0:T(2,128)(2,1)S(1)}, bf16[8,64,2,256]{3,2,1,0:T(2,128)(2,1)}, u32[]{:S(2)}) %copy-start) | copy-done | bytes 524312
  12.4 0.0 copy-start.2
  12.4 0.0 copy-start.4
  12.4 3.0 %resident.1 = bf16[8,64,128]{2,1,0:T(8,128)(2,1)} custom-call(s32[8]{0:T(128)} %len_ref.1, bf16[8,256,128]{2,1,0:T(8,128)(2,1)S(1)} %bitcast.40, bf16[8,2,2,64]{3,2,1,0:T(2,128)(2,1)S(1)} %bitcast.45, bf16[8,64,128]{2,1,0:T(8,128)(2,1)S(1)} %bitcast.41, bf16[8,8,128]{2,1,0:T(8,128)(2,1)S(1)} %bitcast.43), custom_call_target="tpu_custom_call" | custom-call | flops 67108864 | bytes 786432 | tf_op jit(solution)/shard_map/resident/pallas_call | solution.py:282
  15.4 0.1 all-to-all-done.got_ref
  15.5 0.0 copy-done.2
  15.5 0.0 copy-done.4
  15.5 1.4 %arrivals.1 = bf16[6,2,32,128]{3,2,1,0:T(8,128)(2,1)} custom-call(bf16[16,2,16,128]{3,2,1,0:T(8,128)(2,1)S(1)} %all-to-all-done.got_ref, bf16[6,2,32,128]{3,2,1,0:T(8,128)(2,1)S(1)} %bitcast.42, bf16[6,8,128]{2,1,0:T(8,128)(2,1)S(1)} %bitcast.44), custom_call_target="tpu_custom_call" | custom-call | tf_op jit(solution)/shard_map/arrivals/pallas_call | solution.py:305
Async XLA Ops:
  2.3 9.0 %copy-start.1 = (bf16[8,2,4096]{2,1,0:T(2,128)(2,1)S(1)}, bf16[8,2,4096]{2,1,0:T(2,128)(2,1)}, u32[]{:S(2)}) copy-start(bf16[8,2,4096]{2,1,0:T(2,128)(2,1)} %param.18) | copy-start | bytes 393220
  2.3 9.0 %copy-start.3 = (bf16[8,2,2,256]{3,2,1,0:T(2,128)(2,1)S(1)}, bf16[8,2,2,256]{3,2,1,0:T(2,128)(2,1)}, u32[]{:S(2)}) copy-start(bf16[8,2,2,256]{3,2,1,0:T(2,128)(2,1)} %param.19) | copy-start | bytes 49156
  2.3 9.0 %copy-start.5 = (bf16[8,64,2,2]{1,3,2,0:T(2,128)(2,1)S(1)}, bf16[8,64,2,2]{1,3,2,0:T(2,128)(2,1)}, u32[]{:S(2)}) copy-start(bf16[8,64,2,2]{1,3,2,0:T(2,128)(2,1)} %param.16) | copy-start | bytes 12292
  2.4 13.2 %all-to-all-start = ((bf16[16,2,16,128]{3,2,1,0:T(8,128)(2,1)}), bf16[16,2,16,128]{3,2,1,0:T(8,128)(2,1)S(1)}, u32[]{:S(2)}, u32[]{:S(2)}) async-start(bf16[16,2,16,128]{3,2,1,0:T(8,128)(2,1)} %pack.1), calls=%async_computation | async-start | bytes 262144 | tf_op jit(solution)/shard_map/all_to_all | solution.py:337
  11.4 1.0 %copy-start = (bf16[8,64,2,256]{3,2,1,0:T(2,128)(2,1)S(1)}, bf16[8,64,2,256]{3,2,1,0:T(2,128)(2,1)}, u32[]{:S(2)}) copy-start(bf16[8,64,2,256]{3,2,1,0:T(2,128)(2,1)} %param.15) | copy-start | bytes 1572868
  12.4 3.1 %copy-start.2 = (bf16[6,2,4096]{2,1,0:T(2,128)(2,1)S(1)}, bf16[6,2,4096]{2,1,0:T(2,128)(2,1)}, u32[]{:S(2)}) copy-start(bf16[6,2,4096]{2,1,0:T(2,128)(2,1)} %param.20) | copy-start | bytes 294916
  12.4 3.1 %copy-start.4 = (bf16[6,2,2,256]{3,2,1,0:T(2,128)(2,1)S(1)}, bf16[6,2,2,256]{3,2,1,0:T(2,128)(2,1)}, u32[]{:S(2)}) copy-start(bf16[6,2,2,256]{3,2,1,0:T(2,128)(2,1)} %param.21) | copy-start | bytes 36868

commit v5 on v4

v5 whole, which is shorter than its diff:
```python
import functools
import math

import jax
import jax.numpy as jnp
from jax import lax
from jax.experimental import pallas as pl
from jax.experimental.pallas import tpu as pltpu
from jax.sharding import PartitionSpec as P

KVH = 4
HD = 128
HQ = 64
GROUP = HQ // KVH
STEPS = 2

NEGATIVE = -1e30
EMPTY = 1024.0
SCORE_SCALE = 1.0 / math.sqrt(HD)

BF16 = jnp.bfloat16
F32 = jnp.float32


def iota(shape, axis):
    return lax.broadcasted_iota(jnp.int32, shape, axis)


def over(x, n):
    return jnp.right_shift(x, n.bit_length() - 1) if n & (n - 1) == 0 else x // n


def mod(x, n):
    return jnp.bitwise_and(x, n - 1) if n & (n - 1) == 0 else x % n


def dot_nt(a, b):
    return lax.dot_general(a, b, (((1,), (1,)), ((), ())), preferred_element_type=F32)


def dot_nn(a, b):
    return lax.dot_general(a, b, (((1,), (0,)), ((), ())), preferred_element_type=F32)


def top_of(*parts):
    return functools.reduce(jnp.maximum, [jnp.max(p, axis=1, keepdims=True) for p in parts])


def sum_of(*parts):
    return functools.reduce(jnp.add, [jnp.sum(p, axis=1, keepdims=True) for p in parts])


def to_values(weights):
    tiles = [pltpu.roll(weights[:, c : c + HD], 1, 1) for c in range(0, weights.shape[1], HD)]
    return jnp.concatenate(tiles, axis=1).astype(BF16)


def values_up(rows):
    return pltpu.roll(rows.astype(F32), rows.shape[0] - 1, 0).astype(BF16)


def pack_kernel(
    tp, heads, block_rows, dest_hbm, blocks_hbm, codes_hbm, scales_hbm, cache_hbm,
    send_ref, cache_ref, dest_ref, blocks_ref, codes_ref, scales_ref, sems,
):
    pairs = [
        (codes_hbm, codes_ref), (scales_hbm, scales_ref),
        (dest_hbm, dest_ref), (blocks_hbm, blocks_ref), (cache_hbm, cache_ref),
    ]
    copies = [pltpu.make_async_copy(a, b, sems.at[i]) for i, (a, b) in enumerate(pairs)]
    for copy in copies:
        copy.start()
    requests, all_rows = codes_ref.shape[:2]
    rows = all_rows // heads
    per_core = heads // tp
    last = send_ref.shape[0] - 1
    send_ref[...] = jnp.full(send_ref.shape, EMPTY, BF16)
    row_block = over(iota((rows, HD), 0), block_rows)
    to_row = iota((all_rows, all_rows), 0)
    from_row = iota((all_rows, all_rows), 1)
    source = over(mod(to_row, rows), 2) * (2 * heads) + over(to_row, rows) * 2 + mod(to_row, 2)
    by_head = jnp.where(from_row == source, 1.0, 0.0).astype(BF16)
    for copy in copies[:-1]:
        copy.wait()

    def place(r):
        there = last - dest_ref[r] * tp
        held = row_block < blocks_ref[r]
        codes = dot_nn(by_head, codes_ref[r])
        scales = scales_ref[r].astype(F32)
        for j in range(heads):
            values = codes[j * rows : (j + 1) * rows] * scales[:, j : j + 1]
            values = jnp.where(held, values, EMPTY).astype(BF16)
            send_ref[there - j // per_core, j % per_core] = values

    if requests <= 8:
        for r in range(requests):
            place(r)
    else:
        lax.fori_loop(0, requests, lambda r, c: (place(r), c)[1], 0)
    copies[-1].wait()


def resident_kernel(len_ref, codes_ref, scales_ref, query_ref, new_ref, out_ref):
    slots, rows = codes_ref.shape[:2]
    heads = scales_ref.shape[2]
    tokens = rows // (2 * heads)
    queries = query_ref.shape[1]
    new_rows = new_ref.shape[0]

    row = iota((rows, HD), 0)
    source = (mod(row, 2) * heads + mod(over(row, 2), heads)) * tokens + over(row, 2 * heads)
    lane = iota((rows, HD), 1)
    spread = jnp.concatenate(
        [jnp.where(source == lane + c, 1.0, 0.0).astype(BF16) for c in range(0, rows, HD)],
        axis=1,
    )
    flat = jnp.concatenate(
        [scales_ref[:, p, h] for p in range(2) for h in range(heads)], axis=1
    )
    columns = dot_nt(spread, flat).astype(BF16)

    col = iota((queries, rows), 1)
    row_head = over(iota((queries, rows), 0), queries // heads)
    is_key = (mod(col, 2) == 0) & (mod(over(col, 2), heads) == row_head)
    col_token = jnp.where(is_key, over(col, 2 * heads), tokens)

    new_col = iota((queries, new_rows), 1)
    new_row = iota((queries, new_rows), 0)
    new_ok = (
        (mod(new_col, 2) == 0)
        & (mod(over(new_col, 2), heads) == over(new_row, queries // heads))
        & (mod(over(new_col, 2 * heads), STEPS) <= mod(new_row, STEPS))
    )
    new_slot = jnp.where(new_ok, over(new_col, 2 * heads * STEPS), slots)

    every = range(slots)
    new = new_ref[...]
    new_all = dot_nt(query_ref[...].reshape(slots * queries, HD), new)
    caches = [codes_ref[s] * columns[:, s : s + 1] for s in every]
    scores = [dot_nt(query_ref[s], caches[s]) for s in every]
    scores = [jnp.where(col_token < len_ref[s], scores[s] * SCORE_SCALE, NEGATIVE) for s in every]
    new_scores = [
        jnp.where(new_slot == s, new_all[s * queries : (s + 1) * queries] * SCORE_SCALE, NEGATIVE)
        for s in every
    ]
    top = [top_of(scores[s], new_scores[s]) for s in every]
    weights = [jnp.exp(scores[s] - top[s]) for s in every]
    new_weights = [jnp.exp(new_scores[s] - top[s]) for s in every]
    total = [sum_of(weights[s], new_weights[s]) for s in every]
    new_mixed = dot_nn(jnp.concatenate(new_weights, axis=0).astype(BF16), values_up(new))
    mixed = [
        dot_nn(to_values(weights[s]), caches[s]) + new_mixed[s * queries : (s + 1) * queries]
        for s in every
    ]
    for s in every:
        out_ref[s] = (mixed[s] * (1.0 / total[s])).astype(BF16)


def arrival_kernel(
    tp, got_ref, query_ref, new_ref, done_ref, out_hbm, done_hbm, out_ref, sems
):
    step = pl.program_id(0)
    hand_on = pltpu.make_async_copy(done_ref, done_hbm, sems.at[0])
    pl.when(step == 0)(hand_on.start)

    chunks, heads, chunk_rows = got_ref.shape[:3]
    slots, _, per_head = query_ref.shape[:3]
    rows = slots * per_head
    columns = chunks * chunk_rows
    sender_rows = tp * chunk_rows
    piece = min(columns, 256)
    every = range(heads)

    caches = [got_ref[:, h].reshape(columns, HD) for h in every]
    queries = [query_ref[:, h].reshape(rows, HD) for h in every]
    new = new_ref[...]
    ones = jnp.ones((16, HD), BF16)
    scores = [dot_nt(jnp.concatenate([ones, queries[0]], axis=0), caches[0])]
    sums, scores[0] = scores[0][:8], scores[0][16:]
    scores += [dot_nt(queries[h], caches[h]) for h in every[1:]]
    new_all = dot_nt(jnp.concatenate(queries, axis=0), new)

    col = iota((8, columns), 1)
    held = sums < EMPTY
    first = jnp.where(held & (mod(col, sender_rows) == 0), 1.0, 0.0).astype(BF16)
    before = jnp.where(
        over(iota((piece, piece), 0), sender_rows) > over(iota((piece, piece), 1), sender_rows),
        1.0,
        0.0,
    ).astype(BF16)
    base = jnp.zeros((8, 1), F32)
    ranks = []
    for p in reversed(range(0, columns, piece)):
        part = first[:, p : p + piece]
        ranks.insert(0, dot_nn(part, before) + base)
        if p:
            base = base + jnp.sum(part.astype(F32), axis=1, keepdims=True)
    rank = ranks[0] if len(ranks) == 1 else jnp.concatenate(ranks, axis=1)
    slot_of = jnp.where(held & (mod(col, 2) == 0), rank, -1.0)[:1]
    first_slot = (step * slots).astype(F32)
    mine = [slot_of == first_slot + a for a in range(slots)]

    new_col = iota((rows, new.shape[0]), 1)
    new_row = iota((rows, new.shape[0]), 0)
    new_here = (
        (mod(new_col, 2) == 0)
        & (over(new_col, 2 * heads * STEPS) == over(new_row, per_head))
        & (mod(over(new_col, 2 * heads), STEPS) <= mod(new_row, STEPS))
    )
    new_head = jnp.where(new_here, mod(over(new_col, 2), heads), heads)

    scores = [
        jnp.concatenate(
            [
                jnp.where(mine[a], scores[h][a * per_head : (a + 1) * per_head] * SCORE_SCALE, NEGATIVE)
                for a in range(slots)
            ],
            axis=0,
        )
        for h in every
    ]
    new_scores = [
        jnp.where(new_head == h, new_all[h * rows : (h + 1) * rows] * SCORE_SCALE, NEGATIVE)
        for h in every
    ]
    top = [top_of(scores[h], new_scores[h]) for h in every]
    weights = [jnp.exp(scores[h] - top[h]) for h in every]
    new_weights = [jnp.exp(new_scores[h] - top[h]) for h in every]
    total = [sum_of(weights[h], new_weights[h]) for h in every]
    new_mixed = dot_nn(jnp.concatenate(new_weights, axis=0).astype(BF16), values_up(new))
    copies = []
    for h in every:
        mixed = dot_nn(to_values(weights[h]), caches[h]) + new_mixed[h * rows : (h + 1) * rows]
        out_ref[h] = (mixed * (1.0 / total[h])).astype(BF16).reshape(slots, per_head, HD)
        there = out_hbm.at[pl.ds(step * slots, slots), h]
        copies.append(pltpu.make_async_copy(out_ref.at[h], there, sems.at[1 + h]))
        copies[-1].start()
    for copy in copies:
        copy.wait()
    pl.when(step == pl.num_programs(0) - 1)(hand_on.wait)


def whole(memory_space=pltpu.VMEM):
    return pl.BlockSpec(memory_space=memory_space)


def in_hbm(x):
    return pltpu.with_memory_space_constraint(x, pltpu.HBM)


def limit(mib):
    return pltpu.CompilerParams(vmem_limit_bytes=mib * 2**20)


def pack(pre_codes, pre_scales, req_dest, req_blocks, cache, peers, tp):
    requests, blocks, block_tokens = pre_codes.shape[:3]
    tokens = blocks * block_tokens
    codes = (
        pre_codes.reshape(requests, tokens, 2, KVH, HD)
        .transpose(0, 1, 3, 2, 4)
        .reshape(requests, tokens * KVH * 2, HD)
    )
    scales = pre_scales.reshape(requests, tokens * 2, KVH)
    ins = [req_dest, req_blocks, codes, scales, cache]
    return pl.pallas_call(
        functools.partial(pack_kernel, tp, KVH, 2 * block_tokens),
        out_shape=[
            pltpu.VMEM((peers * tp, KVH // tp, tokens * 2, HD), BF16),
            pltpu.VMEM(cache.shape, BF16),
        ],
        in_specs=[whole(pltpu.HBM)] * len(ins),
        out_specs=[whole()] * 2,
        scratch_shapes=[
            pltpu.SMEM(req_dest.shape, jnp.int32),
            pltpu.SMEM(req_blocks.shape, jnp.int32),
            pltpu.VMEM(codes.shape, BF16),
            pltpu.VMEM(scales.shape, BF16),
            pltpu.SemaphoreType.DMA((len(ins),)),
        ],
        compiler_params=limit(16),
        name="pack",
    )(*[in_hbm(x) for x in ins])


def cache_rows(codes):
    slots, tokens, _, width = codes.shape
    heads = width // HD
    return (
        codes.reshape(slots, tokens, 2, heads, HD)
        .transpose(0, 1, 3, 2, 4)
        .reshape(slots, tokens * heads * 2, HD)
    )


def query_rows(query):
    slots, steps, width = query.shape
    return query.reshape(slots, steps, width // HD, HD).transpose(0, 2, 1, 3)


def new_rows_of(new):
    slots, steps, pair, width = new.shape
    heads = width // HD
    return (
        new.reshape(slots, steps, pair, heads, HD)
        .transpose(0, 1, 3, 2, 4)
        .reshape(slots * steps * heads * pair, HD)
    )


def from_rows(out, shape):
    slots, steps, width = shape
    return out.reshape(slots, width // HD, steps, HD).transpose(0, 2, 1, 3).reshape(shape)


def resident(codes, res_scales, res_len, res_query, res_new):
    slots, rows = codes.shape[:2]
    heads = res_scales.shape[-1]
    scales = res_scales.transpose(0, 2, 3, 1)
    query = query_rows(res_query).reshape(slots, heads * GROUP * STEPS, HD)
    work = query.shape[0] * query.shape[1] * rows
    return pl.pallas_call(
        resident_kernel,
        out_shape=pltpu.VMEM(query.shape, BF16),
        in_specs=[whole(pltpu.SMEM)] + [whole()] * 4,
        out_specs=whole(),
        cost_estimate=pl.CostEstimate(
            flops=4 * work * HD,
            bytes_accessed=2 * (codes.size + 2 * query.size),
            transcendentals=work,
        ),
        compiler_params=limit(16),
        name="resident",
    )(in_hbm(res_len), codes, scales, query, new_rows_of(res_new))


def arrivals(got, arr_query, arr_new, done, tp):
    slots, steps, width = arr_query.shape
    heads = width // (HD * GROUP)
    query = query_rows(arr_query).reshape(slots, heads, GROUP * steps, HD)
    new = new_rows_of(arr_new)
    size = max(n for n in range(1, 7) if slots % n == 0)
    small = got.size <= 2**18
    return pl.pallas_call(
        functools.partial(arrival_kernel, tp),
        out_shape=[
            jax.ShapeDtypeStruct(query.shape, BF16),
            jax.ShapeDtypeStruct(done.shape, BF16),
        ],
        grid=(slots // size,),
        in_specs=[
            pl.BlockSpec(got.shape, lambda i: (0, 0, 0, 0)),
            pl.BlockSpec((size,) + query.shape[1:], lambda i: (i, 0, 0, 0)),
            pl.BlockSpec((new.shape[0] // slots * size, HD), lambda i: (i, 0)),
            whole(),
        ],
        out_specs=[whole(pltpu.HBM)] * 2,
        scratch_shapes=[
            pltpu.VMEM((heads, size) + query.shape[2:], BF16),
            pltpu.SemaphoreType.DMA((1 + heads,)),
        ],
        compiler_params=limit(16 if small else 48),
        name="arrivals",
    )(got, query, new, done)


def shards(
    pre_codes,
    pre_scales,
    req_dest,
    req_blocks,
    res_codes,
    res_scales,
    res_len,
    res_query,
    res_new,
    arr_query,
    arr_new,
):
    peers = lax.axis_size("wide")
    tp = lax.axis_size("tp")
    send, cache = pack(
        pre_codes, pre_scales, req_dest, req_blocks, cache_rows(res_codes), peers, tp
    )
    got = lax.all_to_all(
        send,
        ("wide", "tp"),
        split_axis=0,
        concat_axis=0,
        tiled=True,
        axis_index_groups=[list(reversed(range(peers * tp)))],
    )
    done = resident(cache, res_scales, res_len, res_query, res_new)
    arr_out, res_out = arrivals(got, arr_query, arr_new, done, tp)
    return (from_rows(res_out, res_query.shape), from_rows(arr_out, arr_query.shape))


def solution(mesh):
    in_specs = (
        P(("groups", "wide"), None, "tp", None, None),
        P(("groups", "wide"), None, "tp", None, None),
        P(("groups", "wide")),
        P(("groups", "wide")),
        P(("groups", "wide"), None, None, "tp"),
        P(("groups", "wide"), None, None, "tp"),
        P(("groups", "wide")),
        P(("groups", "wide"), None, "tp"),
        P(("groups", "wide"), None, None, "tp"),
        P(("groups", "wide"), None, "tp"),
        P(("groups", "wide"), None, None, "tp"),
    )
    out_specs = (P(("groups", "wide"), None, "tp"), P(("groups", "wide"), None, "tp"))
    return jax.shard_map(shards, mesh=mesh, in_specs=in_specs, out_specs=out_specs, check_vma=False)
```

time: 17.3 us -> 17.2 us (level)
  waiting for transfers between devices: 0.13 us -> 2.14 us
  local copies, waits for them, and re-layouts: 1.06 us -> 0.03 us
  Pallas kernels: 6.06 us -> 5.12 us
    all_to_all x1, waiting for transfers between devices: 0.13 us -> 2.14 us  [shards(): lax.all_to_all(send, ('wide', 'tp'), split_axis=0, concat_axis=0, tiled=T...]
    unnamed x12 -> x10, local copies, waits for them, and re-layouts: 1.06 us -> 0.03 us
    pallas_call x3, Pallas kernels: 6.06 us -> 5.12 us  [the longest x1 2 us: resident(): pl.pallas_call(resident_kernel, out_shape=pltpu.VMEM(query.shape, BF16),...]
  transfers between devices with their start and end apart: 1 -> 1, of which waited for: 1 -> 1; matrix products, arithmetic and copies ran while one was open for 0% -> 0% of each run, Pallas kernels for 18% -> 12%
where the time goes in v5:
time: 17.2 us; the launch traced here: 17 us
  starting transfers between devices  8.98 us (52%)
  Pallas kernels  5.12 us (30%)
  waiting for transfers between devices  2.14 us (12%)
  between operations  0.71 us (4%)
    all_to_all x1, starting transfers between devices, shards(): lax.all_to_all(send, ('wide', 'tp'), split_axis=0, concat_axis=0, tiled=T...  8.98 us
    all_to_all x1, waiting for transfers between devices, shards(): lax.all_to_all(send, ('wide', 'tp'), split_axis=0, concat_axis=0, tiled=T...  2.14 us
    pallas_call x1, Pallas kernels, resident(): pl.pallas_call(resident_kernel, out_shape=pltpu.VMEM(query.shape, BF16),...  2 us
    pallas_call x1, Pallas kernels, pack(): pl.pallas_call(functools.partial(pack_kernel, tp, KVH, 2 * block_tokens),...  1.8 us
    pallas_call x1, Pallas kernels, arrivals(): pl.pallas_call(functools.partial(arrival_kernel, tp), out_shape=[jax.Shap...  1.33 us
  transfers between devices with their start and end apart: 1, of which 1 were waited for; matrix products, arithmetic and copies ran while one was open for 0% of the time, Pallas kernels for 12%

profile of v5, /device:TPU:0, one launch (start us, length us, event | category | flops | bytes accessed | tf_op | source)
XLA Modules:
  0.0 17.0 jit_solution(1162624008275914122)
XLA Ops:
  0.6 1.8 %pack.1 = (bf16[16,2,16,128]{3,2,1,0:T(8,128)(2,1)}, bf16[8,256,128]{2,1,0:T(8,128)(2,1)S(1)}) custom-call(s32[4]{0:T(128)} %dest_hbm.1, s32[4]{0:T(128)} %blocks_hbm.1, bf16[4,64,128]{2,1,0:T(8,128)(2,1)} %bitcast.48, bf16[4,16,4]{2,1,0:T(8,128)(2,1)} %bitcast.49, bf16[8,256,128]{2,1,0:T(8,128)(2,1)} %bitcast.47), custom_call_target="tpu_custom_call" | custom-call | tf_op jit(solution)/shard_map/pack/pallas_call | solution.py:266
  2.4 0.0 copy-start
  2.4 0.0 copy-start.2
  2.5 0.0 copy-start.4
  2.5 9.0 %all-to-all-start = ((bf16[16,2,16,128]{3,2,1,0:T(8,128)(2,1)}), bf16[16,2,16,128]{3,2,1,0:T(8,128)(2,1)S(1)}, u32[]{:S(2)}, u32[]{:S(2)}) async-start(bf16[16,2,16,128]{3,2,1,0:T(8,128)(2,1)} %get-tuple-element.6), calls=%async_computation | async-start | bytes 262144 | tf_op jit(solution)/shard_map/all_to_all | solution.py:385
  11.5 0.0 copy-done
  11.5 0.0 copy-done.2
  11.5 0.0 copy-done.4
  11.5 0.0 copy-start.1
  11.5 0.0 copy-start.3
  11.5 2.0 %resident.1.done_ref = bf16[8,64,128]{2,1,0:T(8,128)(2,1)S(1)} custom-call(s32[8]{0:T(128)} %len_ref.1, bf16[8,256,128]{2,1,0:T(8,128)(2,1)S(1)} %get-tuple-element.7.codes_ref, bf16[8,2,2,64]{3,2,1,0:T(2,128)(2,1)S(1)} %bitcast.46, bf16[8,64,128]{2,1,0:T(8,128)(2,1)S(1)} %bitcast.42, bf16[64,128]{1,0:T(8,128)(2,1)S(1)} %bitcast.44), custom_call_target="tpu_custom_call" | custom-call | flops 67108864 | bytes 786432 | tf_op jit(solution)/shard_map/resident/pallas_call | solution.py:322
  13.5 2.1 %all-to-all-done.got_ref = bf16[16,2,16,128]{3,2,1,0:T(8,128)(2,1)S(1)} async-done(((bf16[16,2,16,128]{3,2,1,0:T(8,128)(2,1)}), bf16[16,2,16,128]{3,2,1,0:T(8,128)(2,1)S(1)}, u32[]{:S(2)}, u32[]{:S(2)}) %all-to-all-start) | async-done | bytes 131104 | tf_op jit(solution)/shard_map/all_to_all | solution.py:385
  15.7 0.0 copy-done.1
  15.7 0.0 copy-done.3
  15.7 1.3 %arrivals.1 = (bf16[6,2,32,128]{3,2,1,0:T(8,128)(2,1)}, bf16[8,64,128]{2,1,0:T(8,128)(2,1)}) custom-call(bf16[16,2,16,128]{3,2,1,0:T(8,128)(2,1)S(1)} %all-to-all-done.got_ref, bf16[6,2,32,128]{3,2,1,0:T(8,128)(2,1)S(1)} %bitcast.43, bf16[48,128]{1,0:T(8,128)(2,1)S(1)} %bitcast.45, bf16[8,64,128]{2,1,0:T(8,128)(2,1)S(1)} %resident.1.done_ref), custom_call_target="tpu_custom_call" | custom-call | tf_op jit(solution)/shard_map/arrivals/pallas_call | solution.py:344
Async XLA Ops:
  2.4 9.0 %copy-start = (bf16[8,2,4096]{2,1,0:T(2,128)(2,1)S(1)}, bf16[8,2,4096]{2,1,0:T(2,128)(2,1)}, u32[]{:S(2)}) copy-start(bf16[8,2,4096]{2,1,0:T(2,128)(2,1)} %param.18) | copy-start | bytes 393220
  2.4 9.0 %copy-start.2 = (bf16[8,2,2,256]{3,2,1,0:T(2,128)(2,1)S(1)}, bf16[8,2,2,256]{3,2,1,0:T(2,128)(2,1)}, u32[]{:S(2)}) copy-start(bf16[8,2,2,256]{3,2,1,0:T(2,128)(2,1)} %param.19) | copy-start | bytes 49156
  2.5 9.0 %copy-start.4 = (bf16[8,64,2,2]{1,3,2,0:T(2,128)(2,1)S(1)}, bf16[8,64,2,2]{1,3,2,0:T(2,128)(2,1)}, u32[]{:S(2)}) copy-start(bf16[8,64,2,2]{1,3,2,0:T(2,128)(2,1)} %param.16) | copy-start | bytes 12292
  2.5 13.2 %all-to-all-start = ((bf16[16,2,16,128]{3,2,1,0:T(8,128)(2,1)}), bf16[16,2,16,128]{3,2,1,0:T(8,128)(2,1)S(1)}, u32[]{:S(2)}, u32[]{:S(2)}) async-start(bf16[16,2,16,128]{3,2,1,0:T(8,128)(2,1)} %get-tuple-element.6), calls=%async_computation | async-start | bytes 262144 | tf_op jit(solution)/shard_map/all_to_all | solution.py:385
  11.5 4.2 %copy-start.1 = (bf16[6,2,4096]{2,1,0:T(2,128)(2,1)S(1)}, bf16[6,2,4096]{2,1,0:T(2,128)(2,1)}, u32[]{:S(2)}) copy-start(bf16[6,2,4096]{2,1,0:T(2,128)(2,1)} %param.20) | copy-start | bytes 294916
  11.5 4.2 %copy-start.3 = (bf16[6,2,2,256]{3,2,1,0:T(2,128)(2,1)S(1)}, bf16[6,2,2,256]{3,2,1,0:T(2,128)(2,1)}, u32[]{:S(2)}) copy-start(bf16[6,2,2,256]{3,2,1,0:T(2,128)(2,1)} %param.21) | copy-start | bytes 36868

commit v6 on v5

--- a/solution.py
+++ b/solution.py
@@ -60,12 +60,12 @@
 
 
 def pack_kernel(
-    tp, heads, block_rows, dest_hbm, blocks_hbm, codes_hbm, scales_hbm, cache_hbm,
-    send_ref, cache_ref, dest_ref, blocks_ref, codes_ref, scales_ref, sems,
+    tp, heads, block_rows, dest_hbm, blocks_hbm, codes_hbm, scales_hbm, send_ref,
+    dest_ref, blocks_ref, codes_ref, scales_ref, sems,
 ):
     pairs = [
         (codes_hbm, codes_ref), (scales_hbm, scales_ref),
-        (dest_hbm, dest_ref), (blocks_hbm, blocks_ref), (cache_hbm, cache_ref),
+        (dest_hbm, dest_ref), (blocks_hbm, blocks_ref),
     ]
     copies = [pltpu.make_async_copy(a, b, sems.at[i]) for i, (a, b) in enumerate(pairs)]
     for copy in copies:
@@ -73,32 +73,31 @@
     requests, all_rows = codes_ref.shape[:2]
     rows = all_rows // heads
     per_core = heads // tp
-    last = send_ref.shape[0] - 1
+    peers = send_ref.shape[0] // tp
     send_ref[...] = jnp.full(send_ref.shape, EMPTY, BF16)
     row_block = over(iota((rows, HD), 0), block_rows)
     to_row = iota((all_rows, all_rows), 0)
     from_row = iota((all_rows, all_rows), 1)
     source = over(mod(to_row, rows), 2) * (2 * heads) + over(to_row, rows) * 2 + mod(to_row, 2)
     by_head = jnp.where(from_row == source, 1.0, 0.0).astype(BF16)
-    for copy in copies[:-1]:
+    for copy in copies:
         copy.wait()
 
     def place(r):
-        there = last - dest_ref[r] * tp
+        there = lax.rem(dest_ref[r] + (peers - peers // 2), peers) * tp
         held = row_block < blocks_ref[r]
         codes = dot_nn(by_head, codes_ref[r])
         scales = scales_ref[r].astype(F32)
         for j in range(heads):
             values = codes[j * rows : (j + 1) * rows] * scales[:, j : j + 1]
             values = jnp.where(held, values, EMPTY).astype(BF16)
-            send_ref[there - j // per_core, j % per_core] = values
+            send_ref[there + j // per_core, j % per_core] = values
 
     if requests <= 8:
         for r in range(requests):
             place(r)
     else:
         lax.fori_loop(0, requests, lambda r, c: (place(r), c)[1], 0)
-    copies[-1].wait()
 
 
 def resident_kernel(len_ref, codes_ref, scales_ref, query_ref, new_ref, out_ref):
@@ -184,19 +183,24 @@
     col = iota((8, columns), 1)
     held = sums < EMPTY
     first = jnp.where(held & (mod(col, sender_rows) == 0), 1.0, 0.0).astype(BF16)
+    starts = list(range(0, columns, piece))
+    half = len(starts) // 2
+
+    def sender(index):
+        at = over(index, sender_rows)
+        return at if half else mod(at + chunks // tp // 2, chunks // tp)
+
     before = jnp.where(
-        over(iota((piece, piece), 0), sender_rows) > over(iota((piece, piece), 1), sender_rows),
-        1.0,
-        0.0,
+        sender(iota((piece, piece), 0)) < sender(iota((piece, piece), 1)), 1.0, 0.0
     ).astype(BF16)
     base = jnp.zeros((8, 1), F32)
-    ranks = []
-    for p in reversed(range(0, columns, piece)):
+    ranks = {}
+    for p in starts[half:] + starts[:half]:
         part = first[:, p : p + piece]
-        ranks.insert(0, dot_nn(part, before) + base)
-        if p:
+        ranks[p] = dot_nn(part, before) + base
+        if half:
             base = base + jnp.sum(part.astype(F32), axis=1, keepdims=True)
-    rank = ranks[0] if len(ranks) == 1 else jnp.concatenate(ranks, axis=1)
+    rank = jnp.concatenate([ranks[p] for p in starts], axis=1)
     slot_of = jnp.where(held & (mod(col, 2) == 0), rank, -1.0)[:1]
     first_slot = (step * slots).astype(F32)
     mine = [slot_of == first_slot + a for a in range(slots)]
@@ -253,7 +257,7 @@
     return pltpu.CompilerParams(vmem_limit_bytes=mib * 2**20)
 
 
-def pack(pre_codes, pre_scales, req_dest, req_blocks, cache, peers, tp):
+def pack(pre_codes, pre_scales, req_dest, req_blocks, peers, tp):
     requests, blocks, block_tokens = pre_codes.shape[:3]
     tokens = blocks * block_tokens
     codes = (
@@ -262,15 +266,12 @@
         .reshape(requests, tokens * KVH * 2, HD)
     )
     scales = pre_scales.reshape(requests, tokens * 2, KVH)
-    ins = [req_dest, req_blocks, codes, scales, cache]
+    ins = [req_dest, req_blocks, codes, scales]
     return pl.pallas_call(
         functools.partial(pack_kernel, tp, KVH, 2 * block_tokens),
-        out_shape=[
-            pltpu.VMEM((peers * tp, KVH // tp, tokens * 2, HD), BF16),
-            pltpu.VMEM(cache.shape, BF16),
-        ],
+        out_shape=pltpu.VMEM((peers * tp, KVH // tp, tokens * 2, HD), BF16),
         in_specs=[whole(pltpu.HBM)] * len(ins),
-        out_specs=[whole()] * 2,
+        out_specs=whole(),
         scratch_shapes=[
             pltpu.SMEM(req_dest.shape, jnp.int32),
             pltpu.SMEM(req_blocks.shape, jnp.int32),
@@ -379,18 +380,16 @@
 ):
     peers = lax.axis_size("wide")
     tp = lax.axis_size("tp")
-    send, cache = pack(
-        pre_codes, pre_scales, req_dest, req_blocks, cache_rows(res_codes), peers, tp
-    )
+    send = pack(pre_codes, pre_scales, req_dest, req_blocks, peers, tp)
     got = lax.all_to_all(
         send,
         ("wide", "tp"),
         split_axis=0,
         concat_axis=0,
         tiled=True,
-        axis_index_groups=[list(reversed(range(peers * tp)))],
-    )
-    done = resident(cache, res_scales, res_len, res_query, res_new)
+        axis_index_groups=[[(i + peers // 2 * tp) % (peers * tp) for i in range(peers * tp)]],
+    )
+    done = resident(cache_rows(res_codes), res_scales, res_len, res_query, res_new)
     arr_out, res_out = arrivals(got, arr_query, arr_new, done, tp)
     return (from_rows(res_out, res_query.shape), from_rows(arr_out, arr_query.shape))
 

time: 17.2 us -> 17.7 us (1.029)
  local copies, waits for them, and re-layouts: 0.03 us -> 1.06 us
  starting transfers between devices: 8.98 us -> 7.98 us
  waiting for transfers between devices: 2.14 us -> 2.59 us
    unnamed x10 -> x12, local copies, waits for them, and re-layouts: 0.03 us -> 1.06 us
    all_to_all x1, starting transfers between devices: 8.98 us -> 7.98 us  [shards(): lax.all_to_all(send, ('wide', 'tp'), split_axis=0, concat_axis=0, tiled=T...]
    all_to_all x1, waiting for transfers between devices: 2.14 us -> 2.59 us  [shards(): lax.all_to_all(send, ('wide', 'tp'), split_axis=0, concat_axis=0, tiled=T...]
where the time goes in v6:
time: 17.7 us; the launch traced here: 17.3 us
  starting transfers between devices  7.98 us (45%)
  Pallas kernels  5.02 us (28%)
  waiting for transfers between devices  2.59 us (15%)
  local copies, waits for them, and re-layouts  1.06 us (6%)
  between operations  0.7 us (4%)
    all_to_all x1, starting transfers between devices, shards(): lax.all_to_all(send, ('wide', 'tp'), split_axis=0, concat_axis=0, tiled=T...  7.98 us
    all_to_all x1, waiting for transfers between devices, shards(): lax.all_to_all(send, ('wide', 'tp'), split_axis=0, concat_axis=0, tiled=T...  2.59 us
    pallas_call x1, Pallas kernels, resident(): pl.pallas_call(resident_kernel, out_shape=pltpu.VMEM(query.shape, BF16),...  1.99 us
    pallas_call x1, Pallas kernels, pack(): pl.pallas_call(functools.partial(pack_kernel, tp, KVH, 2 * block_tokens),...  1.7 us
    pallas_call x1, Pallas kernels, arrivals(): pl.pallas_call(functools.partial(arrival_kernel, tp), out_shape=[jax.Shap...  1.33 us
    unnamed x12, local copies, waits for them, and re-layouts  1.06 us
  transfers between devices with their start and end apart: 1, of which 1 were waited for; matrix products, arithmetic and copies ran while one was open for 0% of the time, Pallas kernels for 12%

profile of v6, /device:TPU:0, one launch (start us, length us, event | category | flops | bytes accessed | tf_op | source)
XLA Modules:
  0.0 17.3 jit_solution(12034035310843142751)
XLA Ops:
  0.6 1.7 %pack.1 = bf16[16,2,16,128]{3,2,1,0:T(8,128)(2,1)} custom-call(s32[4]{0:T(128)} %dest_hbm.1, s32[4]{0:T(128)} %blocks_hbm.1, bf16[4,64,128]{2,1,0:T(8,128)(2,1)} %bitcast.48, bf16[4,16,4]{2,1,0:T(8,128)(2,1)} %bitcast.49), custom_call_target="tpu_custom_call" | custom-call | tf_op jit(solution)/shard_map/pack/pallas_call | solution.py:270
  2.3 0.0 copy-start.1
  2.3 0.0 copy-start.3
  2.4 0.0 copy-start.5
  2.4 8.0 %all-to-all-start = ((bf16[16,2,16,128]{3,2,1,0:T(8,128)(2,1)}), bf16[16,2,16,128]{3,2,1,0:T(8,128)(2,1)S(1)}, u32[]{:S(2)}, u32[]{:S(2)}) async-start(bf16[16,2,16,128]{3,2,1,0:T(8,128)(2,1)} %pack.1), calls=%async_computation | async-start | bytes 262144 | tf_op jit(solution)/shard_map/all_to_all | solution.py:384
  10.3 0.0 copy-done.1
  10.4 0.0 copy-done.3
  10.4 0.0 copy-done.5
  10.4 0.0 copy-start
  10.4 1.0 %copy-done = bf16[8,64,2,256]{3,2,1,0:T(2,128)(2,1)S(1)} copy-done((bf16[8,64,2,256]{3,2,1,0:T(2,128)(2,1)S(1)}, bf16[8,64,2,256]{3,2,1,0:T(2,128)(2,1)}, u32[]{:S(2)}) %copy-start) | copy-done | bytes 524312
  11.4 0.0 copy-start.2
  11.4 0.0 copy-start.4
  11.4 2.0 %resident.1.done_ref = bf16[8,64,128]{2,1,0:T(8,128)(2,1)S(1)} custom-call(s32[8]{0:T(128)} %len_ref.1, bf16[8,256,128]{2,1,0:T(8,128)(2,1)S(1)} %bitcast.42, bf16[8,2,2,64]{3,2,1,0:T(2,128)(2,1)S(1)} %bitcast.47, bf16[8,64,128]{2,1,0:T(8,128)(2,1)S(1)} %bitcast.43, bf16[64,128]{1,0:T(8,128)(2,1)S(1)} %bitcast.45), custom_call_target="tpu_custom_call" | custom-call | flops 67108864 | bytes 786432 | tf_op jit(solution)/shard_map/resident/pallas_call | solution.py:323
  13.4 2.6 %all-to-all-done.got_ref = bf16[16,2,16,128]{3,2,1,0:T(8,128)(2,1)S(1)} async-done(((bf16[16,2,16,128]{3,2,1,0:T(8,128)(2,1)}), bf16[16,2,16,128]{3,2,1,0:T(8,128)(2,1)S(1)}, u32[]{:S(2)}, u32[]{:S(2)}) %all-to-all-start) | async-done | bytes 131104 | tf_op jit(solution)/shard_map/all_to_all | solution.py:384
  16.0 0.0 copy-done.2
  16.0 0.0 copy-done.4
  16.0 1.3 %arrivals.1 = (bf16[6,2,32,128]{3,2,1,0:T(8,128)(2,1)}, bf16[8,64,128]{2,1,0:T(8,128)(2,1)}) custom-call(bf16[16,2,16,128]{3,2,1,0:T(8,128)(2,1)S(1)} %all-to-all-done.got_ref, bf16[6,2,32,128]{3,2,1,0:T(8,128)(2,1)S(1)} %bitcast.44, bf16[48,128]{1,0:T(8,128)(2,1)S(1)} %bitcast.46, bf16[8,64,128]{2,1,0:T(8,128)(2,1)S(1)} %resident.1.done_ref), custom_call_target="tpu_custom_call" | custom-call | tf_op jit(solution)/shard_map/arrivals/pallas_call | solution.py:345
Async XLA Ops:
  2.3 8.0 %copy-start.1 = (bf16[8,2,4096]{2,1,0:T(2,128)(2,1)S(1)}, bf16[8,2,4096]{2,1,0:T(2,128)(2,1)}, u32[]{:S(2)}) copy-start(bf16[8,2,4096]{2,1,0:T(2,128)(2,1)} %param.18) | copy-start | bytes 393220
  2.3 8.0 %copy-start.3 = (bf16[8,2,2,256]{3,2,1,0:T(2,128)(2,1)S(1)}, bf16[8,2,2,256]{3,2,1,0:T(2,128)(2,1)}, u32[]{:S(2)}) copy-start(bf16[8,2,2,256]{3,2,1,0:T(2,128)(2,1)} %param.19) | copy-start | bytes 49156
  2.4 8.0 %copy-start.5 = (bf16[8,64,2,2]{1,3,2,0:T(2,128)(2,1)S(1)}, bf16[8,64,2,2]{1,3,2,0:T(2,128)(2,1)}, u32[]{:S(2)}) copy-start(bf16[8,64,2,2]{1,3,2,0:T(2,128)(2,1)} %param.16) | copy-start | bytes 12292
  2.4 13.6 %all-to-all-start = ((bf16[16,2,16,128]{3,2,1,0:T(8,128)(2,1)}), bf16[16,2,16,128]{3,2,1,0:T(8,128)(2,1)S(1)}, u32[]{:S(2)}, u32[]{:S(2)}) async-start(bf16[16,2,16,128]{3,2,1,0:T(8,128)(2,1)} %pack.1), calls=%async_computation | async-start | bytes 262144 | tf_op jit(solution)/shard_map/all_to_all | solution.py:384
  10.4 1.0 %copy-start = (bf16[8,64,2,256]{3,2,1,0:T(2,128)(2,1)S(1)}, bf16[8,64,2,256]{3,2,1,0:T(2,128)(2,1)}, u32[]{:S(2)}) copy-start(bf16[8,64,2,256]{3,2,1,0:T(2,128)(2,1)} %param.15) | copy-start | bytes 1572868
  11.4 4.6 %copy-start.2 = (bf16[6,2,4096]{2,1,0:T(2,128)(2,1)S(1)}, bf16[6,2,4096]{2,1,0:T(2,128)(2,1)}, u32[]{:S(2)}) copy-start(bf16[6,2,4096]{2,1,0:T(2,128)(2,1)} %param.20) | copy-start | bytes 294916
  11.4 4.6 %copy-start.4 = (bf16[6,2,2,256]{3,2,1,0:T(2,128)(2,1)S(1)}, bf16[6,2,2,256]{3,2,1,0:T(2,128)(2,1)}, u32[]{:S(2)}) copy-start(bf16[6,2,2,256]{3,2,1,0:T(2,128)(2,1)} %param.21) | copy-start | bytes 36868

commit v7 on v6

--- a/solution.py
+++ b/solution.py
@@ -98,6 +98,136 @@
             place(r)
     else:
         lax.fori_loop(0, requests, lambda r, c: (place(r), c)[1], 0)
+
+
+def spread_kernel(
+    tp, heads, block_rows, dest_hbm, blocks_hbm, codes_hbm, scales_hbm, own_hbm, other_ref,
+    dest_ref, blocks_ref, codes_ref, scales_ref, own_ref, sems,
+):
+    pairs = [
+        (codes_hbm, codes_ref), (scales_hbm, scales_ref),
+        (dest_hbm, dest_ref), (blocks_hbm, blocks_ref),
+    ]
+    copies = [pltpu.make_async_copy(a, b, sems.at[i]) for i, (a, b) in enumerate(pairs)]
+    for copy in copies:
+        copy.start()
+    requests, all_rows = codes_ref.shape[:2]
+    rows = all_rows // heads
+    per_core = heads // tp
+    core = lax.axis_index("tp")
+    row_block = over(iota((rows, HD), 0), block_rows)
+    to_row = iota((all_rows, all_rows), 0)
+    from_row = iota((all_rows, all_rows), 1)
+    at_core = mod(over(to_row, rows * per_core) + core, tp) * per_core
+    head = at_core + mod(over(to_row, rows), per_core)
+    source = over(mod(to_row, rows), 2) * (2 * heads) + head * 2 + mod(to_row, 2)
+    by_head = jnp.where(from_row == source, 1.0, 0.0).astype(BF16)
+    tag_row = iota((16, HD), 0)
+    for copy in copies:
+        copy.wait()
+    tags = jnp.full((16, HD), -1.0, F32)
+    for r in range(requests):
+        tags = jnp.where(tag_row == r, dest_ref[r].astype(F32), tags)
+        held = row_block < blocks_ref[r]
+        codes = dot_nn(by_head, codes_ref[r])
+        scales = scales_ref[r].astype(F32)
+        swapped = jnp.concatenate([scales[:, per_core:], scales[:, :per_core]], axis=1)
+        scales = jnp.where(core == 0, scales, swapped)
+        for j in range(heads):
+            values = codes[j * rows : (j + 1) * rows] * scales[:, j : j + 1]
+            values = jnp.where(held, values, EMPTY).astype(BF16)
+            to = own_ref if j < per_core else other_ref
+            at = ((j % per_core) * requests + r) * rows
+            to[at : at + rows] = values
+    at = per_core * requests * rows
+    own_ref[at : at + 16] = tags.astype(BF16)
+    other_ref[at : at + 16] = tags.astype(BF16)
+    out = pltpu.make_async_copy(own_ref, own_hbm, sems.at[0])
+    out.start()
+    out.wait()
+
+
+def gathered_kernel(
+    requests, heads, own_ref, other_ref, query_ref, new_ref, done_ref, out_hbm, done_hbm,
+    out_ref, sems,
+):
+    hand_on = pltpu.make_async_copy(done_ref, done_hbm, sems.at[0])
+    hand_on.start()
+    senders, height = own_ref.shape[:2]
+    slots, _, per_head = query_ref.shape[:3]
+    rows = slots * per_head
+    every = range(heads)
+    span = (height - 16) // heads
+    columns = senders * span
+    here = lax.axis_index("wide").astype(F32)
+
+    tags = own_ref[:, heads * span :].reshape(senders * 16, HD)
+    lane = iota((16, HD), 1)
+    pick = jnp.where(lane == 0, 1.0, 0.0).astype(BF16)
+    dest = dot_nt(pick, tags)
+    match = jnp.where(dest == here, 1.0, 0.0)
+    n = senders * 16
+    before = jnp.where(iota((n, n), 0) < iota((n, n), 1), 1.0, 0.0).astype(BF16)
+    rank = dot_nn(match.astype(BF16), before)
+    place = jnp.where(match > 0, rank + 1, 0.0).astype(BF16)
+    unit = span // requests
+    col = iota((n, columns), 1)
+    tag = iota((n, columns), 0)
+    expand = jnp.where(
+        tag == over(col, span) * 16 + mod(over(col, unit), requests), 1.0, 0.0
+    ).astype(BF16)
+    slot_of = dot_nn(place, expand)[:8] - 1
+
+    parts = [ref[:, h * span : (h + 1) * span].reshape(columns, HD) for h in every for ref in (own_ref, other_ref)]
+    queries = [query_ref[:, h].reshape(rows, HD) for h in every]
+    new = new_ref[...]
+    ones = jnp.ones((16, HD), BF16)
+    caches = [jnp.concatenate([parts[2 * h], parts[2 * h + 1]], axis=0) for h in every]
+    scores = [dot_nt(jnp.concatenate([ones, queries[0]], axis=0), caches[0])]
+    sums, scores[0] = scores[0][:8], scores[0][16:]
+    scores += [dot_nt(queries[h], caches[h]) for h in every[1:]]
+    new_all = dot_nt(jnp.concatenate(queries, axis=0), new)
+    key = mod(iota((8, 2 * columns), 1), 2) == 0
+    slot_of = jnp.concatenate([slot_of, slot_of], axis=1)
+    slot_of = jnp.where((sums < EMPTY) & key, slot_of, -1.0)[:1]
+    mine = [slot_of == a for a in range(slots)]
+
+    new_col = iota((rows, new.shape[0]), 1)
+    new_row = iota((rows, new.shape[0]), 0)
+    new_here = (
+        (mod(new_col, 2) == 0)
+        & (over(new_col, 2 * heads * STEPS) == over(new_row, per_head))
+        & (mod(over(new_col, 2 * heads), STEPS) <= mod(new_row, STEPS))
+    )
+    new_head = jnp.where(new_here, mod(over(new_col, 2), heads), heads)
+    scores = [
+        jnp.concatenate(
+            [
+                jnp.where(mine[a], scores[h][a * per_head : (a + 1) * per_head] * SCORE_SCALE, NEGATIVE)
+                for a in range(slots)
+            ],
+            axis=0,
+        )
+        for h in every
+    ]
+    new_scores = [
+        jnp.where(new_head == h, new_all[h * rows : (h + 1) * rows] * SCORE_SCALE, NEGATIVE)
+        for h in every
+    ]
+    top = [top_of(scores[h], new_scores[h]) for h in every]
+    weights = [jnp.exp(scores[h] - top[h]) for h in every]
+    new_weights = [jnp.exp(new_scores[h] - top[h]) for h in every]
+    total = [sum_of(weights[h], new_weights[h]) for h in every]
+    new_mixed = dot_nn(jnp.concatenate(new_weights, axis=0).astype(BF16), values_up(new))
+    copies = []
+    for h in every:
+        mixed = dot_nn(to_values(weights[h]), caches[h]) + new_mixed[h * rows : (h + 1) * rows]
+        out_ref[h] = (mixed * (1.0 / total[h])).astype(BF16).reshape(slots, per_head, HD)
+        copies.append(pltpu.make_async_copy(out_ref.at[h], out_hbm.at[:, h], sems.at[1 + h]))
+        copies[-1].start()
+    for copy in copies:
+        copy.wait()
+    hand_on.wait()
 
 
 def resident_kernel(len_ref, codes_ref, scales_ref, query_ref, new_ref, out_ref):
@@ -282,6 +412,57 @@
         compiler_params=limit(16),
         name="pack",
     )(*[in_hbm(x) for x in ins])
+
+
+def spread(pre_codes, pre_scales, req_dest, req_blocks, tp):
+    requests, blocks, block_tokens = pre_codes.shape[:3]
+    tokens = blocks * block_tokens
+    codes = (
+        pre_codes.reshape(requests, tokens, 2, KVH, HD)
+        .transpose(0, 1, 3, 2, 4)
+        .reshape(requests, tokens * KVH * 2, HD)
+    )
+    scales = pre_scales.reshape(requests, tokens * 2, KVH)
+    ins = [req_dest, req_blocks, codes, scales]
+    shape = (KVH // tp * requests * tokens * 2 + 16, HD)
+    return pl.pallas_call(
+        functools.partial(spread_kernel, tp, KVH, 2 * block_tokens),
+        out_shape=[pltpu.HBM(shape, BF16), pltpu.VMEM(shape, BF16)],
+        in_specs=[whole(pltpu.HBM)] * len(ins),
+        out_specs=[whole(pltpu.HBM), whole()],
+        scratch_shapes=[
+            pltpu.SMEM(req_dest.shape, jnp.int32),
+            pltpu.SMEM(req_blocks.shape, jnp.int32),
+            pltpu.VMEM(codes.shape, BF16),
+            pltpu.VMEM(scales.shape, BF16),
+            pltpu.VMEM(shape, BF16),
+            pltpu.SemaphoreType.DMA((len(ins),)),
+        ],
+        compiler_params=limit(16),
+        name="spread",
+    )(*[in_hbm(x) for x in ins])
+
+
+def gathered(own, other, requests, arr_query, arr_new, done):
+    slots, steps, width = arr_query.shape
+    heads = width // (HD * GROUP)
+    query = query_rows(arr_query).reshape(slots, heads, GROUP * steps, HD)
+    new = new_rows_of(arr_new)
+    return pl.pallas_call(
+        functools.partial(gathered_kernel, requests, heads),
+        out_shape=[
+            jax.ShapeDtypeStruct(query.shape, BF16),
+            jax.ShapeDtypeStruct(done.shape, BF16),
+        ],
+        in_specs=[whole()] * 5,
+        out_specs=[whole(pltpu.HBM)] * 2,
+        scratch_shapes=[
+            pltpu.VMEM((heads, slots) + query.shape[2:], BF16),
+            pltpu.SemaphoreType.DMA((1 + heads,)),
+        ],
+        compiler_params=limit(24),
+        name="gathered",
+    )(in_hbm(own), in_hbm(other), query, new, done)
 
 
 def cache_rows(codes):
@@ -380,17 +561,26 @@
 ):
     peers = lax.axis_size("wide")
     tp = lax.axis_size("tp")
-    send = pack(pre_codes, pre_scales, req_dest, req_blocks, peers, tp)
-    got = lax.all_to_all(
-        send,
-        ("wide", "tp"),
-        split_axis=0,
-        concat_axis=0,
-        tiled=True,
-        axis_index_groups=[[(i + peers // 2 * tp) % (peers * tp) for i in range(peers * tp)]],
-    )
-    done = resident(cache_rows(res_codes), res_scales, res_len, res_query, res_new)
-    arr_out, res_out = arrivals(got, arr_query, arr_new, done, tp)
+    res = (cache_rows(res_codes), res_scales, res_len, res_query, res_new)
+    if peers <= 8:
+        own, other = spread(pre_codes, pre_scales, req_dest, req_blocks, tp)
+        own = lax.all_gather(own, "wide")
+        other = lax.ppermute(other, "tp", [(t, tp - 1 - t) for t in range(tp)])
+        other = lax.all_gather(other, "wide")
+        done = resident(*res)
+        arr_out, res_out = gathered(own, other, req_dest.shape[0], arr_query, arr_new, done)
+    else:
+        send = pack(pre_codes, pre_scales, req_dest, req_blocks, peers, tp)
+        got = lax.all_to_all(
+            send,
+            ("wide", "tp"),
+            split_axis=0,
+            concat_axis=0,
+            tiled=True,
+            axis_index_groups=[[(i + peers // 2 * tp) % (peers * tp) for i in range(peers * tp)]],
+        )
+        done = resident(*res)
+        arr_out, res_out = arrivals(got, arr_query, arr_new, done, tp)
     return (from_rows(res_out, res_query.shape), from_rows(arr_out, arr_query.shape))
 
 

time: 17.7 us -> 77.1 us (4.36)
  blocking collectives: 0 us -> 67.5 us
  starting transfers between devices: 7.98 us -> 0.52 us
  waiting for transfers between devices: 2.59 us -> 0.01 us
  Pallas kernels: 5.02 us -> 7.05 us
    all_gather x0 -> x2, blocking collectives: none -> 67.5 us  [the longest x1 34.5 us: shards(): own = lax.all_gather(own, 'wide')]
    all_to_all x1 -> x0, starting transfers between devices: 7.98 us -> none  [shards(): lax.all_to_all(send, ('wide', 'tp'), split_axis=0, concat_axis=0, tiled=T...]
    all_to_all x1 -> x0, waiting for transfers between devices: 2.59 us -> none  [shards(): lax.all_to_all(send, ('wide', 'tp'), split_axis=0, concat_axis=0, tiled=T...]
    pallas_call x2, Pallas kernels: 3.03 us -> 5.19 us  [the longest x1 3.5 us: gathered(): pl.pallas_call(functools.partial(gathered_kernel, requests, heads), out_s...]
  transfers between devices with their start and end apart: 1 -> 1, of which waited for: 1 -> 0; matrix products, arithmetic and copies ran while one was open for 0% -> 0% of each run, Pallas kernels for 12% -> 2%
where the time goes in v7:
time: 77.1 us; the launch traced here: 76.8 us
  blocking collectives  67.5 us (88%)
  Pallas kernels  7.05 us (9%)
  local copies, waits for them, and re-layouts  1.06 us (1%)
    all_gather x1, blocking collectives, shards(): own = lax.all_gather(own, 'wide')  34.5 us
    all_gather x1, blocking collectives, shards(): other = lax.all_gather(other, 'wide')  32.9 us
    pallas_call x1, Pallas kernels, gathered(): pl.pallas_call(functools.partial(gathered_kernel, requests, heads), out_s...  3.5 us
    pallas_call x1, Pallas kernels, resident(): pl.pallas_call(resident_kernel, out_shape=pltpu.VMEM(query.shape, BF16),...  1.86 us
    pallas_call x1, Pallas kernels, spread(): pl.pallas_call(functools.partial(spread_kernel, tp, KVH, 2 * block_tokens...  1.68 us
  transfers between devices with their start and end apart: 1, of which 0 were waited for; matrix products, arithmetic and copies ran while one was open for 0% of the time, Pallas kernels for 2%

profile of v7, /device:TPU:0, one launch (start us, length us, event | category | flops | bytes accessed | tf_op | source)
XLA Modules:
  0.0 76.8 jit_solution(11792927959826987197)
XLA Ops:
  0.6 1.7 %spread.1 = (bf16[144,128]{1,0:T(8,128)(2,1)}, bf16[144,128]{1,0:T(8,128)(2,1)S(1)}) custom-call(s32[4]{0:T(128)} %dest_hbm.1, s32[4]{0:T(128)} %blocks_hbm.1, bf16[4,64,128]{2,1,0:T(8,128)(2,1)} %bitcast.52, bf16[4,16,4]{2,1,0:T(8,128)(2,1)} %bitcast.53), custom_call_target="tpu_custom_call" | custom-call | tf_op jit(solution)/shard_map/spread/pallas_call | solution.py:428
  2.3 0.5 collective-permute-start
  2.8 0.0 copy-start.1
  2.8 0.0 copy-start.3
  2.8 0.0 copy-start.5
  2.8 34.5 %all-gather = bf16[1152,128]{1,0:T(8,128)(2,1)} all-gather(bf16[144,128]{1,0:T(8,128)(2,1)} %get-tuple-element.6), channel_id=2, replica_groups=mesh['groups'=2,'wide'=8,'tp'=2] {'wide'}, dimensions={0}, use_global_device_ids=true | all-gather | bytes 331776 | tf_op jit(solution)/shard_map/all_gather | solution.py:567
  37.4 0.0 copy-done.1
  37.4 0.0 copy-done.3
  37.4 0.0 copy-done.5
  37.4 0.0 copy-start
  37.4 1.0 %copy-done = bf16[8,64,2,256]{3,2,1,0:T(2,128)(2,1)S(1)} copy-done((bf16[8,64,2,256]{3,2,1,0:T(2,128)(2,1)S(1)}, bf16[8,64,2,256]{3,2,1,0:T(2,128)(2,1)}, u32[]{:S(2)}) %copy-start) | copy-done | bytes 524312
  38.4 1.9 %resident.1.done_ref = bf16[8,64,128]{2,1,0:T(8,128)(2,1)S(1)} custom-call(s32[8]{0:T(128)} %len_ref.1, bf16[8,256,128]{2,1,0:T(8,128)(2,1)S(1)} %bitcast.44, bf16[8,2,2,64]{3,2,1,0:T(2,128)(2,1)S(1)} %bitcast.49, bf16[8,64,128]{2,1,0:T(8,128)(2,1)S(1)} %bitcast.45, bf16[64,128]{1,0:T(8,128)(2,1)S(1)} %bitcast.47), custom_call_target="tpu_custom_call" | custom-call | flops 67108864 | bytes 786432 | tf_op jit(solution)/shard_map/resident/pallas_call | solution.py:504
  40.3 0.0 copy-start.2
  40.3 0.0 collective-permute-done
  40.3 0.0 copy-start.4
  40.3 32.9 %all-gather.1 = bf16[1152,128]{1,0:T(8,128)(2,1)} all-gather(bf16[144,128]{1,0:T(8,128)(2,1)S(1)} %collective-permute-done), channel_id=3, replica_groups=mesh['groups'=2,'wide'=8,'tp'=2] {'wide'}, dimensions={0}, use_global_device_ids=true | all-gather | bytes 331776 | tf_op jit(solution)/shard_map/all_gather | solution.py:569
  73.3 0.0 copy-done.2
  73.3 0.0 copy-done.4
  73.3 3.5 %gathered.1 = (bf16[6,2,32,128]{3,2,1,0:T(8,128)(2,1)}, bf16[8,64,128]{2,1,0:T(8,128)(2,1)}) custom-call(bf16[8,144,128]{2,1,0:T(8,128)(2,1)} %bitcast.50, bf16[8,144,128]{2,1,0:T(8,128)(2,1)} %bitcast.51, bf16[6,2,32,128]{3,2,1,0:T(8,128)(2,1)S(1)} %bitcast.46, bf16[48,128]{1,0:T(8,128)(2,1)S(1)} %bitcast.48, bf16[8,64,128]{2,1,0:T(8,128)(2,1)S(1)} %resident.1.done_ref), custom_call_target="tpu_custom_call" | custom-call | tf_op jit(solution)/shard_map/gathered/pallas_call | solution.py:451
Async XLA Ops:
  2.3 38.0 %collective-permute-start = (bf16[144,128]{1,0:T(8,128)(2,1)S(1)}, bf16[144,128]{1,0:T(8,128)(2,1)S(1)}, u32[]{:S(2)}, u32[]{:S(2)}) collective-permute-start(bf16[144,128]{1,0:T(8,128)(2,1)S(1)} %get-tuple-element.7), channel_id=1, source_target_pairs={{0,1},{1,0},{2,3},{3,2},{4,5},{5,4},{6,7},{7,6},{8,9},{9,8},{10,11... | collective-permute-start | bytes 110600 | tf_op jit(solution)/shard_map/ppermute | solution.py:568
  2.8 34.5 %copy-start.1 = (bf16[8,2,4096]{2,1,0:T(2,128)(2,1)S(1)}, bf16[8,2,4096]{2,1,0:T(2,128)(2,1)}, u32[]{:S(2)}) copy-start(bf16[8,2,4096]{2,1,0:T(2,128)(2,1)} %param.18) | copy-start | bytes 393220
  2.8 34.5 %copy-start.3 = (bf16[8,2,2,256]{3,2,1,0:T(2,128)(2,1)S(1)}, bf16[8,2,2,256]{3,2,1,0:T(2,128)(2,1)}, u32[]{:S(2)}) copy-start(bf16[8,2,2,256]{3,2,1,0:T(2,128)(2,1)} %param.19) | copy-start | bytes 49156
  2.8 34.5 %copy-start.5 = (bf16[8,64,2,2]{1,3,2,0:T(2,128)(2,1)S(1)}, bf16[8,64,2,2]{1,3,2,0:T(2,128)(2,1)}, u32[]{:S(2)}) copy-start(bf16[8,64,2,2]{1,3,2,0:T(2,128)(2,1)} %param.16) | copy-start | bytes 12292
  37.4 1.0 %copy-start = (bf16[8,64,2,256]{3,2,1,0:T(2,128)(2,1)S(1)}, bf16[8,64,2,256]{3,2,1,0:T(2,128)(2,1)}, u32[]{:S(2)}) copy-start(bf16[8,64,2,256]{3,2,1,0:T(2,128)(2,1)} %param.15) | copy-start | bytes 1572868
  40.3 33.0 %copy-start.2 = (bf16[6,2,4096]{2,1,0:T(2,128)(2,1)S(1)}, bf16[6,2,4096]{2,1,0:T(2,128)(2,1)}, u32[]{:S(2)}) copy-start(bf16[6,2,4096]{2,1,0:T(2,128)(2,1)} %param.20) | copy-start | bytes 294916
  40.3 33.0 %copy-start.4 = (bf16[6,2,2,256]{3,2,1,0:T(2,128)(2,1)S(1)}, bf16[6,2,2,256]{3,2,1,0:T(2,128)(2,1)}, u32[]{:S(2)}) copy-start(bf16[6,2,2,256]{3,2,1,0:T(2,128)(2,1)} %param.21) | copy-start | bytes 36868

commit v8 on v6

--- a/solution.py
+++ b/solution.py
@@ -34,6 +34,20 @@
     return jnp.bitwise_and(x, n - 1) if n & (n - 1) == 0 else x % n
 
 
+def place_of(instance, peers, middle):
+    if middle is None:
+        return instance
+    place = jnp.where(instance > middle, peers - instance, peers - 1 - instance)
+    return jnp.where(instance == middle, 0, place)
+
+
+def instance_at(place, peers, middle):
+    if middle is None:
+        return place
+    instance = jnp.where(place < peers - middle, peers - place, peers - 1 - place)
+    return jnp.where(place == 0, middle, instance)
+
+
 def dot_nt(a, b):
     return lax.dot_general(a, b, (((1,), (1,)), ((), ())), preferred_element_type=F32)
 
@@ -60,17 +74,19 @@
 
 
 def pack_kernel(
-    tp, heads, block_rows, dest_hbm, blocks_hbm, codes_hbm, scales_hbm, send_ref,
+    tp, middle, heads, block_rows, dest_hbm, blocks_hbm, codes_hbm, scales_hbm, send_ref,
     dest_ref, blocks_ref, codes_ref, scales_ref, sems,
 ):
-    pairs = [
-        (codes_hbm, codes_ref), (scales_hbm, scales_ref),
-        (dest_hbm, dest_ref), (blocks_hbm, blocks_ref),
-    ]
+    requests, all_rows = codes_ref.shape[:2]
+    few = requests <= 8
+    pairs = [(dest_hbm, dest_ref), (blocks_hbm, blocks_ref), (scales_hbm, scales_ref)]
+    if few:
+        pairs += [(codes_hbm.at[r], codes_ref.at[r]) for r in range(requests)]
+    else:
+        pairs += [(codes_hbm, codes_ref)]
     copies = [pltpu.make_async_copy(a, b, sems.at[i]) for i, (a, b) in enumerate(pairs)]
     for copy in copies:
         copy.start()
-    requests, all_rows = codes_ref.shape[:2]
     rows = all_rows // heads
     per_core = heads // tp
     peers = send_ref.shape[0] // tp
@@ -80,23 +96,25 @@
     from_row = iota((all_rows, all_rows), 1)
     source = over(mod(to_row, rows), 2) * (2 * heads) + over(to_row, rows) * 2 + mod(to_row, 2)
     by_head = jnp.where(from_row == source, 1.0, 0.0).astype(BF16)
-    for copy in copies:
+    for copy in copies[:3]:
         copy.wait()
 
     def place(r):
-        there = lax.rem(dest_ref[r] + (peers - peers // 2), peers) * tp
+        there = place_of(dest_ref[r], peers, middle) * tp + tp - 1
         held = row_block < blocks_ref[r]
         codes = dot_nn(by_head, codes_ref[r])
         scales = scales_ref[r].astype(F32)
         for j in range(heads):
             values = codes[j * rows : (j + 1) * rows] * scales[:, j : j + 1]
             values = jnp.where(held, values, EMPTY).astype(BF16)
-            send_ref[there + j // per_core, j % per_core] = values
-
-    if requests <= 8:
+            send_ref[there - j // per_core, j % per_core] = values
+
+    if few:
         for r in range(requests):
+            copies[3 + r].wait()
             place(r)
     else:
+        copies[3].wait()
         lax.fori_loop(0, requests, lambda r, c: (place(r), c)[1], 0)
 
 
@@ -157,7 +175,7 @@
 
 
 def arrival_kernel(
-    tp, got_ref, query_ref, new_ref, done_ref, out_hbm, done_hbm, out_ref, sems
+    tp, middle, got_ref, query_ref, new_ref, done_ref, out_hbm, done_hbm, out_ref, sems
 ):
     step = pl.program_id(0)
     hand_on = pltpu.make_async_copy(done_ref, done_hbm, sems.at[0])
@@ -183,24 +201,20 @@
     col = iota((8, columns), 1)
     held = sums < EMPTY
     first = jnp.where(held & (mod(col, sender_rows) == 0), 1.0, 0.0).astype(BF16)
-    starts = list(range(0, columns, piece))
-    half = len(starts) // 2
-
     def sender(index):
-        at = over(index, sender_rows)
-        return at if half else mod(at + chunks // tp // 2, chunks // tp)
+        return instance_at(over(index, sender_rows), chunks // tp, middle)
 
     before = jnp.where(
         sender(iota((piece, piece), 0)) < sender(iota((piece, piece), 1)), 1.0, 0.0
     ).astype(BF16)
     base = jnp.zeros((8, 1), F32)
-    ranks = {}
-    for p in starts[half:] + starts[:half]:
+    ranks = []
+    for p in range(0, columns, piece):
         part = first[:, p : p + piece]
-        ranks[p] = dot_nn(part, before) + base
-        if half:
+        ranks.append(dot_nn(part, before) + base)
+        if p + piece < columns:
             base = base + jnp.sum(part.astype(F32), axis=1, keepdims=True)
-    rank = jnp.concatenate([ranks[p] for p in starts], axis=1)
+    rank = jnp.concatenate(ranks, axis=1)
     slot_of = jnp.where(held & (mod(col, 2) == 0), rank, -1.0)[:1]
     first_slot = (step * slots).astype(F32)
     mine = [slot_of == first_slot + a for a in range(slots)]
@@ -257,7 +271,7 @@
     return pltpu.CompilerParams(vmem_limit_bytes=mib * 2**20)
 
 
-def pack(pre_codes, pre_scales, req_dest, req_blocks, peers, tp):
+def pack(pre_codes, pre_scales, req_dest, req_blocks, peers, tp, middle):
     requests, blocks, block_tokens = pre_codes.shape[:3]
     tokens = blocks * block_tokens
     codes = (
@@ -268,7 +282,7 @@
     scales = pre_scales.reshape(requests, tokens * 2, KVH)
     ins = [req_dest, req_blocks, codes, scales]
     return pl.pallas_call(
-        functools.partial(pack_kernel, tp, KVH, 2 * block_tokens),
+        functools.partial(pack_kernel, tp, middle, KVH, 2 * block_tokens),
         out_shape=pltpu.VMEM((peers * tp, KVH // tp, tokens * 2, HD), BF16),
         in_specs=[whole(pltpu.HBM)] * len(ins),
         out_specs=whole(),
@@ -277,7 +291,7 @@
             pltpu.SMEM(req_blocks.shape, jnp.int32),
             pltpu.VMEM(codes.shape, BF16),
             pltpu.VMEM(scales.shape, BF16),
-            pltpu.SemaphoreType.DMA((len(ins),)),
+            pltpu.SemaphoreType.DMA((3 + (requests if requests <= 8 else 1),)),
         ],
         compiler_params=limit(16),
         name="pack",
@@ -335,7 +349,7 @@
     )(in_hbm(res_len), codes, scales, query, new_rows_of(res_new))
 
 
-def arrivals(got, arr_query, arr_new, done, tp):
+def arrivals(got, arr_query, arr_new, done, tp, middle):
     slots, steps, width = arr_query.shape
     heads = width // (HD * GROUP)
     query = query_rows(arr_query).reshape(slots, heads, GROUP * steps, HD)
@@ -343,7 +357,7 @@
     size = max(n for n in range(1, 7) if slots % n == 0)
     small = got.size <= 2**18
     return pl.pallas_call(
-        functools.partial(arrival_kernel, tp),
+        functools.partial(arrival_kernel, tp, middle),
         out_shape=[
             jax.ShapeDtypeStruct(query.shape, BF16),
             jax.ShapeDtypeStruct(done.shape, BF16),
@@ -380,17 +394,20 @@
 ):
     peers = lax.axis_size("wide")
     tp = lax.axis_size("tp")
-    send = pack(pre_codes, pre_scales, req_dest, req_blocks, peers, tp)
+    middle = peers // 2 - 1 if peers <= 8 else None
+    order = [peers // 2 - 1] + [w for w in reversed(range(peers)) if w != peers // 2 - 1]
+    order = list(range(peers)) if middle is None else order
+    send = pack(pre_codes, pre_scales, req_dest, req_blocks, peers, tp, middle)
     got = lax.all_to_all(
         send,
         ("wide", "tp"),
         split_axis=0,
         concat_axis=0,
         tiled=True,
-        axis_index_groups=[[(i + peers // 2 * tp) % (peers * tp) for i in range(peers * tp)]],
+        axis_index_groups=[[w * tp + t for w in order for t in reversed(range(tp))]],
     )
     done = resident(cache_rows(res_codes), res_scales, res_len, res_query, res_new)
-    arr_out, res_out = arrivals(got, arr_query, arr_new, done, tp)
+    arr_out, res_out = arrivals(got, arr_query, arr_new, done, tp, middle)
     return (from_rows(res_out, res_query.shape), from_rows(arr_out, arr_query.shape))
 
 

time: 17.7 us -> 17 us (0.960)
  waiting for transfers between devices: 2.59 us -> 1.84 us
  Pallas kernels: 5.02 us -> 5.31 us
  starting transfers between devices: 7.98 us -> 7.73 us
    all_to_all x1, waiting for transfers between devices: 2.59 us -> 1.84 us  [shards(): lax.all_to_all(send, ('wide', 'tp'), split_axis=0, concat_axis=0, tiled=T...]
    pallas_call x2, Pallas kernels: 3.03 us -> 3.31 us  [the longest x1 1.98 us: pack(): pl.pallas_call(functools.partial(pack_kernel, tp, middle, KVH, 2 * block_...]
    all_to_all x1, starting transfers between devices: 7.98 us -> 7.73 us  [shards(): lax.all_to_all(send, ('wide', 'tp'), split_axis=0, concat_axis=0, tiled=T...]
where the time goes in v8:
time: 17 us; the launch traced here: 16.6 us
  starting transfers between devices  7.73 us (45%)
  Pallas kernels  5.31 us (31%)
  waiting for transfers between devices  1.84 us (11%)
  local copies, waits for them, and re-layouts  1.06 us (6%)
  between operations  0.7 us (4%)
    all_to_all x1, starting transfers between devices, shards(): lax.all_to_all(send, ('wide', 'tp'), split_axis=0, concat_axis=0, tiled=T...  7.73 us
    pallas_call x1, Pallas kernels, resident(): pl.pallas_call(resident_kernel, out_shape=pltpu.VMEM(query.shape, BF16),...  1.99 us
    pallas_call x1, Pallas kernels, pack(): pl.pallas_call(functools.partial(pack_kernel, tp, middle, KVH, 2 * block_...  1.98 us
    all_to_all x1, waiting for transfers between devices, shards(): lax.all_to_all(send, ('wide', 'tp'), split_axis=0, concat_axis=0, tiled=T...  1.84 us
    pallas_call x1, Pallas kernels, arrivals(): pl.pallas_call(functools.partial(arrival_kernel, tp, middle), out_shape=[...  1.33 us
    unnamed x12, local copies, waits for them, and re-layouts  1.06 us
  transfers between devices with their start and end apart: 1, of which 1 were waited for; matrix products, arithmetic and copies ran while one was open for 0% of the time, Pallas kernels for 12%

profile of v8, /device:TPU:0, one launch (start us, length us, event | category | flops | bytes accessed | tf_op | source)
XLA Modules:
  0.0 16.6 jit_solution(16040785042062037089)
XLA Ops:
  0.6 2.0 %pack.1 = bf16[16,2,16,128]{3,2,1,0:T(8,128)(2,1)} custom-call(s32[4]{0:T(128)} %dest_hbm.1, s32[4]{0:T(128)} %blocks_hbm.1, bf16[4,64,128]{2,1,0:T(8,128)(2,1)} %bitcast.48, bf16[4,16,4]{2,1,0:T(8,128)(2,1)} %bitcast.49), custom_call_target="tpu_custom_call" | custom-call | tf_op jit(solution)/shard_map/pack/pallas_call | solution.py:284
  2.6 0.0 copy-start.1
  2.6 0.0 copy-start.3
  2.6 0.0 copy-start.5
  2.7 7.7 %all-to-all-start = ((bf16[16,2,16,128]{3,2,1,0:T(8,128)(2,1)}), bf16[16,2,16,128]{3,2,1,0:T(8,128)(2,1)S(1)}, u32[]{:S(2)}, u32[]{:S(2)}) async-start(bf16[16,2,16,128]{3,2,1,0:T(8,128)(2,1)} %pack.1), calls=%async_computation | async-start | bytes 262144 | tf_op jit(solution)/shard_map/all_to_all | solution.py:401
  10.4 0.0 copy-done.1
  10.4 0.0 copy-done.3
  10.4 0.0 copy-done.5
  10.4 0.0 copy-start
  10.4 1.0 %copy-done = bf16[8,64,2,256]{3,2,1,0:T(2,128)(2,1)S(1)} copy-done((bf16[8,64,2,256]{3,2,1,0:T(2,128)(2,1)S(1)}, bf16[8,64,2,256]{3,2,1,0:T(2,128)(2,1)}, u32[]{:S(2)}) %copy-start) | copy-done | bytes 524312
  11.5 0.0 copy-start.2
  11.5 0.0 copy-start.4
  11.5 2.0 %resident.1.done_ref = bf16[8,64,128]{2,1,0:T(8,128)(2,1)S(1)} custom-call(s32[8]{0:T(128)} %len_ref.1, bf16[8,256,128]{2,1,0:T(8,128)(2,1)S(1)} %bitcast.42, bf16[8,2,2,64]{3,2,1,0:T(2,128)(2,1)S(1)} %bitcast.47, bf16[8,64,128]{2,1,0:T(8,128)(2,1)S(1)} %bitcast.43, bf16[64,128]{1,0:T(8,128)(2,1)S(1)} %bitcast.45), custom_call_target="tpu_custom_call" | custom-call | flops 67108864 | bytes 786432 | tf_op jit(solution)/shard_map/resident/pallas_call | solution.py:337
  13.5 1.8 %all-to-all-done.got_ref = bf16[16,2,16,128]{3,2,1,0:T(8,128)(2,1)S(1)} async-done(((bf16[16,2,16,128]{3,2,1,0:T(8,128)(2,1)}), bf16[16,2,16,128]{3,2,1,0:T(8,128)(2,1)S(1)}, u32[]{:S(2)}, u32[]{:S(2)}) %all-to-all-start) | async-done | bytes 131104 | tf_op jit(solution)/shard_map/all_to_all | solution.py:401
  15.3 0.0 copy-done.2
  15.3 0.0 copy-done.4
  15.3 1.3 %arrivals.1 = (bf16[6,2,32,128]{3,2,1,0:T(8,128)(2,1)}, bf16[8,64,128]{2,1,0:T(8,128)(2,1)}) custom-call(bf16[16,2,16,128]{3,2,1,0:T(8,128)(2,1)S(1)} %all-to-all-done.got_ref, bf16[6,2,32,128]{3,2,1,0:T(8,128)(2,1)S(1)} %bitcast.44, bf16[48,128]{1,0:T(8,128)(2,1)S(1)} %bitcast.46, bf16[8,64,128]{2,1,0:T(8,128)(2,1)S(1)} %resident.1.done_ref), custom_call_target="tpu_custom_call" | custom-call | tf_op jit(solution)/shard_map/arrivals/pallas_call | solution.py:359
Async XLA Ops:
  2.6 7.8 %copy-start.1 = (bf16[8,2,4096]{2,1,0:T(2,128)(2,1)S(1)}, bf16[8,2,4096]{2,1,0:T(2,128)(2,1)}, u32[]{:S(2)}) copy-start(bf16[8,2,4096]{2,1,0:T(2,128)(2,1)} %param.18) | copy-start | bytes 393220
  2.6 7.8 %copy-start.3 = (bf16[8,2,2,256]{3,2,1,0:T(2,128)(2,1)S(1)}, bf16[8,2,2,256]{3,2,1,0:T(2,128)(2,1)}, u32[]{:S(2)}) copy-start(bf16[8,2,2,256]{3,2,1,0:T(2,128)(2,1)} %param.19) | copy-start | bytes 49156
  2.6 7.8 %copy-start.5 = (bf16[8,64,2,2]{1,3,2,0:T(2,128)(2,1)S(1)}, bf16[8,64,2,2]{1,3,2,0:T(2,128)(2,1)}, u32[]{:S(2)}) copy-start(bf16[8,64,2,2]{1,3,2,0:T(2,128)(2,1)} %param.16) | copy-start | bytes 12292
  2.7 12.6 %all-to-all-start = ((bf16[16,2,16,128]{3,2,1,0:T(8,128)(2,1)}), bf16[16,2,16,128]{3,2,1,0:T(8,128)(2,1)S(1)}, u32[]{:S(2)}, u32[]{:S(2)}) async-start(bf16[16,2,16,128]{3,2,1,0:T(8,128)(2,1)} %pack.1), calls=%async_computation | async-start | bytes 262144 | tf_op jit(solution)/shard_map/all_to_all | solution.py:401
  10.4 1.0 %copy-start = (bf16[8,64,2,256]{3,2,1,0:T(2,128)(2,1)S(1)}, bf16[8,64,2,256]{3,2,1,0:T(2,128)(2,1)}, u32[]{:S(2)}) copy-start(bf16[8,64,2,256]{3,2,1,0:T(2,128)(2,1)} %param.15) | copy-start | bytes 1572868
  11.5 3.8 %copy-start.2 = (bf16[6,2,4096]{2,1,0:T(2,128)(2,1)S(1)}, bf16[6,2,4096]{2,1,0:T(2,128)(2,1)}, u32[]{:S(2)}) copy-start(bf16[6,2,4096]{2,1,0:T(2,128)(2,1)} %param.20) | copy-start | bytes 294916
  11.5 3.8 %copy-start.4 = (bf16[6,2,2,256]{3,2,1,0:T(2,128)(2,1)S(1)}, bf16[6,2,2,256]{3,2,1,0:T(2,128)(2,1)}, u32[]{:S(2)}) copy-start(bf16[6,2,2,256]{3,2,1,0:T(2,128)(2,1)} %param.21) | copy-start | bytes 36868

commit v9 on v6

--- a/solution.py
+++ b/solution.py
@@ -60,38 +60,31 @@
 
 
 def pack_kernel(
-    tp, heads, block_rows, dest_hbm, blocks_hbm, codes_hbm, scales_hbm, send_ref,
-    dest_ref, blocks_ref, codes_ref, scales_ref, sems,
+    tp, order, heads, block_rows, dest_ref, blocks_ref, codes_ref, scales_ref, send_ref
 ):
-    pairs = [
-        (codes_hbm, codes_ref), (scales_hbm, scales_ref),
-        (dest_hbm, dest_ref), (blocks_hbm, blocks_ref),
-    ]
-    copies = [pltpu.make_async_copy(a, b, sems.at[i]) for i, (a, b) in enumerate(pairs)]
-    for copy in copies:
-        copy.start()
     requests, all_rows = codes_ref.shape[:2]
     rows = all_rows // heads
     per_core = heads // tp
-    peers = send_ref.shape[0] // tp
     send_ref[...] = jnp.full(send_ref.shape, EMPTY, BF16)
     row_block = over(iota((rows, HD), 0), block_rows)
     to_row = iota((all_rows, all_rows), 0)
     from_row = iota((all_rows, all_rows), 1)
     source = over(mod(to_row, rows), 2) * (2 * heads) + over(to_row, rows) * 2 + mod(to_row, 2)
     by_head = jnp.where(from_row == source, 1.0, 0.0).astype(BF16)
-    for copy in copies:
-        copy.wait()
 
     def place(r):
-        there = lax.rem(dest_ref[r] + (peers - peers // 2), peers) * tp
+        there = dest_ref[r]
+        if order is not None:
+            spots = [jnp.where(there == w, p, 0) for p, w in enumerate(order)]
+            there = functools.reduce(jnp.add, spots)
+        there = there * tp + tp - 1
         held = row_block < blocks_ref[r]
         codes = dot_nn(by_head, codes_ref[r])
         scales = scales_ref[r].astype(F32)
         for j in range(heads):
             values = codes[j * rows : (j + 1) * rows] * scales[:, j : j + 1]
             values = jnp.where(held, values, EMPTY).astype(BF16)
-            send_ref[there + j // per_core, j % per_core] = values
+            send_ref[there - j // per_core, j % per_core] = values
 
     if requests <= 8:
         for r in range(requests):
@@ -100,7 +93,23 @@
         lax.fori_loop(0, requests, lambda r, c: (place(r), c)[1], 0)
 
 
-def resident_kernel(len_ref, codes_ref, scales_ref, query_ref, new_ref, out_ref):
+def sent_before(size, per_sender, order):
+    def sender(index):
+        at = over(index, per_sender)
+        if order is None:
+            return at
+        return functools.reduce(jnp.add, [jnp.where(at == p, w, 0) for p, w in enumerate(order)])
+
+    row = sender(iota((size, HD), 0))
+    col = sender(iota((8, size), 1))[:1]
+    tiles = [jnp.where(row < col[:, c : c + HD], 1.0, 0.0) for c in range(0, size, HD)]
+    return jnp.concatenate(tiles, axis=1).astype(BF16)
+
+
+def resident_kernel(
+    per_sender, order, len_ref, codes_ref, scales_ref, query_ref, new_ref, out_ref, before_ref
+):
+    before_ref[...] = sent_before(before_ref.shape[0], per_sender, order)
     slots, rows = codes_ref.shape[:2]
     heads = scales_ref.shape[2]
     tokens = rows // (2 * heads)
@@ -157,7 +166,7 @@
 
 
 def arrival_kernel(
-    tp, got_ref, query_ref, new_ref, done_ref, out_hbm, done_hbm, out_ref, sems
+    tp, got_ref, query_ref, new_ref, done_ref, before_ref, out_hbm, done_hbm, out_ref, sems
 ):
     step = pl.program_id(0)
     hand_on = pltpu.make_async_copy(done_ref, done_hbm, sems.at[0])
@@ -168,7 +177,7 @@
     rows = slots * per_head
     columns = chunks * chunk_rows
     sender_rows = tp * chunk_rows
-    piece = min(columns, 256)
+    piece = before_ref.shape[0]
     every = range(heads)
 
     caches = [got_ref[:, h].reshape(columns, HD) for h in every]
@@ -183,24 +192,14 @@
     col = iota((8, columns), 1)
     held = sums < EMPTY
     first = jnp.where(held & (mod(col, sender_rows) == 0), 1.0, 0.0).astype(BF16)
-    starts = list(range(0, columns, piece))
-    half = len(starts) // 2
-
-    def sender(index):
-        at = over(index, sender_rows)
-        return at if half else mod(at + chunks // tp // 2, chunks // tp)
-
-    before = jnp.where(
-        sender(iota((piece, piece), 0)) < sender(iota((piece, piece), 1)), 1.0, 0.0
-    ).astype(BF16)
     base = jnp.zeros((8, 1), F32)
-    ranks = {}
-    for p in starts[half:] + starts[:half]:
+    ranks = []
+    for p in range(0, columns, piece):
         part = first[:, p : p + piece]
-        ranks[p] = dot_nn(part, before) + base
-        if half:
+        ranks.append(dot_nn(part, before_ref[...]) + base)
+        if p + piece < columns:
             base = base + jnp.sum(part.astype(F32), axis=1, keepdims=True)
-    rank = jnp.concatenate([ranks[p] for p in starts], axis=1)
+    rank = jnp.concatenate(ranks, axis=1)
     slot_of = jnp.where(held & (mod(col, 2) == 0), rank, -1.0)[:1]
     first_slot = (step * slots).astype(F32)
     mine = [slot_of == first_slot + a for a in range(slots)]
@@ -257,7 +256,7 @@
     return pltpu.CompilerParams(vmem_limit_bytes=mib * 2**20)
 
 
-def pack(pre_codes, pre_scales, req_dest, req_blocks, peers, tp):
+def pack(pre_codes, pre_scales, req_dest, req_blocks, peers, tp, order):
     requests, blocks, block_tokens = pre_codes.shape[:3]
     tokens = blocks * block_tokens
     codes = (
@@ -268,17 +267,10 @@
     scales = pre_scales.reshape(requests, tokens * 2, KVH)
     ins = [req_dest, req_blocks, codes, scales]
     return pl.pallas_call(
-        functools.partial(pack_kernel, tp, KVH, 2 * block_tokens),
+        functools.partial(pack_kernel, tp, order, KVH, 2 * block_tokens),
         out_shape=pltpu.VMEM((peers * tp, KVH // tp, tokens * 2, HD), BF16),
-        in_specs=[whole(pltpu.HBM)] * len(ins),
+        in_specs=[whole(pltpu.SMEM)] * 2 + [whole()] * 2,
         out_specs=whole(),
-        scratch_shapes=[
-            pltpu.SMEM(req_dest.shape, jnp.int32),
-            pltpu.SMEM(req_blocks.shape, jnp.int32),
-            pltpu.VMEM(codes.shape, BF16),
-            pltpu.VMEM(scales.shape, BF16),
-            pltpu.SemaphoreType.DMA((len(ins),)),
-        ],
         compiler_params=limit(16),
         name="pack",
     )(*[in_hbm(x) for x in ins])
@@ -314,17 +306,18 @@
     return out.reshape(slots, width // HD, steps, HD).transpose(0, 2, 1, 3).reshape(shape)
 
 
-def resident(codes, res_scales, res_len, res_query, res_new):
+def resident(codes, res_scales, res_len, res_query, res_new, got, tp, order):
     slots, rows = codes.shape[:2]
     heads = res_scales.shape[-1]
     scales = res_scales.transpose(0, 2, 3, 1)
     query = query_rows(res_query).reshape(slots, heads * GROUP * STEPS, HD)
     work = query.shape[0] * query.shape[1] * rows
+    piece = min(got.shape[0] * got.shape[2], 256)
     return pl.pallas_call(
-        resident_kernel,
-        out_shape=pltpu.VMEM(query.shape, BF16),
+        functools.partial(resident_kernel, tp * got.shape[2], order),
+        out_shape=[pltpu.VMEM(query.shape, BF16), pltpu.VMEM((piece, piece), BF16)],
         in_specs=[whole(pltpu.SMEM)] + [whole()] * 4,
-        out_specs=whole(),
+        out_specs=[whole()] * 2,
         cost_estimate=pl.CostEstimate(
             flops=4 * work * HD,
             bytes_accessed=2 * (codes.size + 2 * query.size),
@@ -335,7 +328,7 @@
     )(in_hbm(res_len), codes, scales, query, new_rows_of(res_new))
 
 
-def arrivals(got, arr_query, arr_new, done, tp):
+def arrivals(got, arr_query, arr_new, done, before, tp):
     slots, steps, width = arr_query.shape
     heads = width // (HD * GROUP)
     query = query_rows(arr_query).reshape(slots, heads, GROUP * steps, HD)
@@ -354,6 +347,7 @@
             pl.BlockSpec((size,) + query.shape[1:], lambda i: (i, 0, 0, 0)),
             pl.BlockSpec((new.shape[0] // slots * size, HD), lambda i: (i, 0)),
             whole(),
+            whole(),
         ],
         out_specs=[whole(pltpu.HBM)] * 2,
         scratch_shapes=[
@@ -362,7 +356,7 @@
         ],
         compiler_params=limit(16 if small else 48),
         name="arrivals",
-    )(got, query, new, done)
+    )(got, query, new, done, before)
 
 
 def shards(
@@ -380,17 +374,22 @@
 ):
     peers = lax.axis_size("wide")
     tp = lax.axis_size("tp")
-    send = pack(pre_codes, pre_scales, req_dest, req_blocks, peers, tp)
+    order = [5, 1, 2, 3, 4, 6, 7, 0] if peers == 8 else None
+    send = pack(pre_codes, pre_scales, req_dest, req_blocks, peers, tp, order)
     got = lax.all_to_all(
         send,
         ("wide", "tp"),
         split_axis=0,
         concat_axis=0,
         tiled=True,
-        axis_index_groups=[[(i + peers // 2 * tp) % (peers * tp) for i in range(peers * tp)]],
-    )
-    done = resident(cache_rows(res_codes), res_scales, res_len, res_query, res_new)
-    arr_out, res_out = arrivals(got, arr_query, arr_new, done, tp)
+        axis_index_groups=[
+            [w * tp + t for w in order or range(peers) for t in reversed(range(tp))]
+        ],
+    )
+    done, before = resident(
+        cache_rows(res_codes), res_scales, res_len, res_query, res_new, send, tp, order
+    )
+    arr_out, res_out = arrivals(got, arr_query, arr_new, done, before, tp)
     return (from_rows(res_out, res_query.shape), from_rows(arr_out, arr_query.shape))
 
 

time: 17.7 us -> 16.6 us (0.938)
  waiting for transfers between devices: 2.59 us -> 1.6 us
    all_to_all x1, waiting for transfers between devices: 2.59 us -> 1.6 us  [shards(): lax.all_to_all(send, ('wide', 'tp'), split_axis=0, concat_axis=0, tiled=T...]
where the time goes in v9:
time: 16.6 us; the launch traced here: 16.3 us
  starting transfers between devices  7.97 us (48%)
  Pallas kernels  5 us (30%)
  waiting for transfers between devices  1.6 us (10%)
  local copies, waits for them, and re-layouts  1.06 us (6%)
  between operations  0.67 us (4%)
    all_to_all x1, starting transfers between devices, shards(): lax.all_to_all(send, ('wide', 'tp'), split_axis=0, concat_axis=0, tiled=T...  7.97 us
    pallas_call x1, Pallas kernels, resident(): pl.pallas_call(functools.partial(resident_kernel, tp * got.shape[2], orde...  2.01 us
    pallas_call x1, Pallas kernels, pack(): pl.pallas_call(functools.partial(pack_kernel, tp, order, KVH, 2 * block_t...  1.66 us
    all_to_all x1, waiting for transfers between devices, shards(): lax.all_to_all(send, ('wide', 'tp'), split_axis=0, concat_axis=0, tiled=T...  1.6 us
    pallas_call x1, Pallas kernels, arrivals(): pl.pallas_call(functools.partial(arrival_kernel, tp), out_shape=[jax.Shap...  1.33 us
    unnamed x12, local copies, waits for them, and re-layouts  1.06 us
  transfers between devices with their start and end apart: 1, of which 1 were waited for; matrix products, arithmetic and copies ran while one was open for 0% of the time, Pallas kernels for 12%

profile of v9, /device:TPU:0, one launch (start us, length us, event | category | flops | bytes accessed | tf_op | source)
XLA Modules:
  0.0 16.3 jit_solution(1979893185725030388)
XLA Ops:
  0.6 1.7 %pack.1 = bf16[16,2,16,128]{3,2,1,0:T(8,128)(2,1)} custom-call(s32[4]{0:T(128)} %dest_ref.1, s32[4]{0:T(128)} %blocks_ref.1, bf16[4,64,128]{2,1,0:T(8,128)(2,1)} %bitcast.48, bf16[4,16,4]{2,1,0:T(8,128)(2,1)} %bitcast.49), custom_call_target="tpu_custom_call" | custom-call | tf_op jit(solution)/shard_map/pack/pallas_call | solution.py:269
  2.3 0.0 copy-start.1
  2.3 0.0 copy-start.3
  2.3 0.0 copy-start.5
  2.3 8.0 %all-to-all-start = ((bf16[16,2,16,128]{3,2,1,0:T(8,128)(2,1)}), bf16[16,2,16,128]{3,2,1,0:T(8,128)(2,1)S(1)}, u32[]{:S(2)}, u32[]{:S(2)}) async-start(bf16[16,2,16,128]{3,2,1,0:T(8,128)(2,1)} %pack.1), calls=%async_computation | async-start | bytes 262144 | tf_op jit(solution)/shard_map/all_to_all | solution.py:379
  10.3 0.0 copy-done.1
  10.3 0.0 copy-done.3
  10.3 0.0 copy-done.5
  10.3 0.0 copy-start
  10.3 1.0 %copy-done = bf16[8,64,2,256]{3,2,1,0:T(2,128)(2,1)S(1)} copy-done((bf16[8,64,2,256]{3,2,1,0:T(2,128)(2,1)S(1)}, bf16[8,64,2,256]{3,2,1,0:T(2,128)(2,1)}, u32[]{:S(2)}) %copy-start) | copy-done | bytes 524312
  11.3 0.0 copy-start.2
  11.3 0.0 copy-start.4
  11.3 2.0 %resident.1 = (bf16[8,64,128]{2,1,0:T(8,128)(2,1)S(1)}, bf16[256,256]{1,0:T(8,128)(2,1)S(1)}) custom-call(s32[8]{0:T(128)} %len_ref.1, bf16[8,256,128]{2,1,0:T(8,128)(2,1)S(1)} %bitcast.42, bf16[8,2,2,64]{3,2,1,0:T(2,128)(2,1)S(1)} %bitcast.47, bf16[8,64,128]{2,1,0:T(8,128)(2,1)S(1)} %bitcast.43, bf16[64,128]{1,0:T(8,128)(2,1)S(1)} %bitcast.45), custom_call_target="tpu_custom_call" | custom-call | flops 67108864 | bytes 786432 | tf_op jit(solution)/shard_map/resident/pallas_call | solution.py:316
  13.4 1.6 %all-to-all-done.got_ref = bf16[16,2,16,128]{3,2,1,0:T(8,128)(2,1)S(1)} async-done(((bf16[16,2,16,128]{3,2,1,0:T(8,128)(2,1)}), bf16[16,2,16,128]{3,2,1,0:T(8,128)(2,1)S(1)}, u32[]{:S(2)}, u32[]{:S(2)}) %all-to-all-start) | async-done | bytes 131104 | tf_op jit(solution)/shard_map/all_to_all | solution.py:379
  15.0 0.0 copy-done.2
  15.0 0.0 copy-done.4
  15.0 1.3 %arrivals.1 = (bf16[6,2,32,128]{3,2,1,0:T(8,128)(2,1)}, bf16[8,64,128]{2,1,0:T(8,128)(2,1)}) custom-call(bf16[16,2,16,128]{3,2,1,0:T(8,128)(2,1)S(1)} %all-to-all-done.got_ref, bf16[6,2,32,128]{3,2,1,0:T(8,128)(2,1)S(1)} %bitcast.44, bf16[48,128]{1,0:T(8,128)(2,1)S(1)} %bitcast.46, bf16[8,64,128]{2,1,0:T(8,128)(2,1)S(1)} %get-tuple-element.6.done_ref, ...), custom_call_target="tpu_custom_call" | custom-call | tf_op jit(solution)/shard_map/arrivals/pallas_call | solution.py:338
Async XLA Ops:
  2.3 8.0 %copy-start.1 = (bf16[8,2,4096]{2,1,0:T(2,128)(2,1)S(1)}, bf16[8,2,4096]{2,1,0:T(2,128)(2,1)}, u32[]{:S(2)}) copy-start(bf16[8,2,4096]{2,1,0:T(2,128)(2,1)} %param.18) | copy-start | bytes 393220
  2.3 8.0 %copy-start.3 = (bf16[8,2,2,256]{3,2,1,0:T(2,128)(2,1)S(1)}, bf16[8,2,2,256]{3,2,1,0:T(2,128)(2,1)}, u32[]{:S(2)}) copy-start(bf16[8,2,2,256]{3,2,1,0:T(2,128)(2,1)} %param.19) | copy-start | bytes 49156
  2.3 8.0 %copy-start.5 = (bf16[8,64,2,2]{1,3,2,0:T(2,128)(2,1)S(1)}, bf16[8,64,2,2]{1,3,2,0:T(2,128)(2,1)}, u32[]{:S(2)}) copy-start(bf16[8,64,2,2]{1,3,2,0:T(2,128)(2,1)} %param.16) | copy-start | bytes 12292
  2.3 12.7 %all-to-all-start = ((bf16[16,2,16,128]{3,2,1,0:T(8,128)(2,1)}), bf16[16,2,16,128]{3,2,1,0:T(8,128)(2,1)S(1)}, u32[]{:S(2)}, u32[]{:S(2)}) async-start(bf16[16,2,16,128]{3,2,1,0:T(8,128)(2,1)} %pack.1), calls=%async_computation | async-start | bytes 262144 | tf_op jit(solution)/shard_map/all_to_all | solution.py:379
  10.3 1.0 %copy-start = (bf16[8,64,2,256]{3,2,1,0:T(2,128)(2,1)S(1)}, bf16[8,64,2,256]{3,2,1,0:T(2,128)(2,1)}, u32[]{:S(2)}) copy-start(bf16[8,64,2,256]{3,2,1,0:T(2,128)(2,1)} %param.15) | copy-start | bytes 1572868
  11.3 3.6 %copy-start.2 = (bf16[6,2,4096]{2,1,0:T(2,128)(2,1)S(1)}, bf16[6,2,4096]{2,1,0:T(2,128)(2,1)}, u32[]{:S(2)}) copy-start(bf16[6,2,4096]{2,1,0:T(2,128)(2,1)} %param.20) | copy-start | bytes 294916
  11.3 3.6 %copy-start.4 = (bf16[6,2,2,256]{3,2,1,0:T(2,128)(2,1)S(1)}, bf16[6,2,2,256]{3,2,1,0:T(2,128)(2,1)}, u32[]{:S(2)}) copy-start(bf16[6,2,2,256]{3,2,1,0:T(2,128)(2,1)} %param.21) | copy-start | bytes 36868
